TPU v7x, 256 devices: a whole 4x4x8 slice. The times are simulated.
256 devices in a mesh: ctx: 32 (over x, z_hi, core), tp: 8 (over y, z_lo).
Axes of the slice: x: 4, y: 4, z: 8 (z_hi: 4, z_lo: 2; z = z_hi * 2 + z_lo), core: 2. Of those that a mesh axis runs over, the one named last changes fastest.
Arguments:
- query_branch: bfloat16 [16384, 4096], P('ctx', 'tp'), may hold values from -6 to 6
- key_branch: bfloat16 [16384, 4096], P('ctx', 'tp'), may hold values from 0 to 2
- value_branch: bfloat16 [16384, 4096], P('ctx', 'tp'), may hold values from 0 to 2
- filters: bfloat16 [16384, 4096], P('ctx', 'tp'), may hold values from -1.1 to 1.1
- skip_gain: float32 [4096], P('tp'), may hold values from -1 to 1
- out_weight: bfloat16 [4096, 4096], P('tp'), may hold values from -0.09375 to 0.09375
Outputs:
- mixed: bfloat16 [16384, 4096], P('ctx')
All inputs are finite; a program needn't handle non-finite values.
Results may differ from a plain program's by a relative error of at most 0.018.
Values may be sent and summed in bfloat16 or wider, within the bound.
No kernel may reach another device: no remote copies, remote signals or barrier semaphores. Data moves between devices by JAX's collectives and lax.ppermute only.
A program may use at most 64 MiB of HBM per device.

v0:
```python
import math

import jax
import jax.numpy as jnp
from jax import lax
from jax.sharding import PartitionSpec as P


def cosine_lookup_table(period, row_count, column_count, row_start, column_start):
    row_index = jnp.arange(row_count, dtype=jnp.int32) + row_start
    column_number_index = jnp.arange(column_count, dtype=jnp.int32) + column_start
    phase = row_index[:, None] * column_number_index[None, :] % period
    angle = phase.astype(jnp.float32) * (2.0 * math.pi / period)
    return (jnp.cos(angle), jnp.sin(angle))


def round_half(value):
    return lax.optimization_barrier(value.astype(jnp.bfloat16))


def body(query_branch, key_branch, value_branch, filters, skip_gain, out_weight):
    ctx_count = lax.axis_size("ctx")
    ctx_index = lax.axis_index("ctx")
    seq_rows, channels = query_branch.shape
    stride = seq_rows // ctx_count
    blocks = 2 * ctx_count
    period = 2 * seq_rows * ctx_count
    inverse_len = 1.0 / period
    mixer = round_half(key_branch.astype(jnp.float32) * value_branch.astype(jnp.float32))
    line_cos, line_sin = cosine_lookup_table(seq_rows, seq_rows, seq_rows, 0, 0)
    line_cos = line_cos.astype(jnp.bfloat16)
    line_sin = line_sin.astype(jnp.bfloat16)
    forward_table = jnp.concatenate(
        [jnp.concatenate([line_cos, line_sin], 1), jnp.concatenate([-line_sin, line_cos], 1)], 0
    )
    inverse_table = jnp.concatenate(
        [jnp.concatenate([line_cos, -line_sin], 1), jnp.concatenate([line_sin, line_cos], 1)], 0
    )
    arrived = (
        lax.all_to_all(mixer[None], "ctx", split_axis=1, concat_axis=0, tiled=True),
        lax.all_to_all(filters[None], "ctx", split_axis=1, concat_axis=0, tiled=True),
    )
    block_cos, block_sin = cosine_lookup_table(blocks, blocks, ctx_count, 0, 0)
    block_cos = block_cos.astype(jnp.bfloat16)
    block_sin = block_sin.astype(jnp.bfloat16)
    twist_cos, twist_sin = cosine_lookup_table(period, stride, blocks, ctx_index * stride, 0)
    twist_cos = twist_cos[:, :, None]
    twist_sin = twist_sin[:, :, None]

    def first_section(signal):
        real_part = jnp.einsum("kn,nmc->mkc", block_cos, signal, preferred_element_type=jnp.float32)
        imag_part = -jnp.einsum(
            "kn,nmc->mkc", block_sin, signal, preferred_element_type=jnp.float32
        )
        first_real = real_part * twist_cos + imag_part * twist_sin
        first_imag = imag_part * twist_cos - real_part * twist_sin
        stacked = jnp.stack([first_real, first_imag]).astype(jnp.bfloat16)
        return stacked.reshape(2, stride, ctx_count, 2, channels)

    outgoing = (first_section(arrived[0]), first_section(arrived[1]))
    by_offset = (
        lax.all_to_all(outgoing[0], "ctx", split_axis=2, concat_axis=1, tiled=True),
        lax.all_to_all(outgoing[1], "ctx", split_axis=2, concat_axis=1, tiled=True),
    )
    operand = jnp.concatenate(
        [
            by_offset[0].reshape(2 * seq_rows, 2 * channels),
            by_offset[1].reshape(2 * seq_rows, 2 * channels),
        ],
        axis=1,
    )
    spectrum = jnp.dot(forward_table, operand, preferred_element_type=jnp.float32)
    mixer_real = spectrum[:seq_rows, : 2 * channels]
    mixer_imag = spectrum[seq_rows:, : 2 * channels]
    filter_real = spectrum[:seq_rows, 2 * channels :]
    filter_imag = spectrum[seq_rows:, 2 * channels :]
    product = jnp.concatenate(
        [
            (mixer_real * filter_real - mixer_imag * filter_imag) * inverse_len,
            (mixer_real * filter_imag + mixer_imag * filter_real) * inverse_len,
        ],
        0,
    ).astype(jnp.bfloat16)
    inverse = jnp.dot(inverse_table, product, preferred_element_type=jnp.float32)
    back_real = inverse[:seq_rows].reshape(seq_rows, 2, channels)
    back_imag = inverse[seq_rows:].reshape(seq_rows, 2, channels)
    second_cos, second_sin = cosine_lookup_table(period, seq_rows, 2, 0, 2 * ctx_index)
    second_cos = second_cos[:, :, None]
    second_sin = second_sin[:, :, None]
    second = jnp.stack(
        [
            back_real * second_cos - back_imag * second_sin,
            back_imag * second_cos + back_real * second_sin,
        ]
    ).astype(jnp.bfloat16)
    second = second.reshape(2, ctx_count, stride, 1, 2, channels)
    returned = lax.all_to_all(second, "ctx", split_axis=1, concat_axis=3, tiled=True).reshape(
        2, stride, blocks, channels
    )
    back_cos, back_sin = cosine_lookup_table(blocks, ctx_count, blocks, 0, 0)
    back_cos = back_cos.astype(jnp.bfloat16)
    back_sin = back_sin.astype(jnp.bfloat16)
    conv = jnp.einsum(
        "nk,mkc->nmc", back_cos, returned[0], preferred_element_type=jnp.float32
    ) - jnp.einsum("nk,mkc->nmc", back_sin, returned[1], preferred_element_type=jnp.float32)
    conv = conv.astype(jnp.bfloat16)
    conv_rows = lax.all_to_all(conv, "ctx", split_axis=0, concat_axis=1, tiled=True).reshape(
        seq_rows, channels
    )
    gated = (
        query_branch.astype(jnp.float32)
        * (conv_rows.astype(jnp.float32) + skip_gain[None, :] * mixer.astype(jnp.float32))
    ).astype(jnp.bfloat16)
    partial_value = jnp.dot(gated, out_weight, preferred_element_type=jnp.float32)
    summed = lax.psum(partial_value.astype(jnp.bfloat16), "tp")
    return summed


def solution(mesh):
    placed = (
        P("ctx", "tp"),
        P("ctx", "tp"),
        P("ctx", "tp"),
        P("ctx", "tp"),
        P("tp"),
        P("tp", None),
    )
    return jax.shard_map(
        body, mesh=mesh, in_specs=placed, out_specs=P("ctx", None), check_vma=False
    )
```

profile of v0, /device:TPU:2, one launch (start us, length us, event | category | flops | bytes accessed | tf_op | source)
XLA Modules:
  0.0 499.2 jit_solution(15908772302080005161)
XLA Ops:
  10.0 3.8 reduce.1
  15.0 11.6 %all-to-all-start = ((bf16[32,2,4096]{2,1,0:T(2,128)(2,1)}), bf16[32,2,4096]{2,1,0:T(2,128)(2,1)S(1)}, u32[]{:S(2)}, u32[]{:S(2)}) async-start(bf16[32,2,4096]{2,1,0:T(2,128)(2,1)} %reshape.285), calls=%async_computation | async-start | bytes 1048576 | tf_op jit(solution)/shard_map/all_to_all | solution.py:40
  27.5 3.8 reduce
  32.5 10.7 %all-to-all-done = bf16[32,2,4096]{2,1,0:T(2,128)(2,1)S(1)} async-done(((bf16[32,2,4096]{2,1,0:T(2,128)(2,1)}), bf16[32,2,4096]{2,1,0:T(2,128)(2,1)S(1)}, u32[]{:S(2)}, u32[]{:S(2)}) %all-to-all-start) | async-done | bytes 524320 | tf_op jit(solution)/shard_map/all_to_all | solution.py:40
  43.2 7.4 %all-to-all-start.2 = ((bf16[32,2,4096]{2,1,0:T(2,128)(2,1)}), bf16[32,2,4096]{2,1,0:T(2,128)(2,1)}, u32[]{:S(2)}, u32[]{:S(2)}) async-start(bf16[32,2,4096]{2,1,0:T(2,128)(2,1)} %reshape.283), calls=%async_computation.2 | async-start | bytes 1048576 | tf_op jit(solution)/shard_map/all_to_all | solution.py:41
  54.1 3.0 pad_maximum_fusion.6
  57.1 3.7 copy.69
  60.8 5.7 %all-to-all-done.2 = bf16[32,2,4096]{2,1,0:T(2,128)(2,1)} async-done(((bf16[32,2,4096]{2,1,0:T(2,128)(2,1)}), bf16[32,2,4096]{2,1,0:T(2,128)(2,1)}, u32[]{:S(2)}, u32[]{:S(2)}) %all-to-all-start.2) | async-done | bytes 524320 | tf_op jit(solution)/shard_map/all_to_all | solution.py:41
  66.4 7.4 %all-to-all-start.1 = ((bf16[2,16,32,2,512]{4,3,1,0,2:T(2,128)(2,1)}), bf16[2,16,32,2,512]{4,3,1,0,2:T(2,128)(2,1)S(1)}, u32[]{:S(2)}, u32[]{:S(2)}) async-start(bf16[2,16,32,2,512]{4,3,1,0,2:T(2,128)(2,1)} %copy.69), calls=%async_computation.1 | async-start | bytes 4194304 | tf_op jit(solution)/shard_map/all_to_all | solution.py:62
  73.9 3.6 reshape.284
  80.4 2.2 stack.30
  83.8 4.7 pad_maximum_fusion.7
  88.5 3.6 copy.70
  92.1 31.1 %all-to-all-done.1 = bf16[2,16,32,2,512]{4,3,1,0,2:T(2,128)(2,1)S(1)} async-done(((bf16[2,16,32,2,512]{4,3,1,0,2:T(2,128)(2,1)}), bf16[2,16,32,2,512]{4,3,1,0,2:T(2,128)(2,1)S(1)}, u32[]{:S(2)}, u32[]{:S(2)}) %all-to-all-start.1) | async-done | bytes 2097184 | tf_op jit(solution)/shard_map/all_to_all | solution.py:62
  123.2 7.2 %all-to-all-start.3 = ((bf16[2,16,32,2,512]{4,3,1,0,2:T(2,128)(2,1)}), bf16[2,16,32,2,512]{4,3,1,0,2:T(2,128)(2,1)}, u32[]{:S(2)}, u32[]{:S(2)}) async-start(bf16[2,16,32,2,512]{4,3,1,0,2:T(2,128)(2,1)} %copy.70), calls=%async_computation.3 | async-start | bytes 4194304 | tf_op jit(solution)/shard_map/all_to_all | solution.py:63
  131.1 4.0 fusion.43
  135.1 5.3 %sine_convert_fusion = (bf16[512,512]{1,0:T(8,128)(2,1)}, bf16[512,512]{1,0:T(8,128)(2,1)}) fusion(), kind=kLoop, calls=%fused_computation.50 | loop fusion | flops 4194304 | bytes 1048576 | tf_op jit(solution)/shard_map/convert_element_type | solution.py:32
  142.8 37.5 %all-to-all-done.3 = bf16[2,16,32,2,512]{4,3,1,0,2:T(2,128)(2,1)} async-done(((bf16[2,16,32,2,512]{4,3,1,0,2:T(2,128)(2,1)}), bf16[2,16,32,2,512]{4,3,1,0,2:T(2,128)(2,1)}, u32[]{:S(2)}, u32[]{:S(2)}) %all-to-all-start.3) | async-done | bytes 2097184 | tf_op jit(solution)/shard_map/all_to_all | solution.py:63
  180.3 3.4 copy.62
  184.9 4.5 fusion
  190.5 2.3 fusion.5
  192.9 2.3 fusion.108
  195.2 3.0 reshape.276
  198.3 4.2 reshape.277
  202.4 4.2 fusion.30
  206.6 2.8 pad_maximum_fusion.8
  209.4 56.8 %all_to_all.78 = bf16[2,32,16,1,2,512]{5,4,2,3,0,1:T(2,128)(2,1)S(1)} all-to-all(bf16[2,32,16,1,2,512]{5,4,2,3,0,1:T(2,128)(2,1)S(1)} %pad_maximum_fusion.8), channel_id=1, replica_groups=mesh['ctx'=32,'tp'=8] {'ctx'}, dimensions={1} | all-to-all | bytes 4194304 | tf_op jit(solution)/shard_map/all_to_all | solution.py:97
  266.2 2.3 fusion.109
  273.2 22.5 %all_to_all.79 = bf16[32,16,512]{2,1,0:T(8,128)(2,1)S(1)} all-to-all(bf16[32,16,512]{2,1,0:T(8,128)(2,1)S(1)} %copy.68), channel_id=1, replica_groups=mesh['ctx'=32,'tp'=8] {'ctx'}, dimensions={0} | all-to-all | bytes 1048576 | tf_op jit(solution)/shard_map/all_to_all | solution.py:107
  295.7 5.4 %convolution_convert_fusion = bf16[512,4096]{1,0:T(8,128)(2,1)} fusion(bf16[512,4096]{1,0:T(8,128)(2,1)S(1)} %copy-done.6, bf16[512,512]{1,0:T(8,128)(2,1)S(1)} %bitcast.100, bf16[512,512]{1,0:T(8,128)(2,1)S(1)} %copy-done.2, bf16[512,512]{1,0:T(8,128)(2,1)} %param.6, f32[512]{0:T(512)S(1)} %copy-done.7), kind=kOutput, calls=%fused_computation | convolution fusion | flops 2151415808 | bytes 9963520 | tf_op jit(solution)/shard_map/dot_general | solution.py:114
  301.2 186.3 %all-reduce.2.cloned.1.call-done = bf16[512,4096]{1,0:T(8,128)(2,1)} async-done(((bf16[512,4096]{1,0:T(8,128)(2,1)}), bf16[512,4096]{1,0:T(8,128)(2,1)}) %all-reduce.2.cloned.1.call-update) | async-done | bytes 4194320 | tf_op jit(solution)/shard_map/psum | solution.py:115
  487.4 4.7 copy.92
  (52 shorter events, 24.2 us)
Async XLA Ops:
  7.9 0.8 copy-start.1
  9.5 17.2 %copy-start.3 = (bf16[512,512]{1,0:T(8,128)(2,1)S(1)}, bf16[512,512]{1,0:T(8,128)(2,1)}, u32[]{:S(2)}) copy-start(bf16[512,512]{1,0:T(8,128)(2,1)} %param.9) | copy-start | bytes 1572868
  15.0 28.2 %all-to-all-start = ((bf16[32,2,4096]{2,1,0:T(2,128)(2,1)}), bf16[32,2,4096]{2,1,0:T(2,128)(2,1)S(1)}, u32[]{:S(2)}, u32[]{:S(2)}) async-start(bf16[32,2,4096]{2,1,0:T(2,128)(2,1)} %reshape.285), calls=%async_computation | async-start | bytes 1048576 | tf_op jit(solution)/shard_map/all_to_all | solution.py:40
  43.2 23.3 %all-to-all-start.2 = ((bf16[32,2,4096]{2,1,0:T(2,128)(2,1)}), bf16[32,2,4096]{2,1,0:T(2,128)(2,1)}, u32[]{:S(2)}, u32[]{:S(2)}) async-start(bf16[32,2,4096]{2,1,0:T(2,128)(2,1)} %reshape.283), calls=%async_computation.2 | async-start | bytes 1048576 | tf_op jit(solution)/shard_map/all_to_all | solution.py:41
  66.4 56.8 %all-to-all-start.1 = ((bf16[2,16,32,2,512]{4,3,1,0,2:T(2,128)(2,1)}), bf16[2,16,32,2,512]{4,3,1,0,2:T(2,128)(2,1)S(1)}, u32[]{:S(2)}, u32[]{:S(2)}) async-start(bf16[2,16,32,2,512]{4,3,1,0,2:T(2,128)(2,1)} %copy.69), calls=%async_computation.1 | async-start | bytes 4194304 | tf_op jit(solution)/shard_map/all_to_all | solution.py:62
  123.2 57.0 %all-to-all-start.3 = ((bf16[2,16,32,2,512]{4,3,1,0,2:T(2,128)(2,1)}), bf16[2,16,32,2,512]{4,3,1,0,2:T(2,128)(2,1)}, u32[]{:S(2)}, u32[]{:S(2)}) async-start(bf16[2,16,32,2,512]{4,3,1,0,2:T(2,128)(2,1)} %copy.70), calls=%async_computation.3 | async-start | bytes 4194304 | tf_op jit(solution)/shard_map/all_to_all | solution.py:63
  130.5 357.0 %all-reduce.2.cloned.1.call-start = ((), (), s32[]{:S(2)}) async-start(), calls=%async_computation.6 | async-start | bytes 8388608 | tf_op jit(solution)/shard_map/psum | solution.py:115
  183.7 1.0 copy-start.4
  183.7 1.2 copy-start.5
  269.8 1.2 copy-start
  272.0 23.6 %copy-start.7 = (f32[512]{0:T(512)S(1)}, f32[512]{0:T(512)}, u32[]{:S(2)}) copy-start(f32[512]{0:T(512)} %param.10) | copy-start | bytes 6148
  272.5 23.2 %copy-start.2 = (bf16[512,512]{1,0:T(8,128)(2,1)S(1)}, bf16[512,512]{1,0:T(8,128)(2,1)}, u32[]{:S(2)}) copy-start(bf16[512,512]{1,0:T(8,128)(2,1)} %copy-done.1) | copy-start | bytes 1572868
  272.5 23.2 %copy-start.6 = (bf16[512,4096]{1,0:T(8,128)(2,1)S(1)}, bf16[512,4096]{1,0:T(8,128)(2,1)}, u32[]{:S(2)}) copy-start(bf16[512,4096]{1,0:T(8,128)(2,1)} %param.11) | copy-start | bytes 12582916
Sparse Core Ops, SparseCore 0:
  301.3 186.1 all-reduce.1
where the time goes:
time: 508 us; the launch traced here: 499 us
  waiting for transfers between devices  271 us (53%)
  blocking collectives  79.3 us (16%)
  local copies, waits for them, and re-layouts  49.1 us (10%)
  other arithmetic  34.3 us (7%)
  starting transfers between devices  33.7 us (7%)
  matrix products  17.6 us (3%)
  between operations  14 us (3%)
    psum x1, waiting for transfers between devices, body(): summed = lax.psum(partial_value.astype(jnp.bfloat16), 'tp')  186 us
    all_to_all x1, blocking collectives, body(): lax.all_to_all(second, 'ctx', split_axis=1, concat_axis=3, tiled=True)  56.8 us
    all_to_all x1, waiting for transfers between devices, body(): lax.all_to_all(outgoing[1], 'ctx', split_axis=2, concat_axis=1, tiled=True)  37.5 us
    all_to_all x1, waiting for transfers between devices, body(): lax.all_to_all(outgoing[0], 'ctx', split_axis=2, concat_axis=1, tiled=True)  31.1 us
    all_to_all x1, blocking collectives, body(): lax.all_to_all(conv, 'ctx', split_axis=0, concat_axis=1, tiled=True)  22.5 us
    unnamed x26, local copies, waits for them, and re-layouts  15.4 us
    another operation x6, local copies, waits for them, and re-layouts, first_section(): stacked = jnp.stack([first_real, first_imag]).astype(jnp.bfloat16)  11.6 us
    all_to_all x1, starting transfers between devices, body(): lax.all_to_all(mixer[None], 'ctx', split_axis=1, concat_axis=0, tiled=True)  11.6 us
  transfers between devices with their start and end apart: 5, of which 5 were waited for; matrix products, arithmetic and copies ran while one was open for 9% of the time, Pallas kernels for 0%

commit v1 on v0

v1 whole, which is shorter than its diff:
```python
import math

import jax
import jax.numpy as jnp
import ml_dtypes
import numpy as np
from jax import lax
from jax.experimental import pallas as pl
from jax.experimental.pallas import tpu as pltpu
from jax.sharding import PartitionSpec as P

VMEM_BYTES = 40 * 1024 * 1024
GROUP = 4


def transform_tables(rows):
    j = np.arange(rows, dtype=np.int64)[:, None]
    f = np.arange(rows, dtype=np.int64)[None, :]
    angle = (j * (2 * f + 1) % (4 * rows)) * (2.0 * math.pi / (4 * rows))
    cos, sin = np.cos(angle), np.sin(angle)
    forward = np.concatenate([cos, -sin], 1)
    inverse = np.concatenate([cos.T, -sin.T], 0) / rows
    return forward.astype(ml_dtypes.bfloat16), inverse.astype(ml_dtypes.bfloat16)


def pack_kernel(key_ref, value_ref, filter_ref, out_ref):
    parts, both, rows = out_ref.shape
    share = both // 2
    mixer = key_ref[...].astype(jnp.float32) * value_ref[...].astype(jnp.float32)
    out_ref[:, :share, :] = mixer.astype(jnp.bfloat16).T.reshape(parts, share, rows)
    out_ref[:, share:, :] = filter_ref[...].T.reshape(parts, share, rows)


def conv_kernel(signal_ref, forward_ref, inverse_ref, out_ref, mixer_spec, filter_spec, product):
    blocks, both, rows = signal_ref.shape
    share = both // 2
    forward = forward_ref[...]

    def spectrum(signal):
        flat = signal.reshape(blocks * share, rows)
        value = jnp.dot(flat, forward, preferred_element_type=jnp.float32)
        return value.reshape(blocks, share, 2 * rows)

    mixer_spec[...] = spectrum(signal_ref[:, :share, :])
    filter_spec[...] = spectrum(signal_ref[:, share:, :])

    lane = lax.broadcasted_iota(jnp.int32, (8, 128), 1)
    sign = jnp.where(lane % 2 == 0, 1.0, -1.0).astype(jnp.float32)
    lane_tiles = rows // 128

    def tile(step, carry):
        row = pl.multiple_of((step // lane_tiles) * 8, 8)
        real = pl.multiple_of((step % lane_tiles) * 128, 128)
        imag = pl.multiple_of(rows + (step % lane_tiles) * 128, 128)

        def load(ref, block):
            return (
                ref[block, pl.ds(row, 8), pl.ds(real, 128)],
                ref[block, pl.ds(row, 8), pl.ds(imag, 128)],
            )

        def window(block):
            now_real, now_imag = load(mixer_spec, block)
            if block > 0:
                last_real, last_imag = load(mixer_spec, block - 1)
                now_real, now_imag = now_real - sign * last_imag, now_imag + sign * last_real
            return now_real, now_imag

        for block in reversed(range(blocks)):
            now_real, now_imag = window(block)
            mixer_spec[block, pl.ds(row, 8), pl.ds(real, 128)] = now_real
            mixer_spec[block, pl.ds(row, 8), pl.ds(imag, 128)] = now_imag

        for first in range(0, blocks, GROUP):
            sums = [[None] * 3 for _ in range(GROUP)]
            held = {}
            for lag in range(first + GROUP):
                filter_real, filter_imag = load(filter_spec, lag)
                filter_both = filter_real + filter_imag
                for i in range(GROUP):
                    block = first + i - lag
                    if block < 0:
                        continue
                    if block not in held:
                        real_part, imag_part = load(mixer_spec, block)
                        held[block] = (real_part, imag_part, real_part + imag_part)
                    terms = (
                        filter_real * held[block][0],
                        filter_imag * held[block][1],
                        filter_both * held[block][2],
                    )
                    for s in range(3):
                        sums[i][s] = terms[s] if sums[i][s] is None else sums[i][s] + terms[s]
                held.pop(first + GROUP - 1 - lag, None)
            for i in range(GROUP):
                one, two, three = sums[i]
                product[first + i, pl.ds(row, 8), pl.ds(real, 128)] = one - two
                product[first + i, pl.ds(row, 8), pl.ds(imag, 128)] = three - one - two
        return carry

    lax.fori_loop(0, (share // 8) * lane_tiles, tile, 0)
    flat = product[...].astype(jnp.bfloat16).reshape(blocks * share, 2 * rows)
    conv = jnp.dot(flat, inverse_ref[...], preferred_element_type=jnp.float32)
    out_ref[...] = conv.astype(jnp.bfloat16).reshape(blocks, share, rows)


def project_kernel(conv_ref, query_ref, key_ref, value_ref, gain_ref, weight_ref, out_ref):
    rows, channels = query_ref.shape
    conv = conv_ref[...].reshape(channels, rows).T.astype(jnp.float32)
    mixer = key_ref[...].astype(jnp.float32) * value_ref[...].astype(jnp.float32)
    mixer = mixer.astype(jnp.bfloat16).astype(jnp.float32)
    gated = query_ref[...].astype(jnp.float32) * (conv + gain_ref[...] * mixer)
    gated = gated.astype(jnp.bfloat16)
    width = 1024
    for start in range(0, out_ref.shape[1], width):
        value = jnp.dot(
            gated, weight_ref[:, start : start + width], preferred_element_type=jnp.float32
        )
        out_ref[:, start : start + width] = value.astype(jnp.bfloat16)


def whole(kernel, out_shape, scratch=()):
    return pl.pallas_call(
        kernel,
        out_shape=jax.ShapeDtypeStruct(out_shape, jnp.bfloat16),
        scratch_shapes=list(scratch),
        compiler_params=pltpu.CompilerParams(vmem_limit_bytes=VMEM_BYTES),
    )


def body(query_branch, key_branch, value_branch, filters, skip_gain, out_weight):
    ctx_count = lax.axis_size("ctx")
    rows, channels = query_branch.shape
    share = channels // ctx_count
    forward, inverse = (jnp.asarray(table) for table in transform_tables(rows))

    with jax.named_scope("pack"):
        outgoing = whole(pack_kernel, (ctx_count, 2 * share, rows))(
            key_branch, value_branch, filters
        )
    arrived = lax.all_to_all(outgoing, "ctx", split_axis=0, concat_axis=0, tiled=True)
    spec = pltpu.VMEM((ctx_count, share, 2 * rows), jnp.float32)
    with jax.named_scope("conv"):
        conv = whole(conv_kernel, (ctx_count, share, rows), (spec, spec, spec))(
            arrived, forward, inverse
        )
    conv = lax.all_to_all(conv, "ctx", split_axis=0, concat_axis=0, tiled=True)
    with jax.named_scope("project"):
        partial_value = whole(project_kernel, (rows, out_weight.shape[1]))(
            conv, query_branch, key_branch, value_branch, skip_gain[None, :], out_weight
        )
    tp_count = lax.axis_size("tp")
    pieces = lax.all_to_all(partial_value, "tp", split_axis=0, concat_axis=0, tiled=True)
    pieces = pieces.reshape(tp_count, rows // tp_count, -1)
    summed = pieces.astype(jnp.float32).sum(0).astype(jnp.bfloat16)
    return lax.all_gather(summed, "tp", axis=0, tiled=True)


def solution(mesh):
    placed = (
        P("ctx", "tp"),
        P("ctx", "tp"),
        P("ctx", "tp"),
        P("ctx", "tp"),
        P("tp"),
        P("tp", None),
    )
    return jax.shard_map(
        body, mesh=mesh, in_specs=placed, out_specs=P("ctx", None), check_vma=False
    )
```

time: 508 us -> 244 us (0.48); the launches traced: 499 us -> 243 us
  waiting for transfers between devices: 271 us -> 88.9 us
  local copies, waits for them, and re-layouts: 49.1 us -> 10.3 us
  blocking collectives: 79.3 us -> 117 us
  starting transfers between devices: 33.7 us -> 0.01 us
  other arithmetic: 34.3 us -> 3.84 us
  matrix products: 17.6 us -> 0 us
  Pallas kernels: 0 us -> 9.74 us
    psum x1 -> x0, waiting for transfers between devices: 186 us -> none  [body(): summed = lax.psum(partial_value.astype(jnp.bfloat16), 'tp')]
    all_gather x0 -> x1, waiting for transfers between devices: none -> 88.9 us  [body(): return lax.all_gather(summed, 'tp', axis=0, tiled=True)]
    all_to_all x4 -> x0, waiting for transfers between devices: 84.9 us -> none  [the longest x1 37.5 us: body(): lax.all_to_all(outgoing[1], 'ctx', split_axis=2, concat_axis=1, tiled=True)]
    all_to_all x2 -> x3, blocking collectives: 79.3 us -> 117 us  [the longest x1 55 us: body(): lax.all_to_all(partial_value, 'tp', split_axis=0, concat_axis=0, tiled=True)]
    all_to_all x4 -> x0, starting transfers between devices: 33.7 us -> none  [the longest x1 11.6 us: body(): lax.all_to_all(mixer[None], 'ctx', split_axis=1, concat_axis=0, tiled=True)]
    dot_general x9 -> x0, matrix products: 17.6 us -> none  [the longest x1 5.43 us: body(): jnp.dot(gated, out_weight, preferred_element_type=jnp.float32)]
    another operation x5 -> x0, other arithmetic: 15.7 us -> none  [the longest x2 7.64 us: first_section(): stacked = jnp.stack([first_real, first_imag]).astype(jnp.bfloat16)]
    another operation x6 -> x0, local copies, waits for them, and re-layouts: 11.6 us -> none  [first_section(): stacked = jnp.stack([first_real, first_imag]).astype(jnp.bfloat16)]
  transfers between devices with their start and end apart: 5 -> 1, of which waited for: 5 -> 1; matrix products, arithmetic and copies ran while one was open for 9% -> 0% of each run, Pallas kernels for 0% -> 0%
where the time goes in v1:
time: 244 us; the launch traced here: 243 us
  blocking collectives  117 us (48%)
  waiting for transfers between devices  88.9 us (36%)
  between operations  13.4 us (5%)
  local copies, waits for them, and re-layouts  10.3 us (4%)
  Pallas kernels  9.74 us (4%)
  other arithmetic  3.84 us (2%)
    all_gather x1, waiting for transfers between devices, body(): return lax.all_gather(summed, 'tp', axis=0, tiled=True)  88.9 us
    all_to_all x1, blocking collectives, body(): lax.all_to_all(partial_value, 'tp', split_axis=0, concat_axis=0, tiled=True)  55 us
    all_to_all x1, blocking collectives, body(): lax.all_to_all(outgoing, 'ctx', split_axis=0, concat_axis=0, tiled=True)  39.4 us
    all_to_all x1, blocking collectives, body(): conv = lax.all_to_all(conv, 'ctx', split_axis=0, concat_axis=0, tiled=True)  22.3 us
    unnamed x21, local copies, waits for them, and re-layouts  10.3 us
    pallas_call x1, Pallas kernels, body(): whole(conv_kernel, (ctx_count, share, rows), (spec, spec, spec))  6.91 us
  transfers between devices with their start and end apart: 1, of which 1 were waited for; matrix products, arithmetic and copies ran while one was open for 0% of the time, Pallas kernels for 0%

profile of v1, /device:TPU:2, one launch (start us, length us, event | category | flops | bytes accessed | tf_op | source)
XLA Modules:
  0.0 242.9 jit_solution(13811043140281381606)
XLA Ops:
  6.5 0.0 all-gather.2.cloned.1.call-start
  6.5 0.0 copy-start.1
  6.5 1.0 copy-done.1
  7.6 0.0 copy-start.3
  7.6 1.0 copy-done.3
  8.6 0.0 copy-start.7
  8.6 1.0 copy-done.7
  9.7 0.0 copy-start
  9.7 0.0 copy-start.2
  9.7 0.0 copy-start.4
  9.7 0.3 pack.1
  10.0 39.4 %all_to_all.19.signal_ref = bf16[32,32,512]{2,1,0:T(8,128)(2,1)S(1)} all-to-all(bf16[32,32,512]{2,1,0:T(8,128)(2,1)S(1)} %pack.1), channel_id=1, replica_groups=mesh['ctx'=32,'tp'=8] {'ctx'}, dimensions={0} | all-to-all | bytes 2097152 | tf_op jit(solution)/shard_map/all_to_all | solution.py:141
  49.4 0.0 copy-start.5
  49.4 1.2 copy-done.5
  50.6 0.0 copy-start.6
  50.6 1.2 copy-done.6
  51.8 0.0 copy-start.8
  51.8 0.0 copy-start.9
  51.8 6.9 %conv.1 = bf16[32,16,512]{2,1,0:T(8,128)(2,1)S(1)} custom-call(bf16[32,32,512]{2,1,0:T(8,128)(2,1)S(1)} %all_to_all.19.signal_ref, bf16[512,1024]{1,0:T(8,128)(2,1)S(1)} %copy-done.6, bf16[1024,512]{1,0:T(8,128)(2,1)S(1)} %copy-done.5), custom_call_target="tpu_custom_call" | custom-call | tf_op jit(solution)/shard_map/conv/pallas_call | solution.py:144
  58.7 22.3 %all_to_all.20.conv_ref = bf16[32,16,512]{2,1,0:T(8,128)(2,1)S(1)} all-to-all(bf16[32,16,512]{2,1,0:T(8,128)(2,1)S(1)} %conv.1), channel_id=1, replica_groups=mesh['ctx'=32,'tp'=8] {'ctx'}, dimensions={0} | all-to-all | bytes 1048576 | tf_op jit(solution)/shard_map/all_to_all | solution.py:147
  81.1 0.0 copy-done
  81.1 0.0 copy-done.2
  81.1 0.0 copy-done.4
  81.1 0.0 copy-done.8
  81.1 0.0 copy-done.9
  81.1 2.5 %project.1 = bf16[512,4096]{1,0:T(8,128)(2,1)S(1)} custom-call(bf16[32,16,512]{2,1,0:T(8,128)(2,1)S(1)} %all_to_all.20.conv_ref, bf16[512,512]{1,0:T(8,128)(2,1)S(1)} %copy-done.8, bf16[512,512]{1,0:T(8,128)(2,1)S(1)} %copy-done.2, bf16[512,512]{1,0:T(8,128)(2,1)S(1)} %copy-done.4, f32[1,512]{1,0:T(1,128)S(1)} %bitcast.3, bf16[512,4096]{1,0:T(8,128)(2,1)S(1)} %copy-done), custom_call_target="tpu_custom_call" | custom-call | tf_op jit(solution)/shard_map/project/pallas_call | solution.py:149
  83.6 55.0 %all_to_all.21 = bf16[8,64,4096]{2,1,0:T(8,128)(2,1)} all-to-all(bf16[8,64,4096]{2,1,0:T(8,128)(2,1)S(1)} %bitcast.2), channel_id=1, replica_groups=mesh['ctx'=32,'tp'=8] {'tp'}, dimensions={0} | all-to-all | bytes 8388608 | tf_op jit(solution)/shard_map/all_to_all | solution.py:153
  138.6 3.8 %reduce_sum.12 = bf16[64,4096]{1,0:T(8,128)(2,1)} reduce(bf16[8,64,4096]{2,1,0:T(8,128)(2,1)} %all_to_all.21, bf16[]{:T(256)} %constant.6.clone.1), dimensions={0}, to_apply=%region_0.0 | reduce | flops 1835008 | bytes 4718594 | tf_op jit(solution)/shard_map/reduce_sum | solution.py:155
  142.4 0.0 all-gather.2.cloned.1.call-update
  142.5 88.9 %all-gather.2.cloned.1.call-done = bf16[512,4096]{1,0:T(8,128)(2,1)} async-done(((bf16[64,4096]{1,0:T(8,128)(2,1)}), bf16[512,4096]{1,0:T(8,128)(2,1)}) %all-gather.2.cloned.1.call-update) | async-done | bytes 4194320 | tf_op jit(solution)/shard_map/all_gather | solution.py:156
  231.4 4.7 %copy.10 = bf16[512,4096]{1,0:T(8,128)(2,1)} copy(bf16[512,4096]{1,0:T(8,128)(2,1)} %all-gather.2.cloned.1.call-done) | data formatting | bytes 8388608
Async XLA Ops:
  6.5 224.8 %all-gather.2.cloned.1.call-start = ((), (), s32[]{:S(2)}) async-start(), calls=%async_computation.3 | async-start | bytes 4718592 | tf_op jit(solution)/shard_map/all_gather | solution.py:156
  6.5 1.0 copy-start.1
  7.6 1.0 copy-start.3
  8.6 1.0 copy-start.7
  9.7 71.4 %copy-start = (bf16[512,4096]{1,0:T(8,128)(2,1)S(1)}, bf16[512,4096]{1,0:T(8,128)(2,1)}, u32[]{:S(2)}) copy-start(bf16[512,4096]{1,0:T(8,128)(2,1)} %weight_ref.1) | copy-start | bytes 12582916
  9.7 71.4 %copy-start.2 = (bf16[512,512]{1,0:T(8,128)(2,1)S(1)}, bf16[512,512]{1,0:T(8,128)(2,1)}, u32[]{:S(2)}) copy-start(bf16[512,512]{1,0:T(8,128)(2,1)} %key_ref.3) | copy-start | bytes 1572868
  9.7 71.4 %copy-start.4 = (bf16[512,512]{1,0:T(8,128)(2,1)S(1)}, bf16[512,512]{1,0:T(8,128)(2,1)}, u32[]{:S(2)}) copy-start(bf16[512,512]{1,0:T(8,128)(2,1)} %value_ref.3) | copy-start | bytes 1572868
  49.4 1.2 copy-start.5
  50.6 1.2 copy-start.6
  51.8 29.3 %copy-start.8 = (bf16[512,512]{1,0:T(8,128)(2,1)S(1)}, bf16[512,512]{1,0:T(8,128)(2,1)}, u32[]{:S(2)}) copy-start(bf16[512,512]{1,0:T(8,128)(2,1)} %query_ref.1) | copy-start | bytes 1572868
  51.8 29.3 %copy-start.9 = (f32[512]{0:T(512)S(1)}, f32[512]{0:T(512)}, u32[]{:S(2)}) copy-start(f32[512]{0:T(512)} %param.12) | copy-start | bytes 6148
Sparse Core Ops, SparseCore 0:
  142.6 88.7 all-gather.1

commit v2 on v1

--- a/solution.py
+++ b/solution.py
@@ -9,8 +9,13 @@
 from jax.experimental.pallas import tpu as pltpu
 from jax.sharding import PartitionSpec as P
 
-VMEM_BYTES = 40 * 1024 * 1024
+VMEM_BYTES = 24 * 1024 * 1024
 GROUP = 4
+TP = 8
+CUTS = (0, 1408, 2688, 4096)
+ALONG_Z = [(i, i ^ 1) for i in range(TP)]
+UP_Y = [(i, (i + 2) % TP) for i in range(TP)]
+DOWN_Y = [(i, (i - 2) % TP) for i in range(TP)]
 
 
 def transform_tables(rows):
@@ -104,28 +109,97 @@
     out_ref[...] = conv.astype(jnp.bfloat16).reshape(blocks, share, rows)
 
 
-def project_kernel(conv_ref, query_ref, key_ref, value_ref, gain_ref, weight_ref, out_ref):
+def project_kernel(
+    order_ref, conv_ref, query_ref, key_ref, value_ref, gain_ref, weight_ref, *refs
+):
+    outs, (conv_rows, gated_rows) = refs[:-2], refs[-2:]
     rows, channels = query_ref.shape
-    conv = conv_ref[...].reshape(channels, rows).T.astype(jnp.float32)
-    mixer = key_ref[...].astype(jnp.float32) * value_ref[...].astype(jnp.float32)
-    mixer = mixer.astype(jnp.bfloat16).astype(jnp.float32)
-    gated = query_ref[...].astype(jnp.float32) * (conv + gain_ref[...] * mixer)
-    gated = gated.astype(jnp.bfloat16)
-    width = 1024
-    for start in range(0, out_ref.shape[1], width):
-        value = jnp.dot(
-            gated, weight_ref[:, start : start + width], preferred_element_type=jnp.float32
-        )
-        out_ref[:, start : start + width] = value.astype(jnp.bfloat16)
-
-
-def whole(kernel, out_shape, scratch=()):
+    conv_rows[...] = conv_ref[...].reshape(channels, rows).T
+    piece = rows // TP
+    for slot in range(TP):
+        here = pl.ds(pl.multiple_of(order_ref[slot] * piece, piece), piece)
+        mixer = key_ref[here, :].astype(jnp.float32) * value_ref[here, :].astype(jnp.float32)
+        mixer = mixer.astype(jnp.bfloat16).astype(jnp.float32)
+        total = conv_rows[here, :].astype(jnp.float32) + gain_ref[...] * mixer
+        gated = query_ref[here, :].astype(jnp.float32) * total
+        gated_rows[slot * piece : (slot + 1) * piece, :] = gated.astype(jnp.bfloat16)
+    gated = gated_rows[...]
+    for cut, start in enumerate(CUTS[:-1]):
+        columns = slice(start, CUTS[cut + 1])
+        value = jnp.dot(gated, weight_ref[:, columns], preferred_element_type=jnp.float32)
+        value = value.astype(jnp.bfloat16)
+        for slot in range(TP):
+            outs[slot][:, columns] = value[slot * piece : (slot + 1) * piece]
+
+
+def whole(kernel, shapes, scratch=(), scalars=0, operands=0):
+    several = isinstance(shapes, list)
+    out = [jax.ShapeDtypeStruct(shape, jnp.bfloat16) for shape in (shapes if several else [shapes])]
+    specs = {}
+    if scalars:
+        specs["in_specs"] = [pl.BlockSpec(memory_space=pltpu.SMEM)] * scalars + [
+            pl.BlockSpec(memory_space=pltpu.VMEM)
+        ] * operands
     return pl.pallas_call(
         kernel,
-        out_shape=jax.ShapeDtypeStruct(out_shape, jnp.bfloat16),
+        out_shape=out if several else out[0],
         scratch_shapes=list(scratch),
         compiler_params=pltpu.CompilerParams(vmem_limit_bytes=VMEM_BYTES),
-    )
+        **specs,
+    )
+
+
+def along_z(value):
+    return lax.ppermute(value, "tp", ALONG_Z)
+
+
+def up_y(value):
+    return lax.ppermute(value, "tp", UP_Y)
+
+
+def down_y(value):
+    return lax.ppermute(value, "tp", DOWN_Y)
+
+
+def add(*terms):
+    return sum(term.astype(jnp.float32) for term in terms).astype(jnp.bfloat16)
+
+
+def add_part(whole_value, part, cut):
+    first, last = CUTS[cut], CUTS[cut + 1]
+    return jnp.concatenate(
+        [whole_value[:, :first], add(whole_value[:, first:last], part), whole_value[:, last:]], 1
+    )
+
+
+def reduce_pieces(own, own_z, up, up_z, far, far_z, down, down_z):
+    first = far_z[:, CUTS[0] : CUTS[1]], far_z[:, CUTS[1] : CUTS[2]], far_z[:, CUTS[2] : CUTS[3]]
+    far = add_part(far, along_z(first[0]), 0)
+    down_z = add_part(down_z, down_y(first[1]), 1)
+    up_z = add_part(up_z, up_y(first[2]), 2)
+    from_z, from_up, from_down = along_z(up_z), down_y(down_z), up_y(far)
+    from_up, down = lax.optimization_barrier((from_up, down))
+    up = add(up, from_z, from_down)
+    own_z = add(own_z, from_up)
+    return add(own, along_z(own_z), up_y(up), down_y(down))
+
+
+def gather_pieces(own, order):
+    own_z, down, up = along_z(own), up_y(own), down_y(own)
+    up_z, down_z, far = along_z(up), up_y(own_z), down_y(up)
+    far_z = jnp.concatenate(
+        [
+            along_z(far[:, CUTS[0] : CUTS[1]]),
+            up_y(down_z[:, CUTS[1] : CUTS[2]]),
+            down_y(up_z[:, CUTS[2] : CUTS[3]]),
+        ],
+        1,
+    )
+    piece, columns = own.shape
+    out = jnp.zeros((TP * piece, columns), own.dtype)
+    for slot, value in enumerate((own, own_z, up, up_z, far, far_z, down, down_z)):
+        out = lax.dynamic_update_slice(out, value, (order[slot] * piece, 0))
+    return out
 
 
 def body(query_branch, key_branch, value_branch, filters, skip_gain, out_weight):
@@ -145,15 +219,22 @@
             arrived, forward, inverse
         )
     conv = lax.all_to_all(conv, "ctx", split_axis=0, concat_axis=0, tiled=True)
+    place = lax.axis_index("tp")
+    slots = jnp.arange(TP, dtype=jnp.int32)
+    order = (place // 2 + slots // 2) % (TP // 2) * 2 + (place + slots) % 2
+    piece = rows // TP
     with jax.named_scope("project"):
-        partial_value = whole(project_kernel, (rows, out_weight.shape[1]))(
-            conv, query_branch, key_branch, value_branch, skip_gain[None, :], out_weight
-        )
-    tp_count = lax.axis_size("tp")
-    pieces = lax.all_to_all(partial_value, "tp", split_axis=0, concat_axis=0, tiled=True)
-    pieces = pieces.reshape(tp_count, rows // tp_count, -1)
-    summed = pieces.astype(jnp.float32).sum(0).astype(jnp.bfloat16)
-    return lax.all_gather(summed, "tp", axis=0, tiled=True)
+        pieces = whole(
+            project_kernel,
+            [(piece, out_weight.shape[1])] * TP,
+            (pltpu.VMEM((rows, channels), jnp.bfloat16), pltpu.VMEM((rows, channels), jnp.bfloat16)),
+            scalars=1,
+            operands=6,
+        )(order, conv, query_branch, key_branch, value_branch, skip_gain[None, :], out_weight)
+    with jax.named_scope("reduce"):
+        summed = reduce_pieces(*pieces)
+    with jax.named_scope("gather"):
+        return gather_pieces(summed, order)
 
 
 def solution(mesh):

time: 244 us -> 163 us (0.67)
  blocking collectives: 117 us -> 39.2 us
  starting transfers between devices: 0.01 us -> 31 us
  waiting for transfers between devices: 88.9 us -> 59.8 us
  between operations: 13.4 us -> 5.24 us
  local copies, waits for them, and re-layouts: 10.3 us -> 13.6 us
    all_gather x1 -> x0, waiting for transfers between devices: 88.9 us -> none  [body(): return lax.all_gather(summed, 'tp', axis=0, tiled=True)]
    all_to_all x2 -> x0, blocking collectives: 77.3 us -> none  [the longest x1 55 us: body(): lax.all_to_all(partial_value, 'tp', split_axis=0, concat_axis=0, tiled=True)]
    ppermute x0 -> x18, waiting for transfers between devices: none -> 43.6 us  [the longest x6 26 us: down_y(): return lax.ppermute(value, 'tp', DOWN_Y)]
    ppermute x0 -> x18, starting transfers between devices: none -> 24.5 us  [the longest x6 15.4 us: down_y(): return lax.ppermute(value, 'tp', DOWN_Y)]
    all_to_all x0 -> x1, waiting for transfers between devices: none -> 16.2 us  [body(): conv = lax.all_to_all(conv, 'ctx', split_axis=0, concat_axis=0, tiled=True)]
    all_to_all x0 -> x1, starting transfers between devices: none -> 6.53 us  [body(): conv = lax.all_to_all(conv, 'ctx', split_axis=0, concat_axis=0, tiled=True)]
    dynamic_update_slice x0 -> x6, local copies, waits for them, and re-layouts: none -> 4.96 us  [gather_pieces(): out = lax.dynamic_update_slice(out, value, (order[slot] * piece, 0))]
    reduce_sum x1 -> x0, other arithmetic: 3.84 us -> none  [body(): summed = pieces.astype(jnp.float32).sum(0).astype(jnp.bfloat16)]
  transfers between devices with their start and end apart: 1 -> 19, of which waited for: 1 -> 11; matrix products, arithmetic and copies ran while one was open for 0% -> 4% of each run, Pallas kernels for 0% -> 0%
where the time goes in v2:
time: 163 us
  waiting for transfers between devices  59.8 us (37%)
  blocking collectives  39.2 us (24%)
  starting transfers between devices  31 us (19%)
  local copies, waits for them, and re-layouts  13.6 us (8%)
  Pallas kernels  11.4 us (7%)
  between operations  5.24 us (3%)
  other arithmetic  2.49 us (2%)
    all_to_all x1, blocking collectives, body(): lax.all_to_all(outgoing, 'ctx', split_axis=0, concat_axis=0, tiled=True)  39.2 us
    ppermute x6, waiting for transfers between devices, down_y(): return lax.ppermute(value, 'tp', DOWN_Y)  26 us
    all_to_all x1, waiting for transfers between devices, body(): conv = lax.all_to_all(conv, 'ctx', split_axis=0, concat_axis=0, tiled=True)  16.2 us
    ppermute x6, starting transfers between devices, down_y(): return lax.ppermute(value, 'tp', DOWN_Y)  15.4 us
    ppermute x6, waiting for transfers between devices, up_y(): return lax.ppermute(value, 'tp', UP_Y)  10.2 us
    pallas_call x1, Pallas kernels, body(): whole(conv_kernel, (ctx_count, share, rows), (spec, spec, spec))  7.69 us
    ppermute x6, waiting for transfers between devices, along_z(): return lax.ppermute(value, 'tp', ALONG_Z)  7.37 us
    unnamed x22, local copies, waits for them, and re-layouts  7.34 us
  transfers between devices with their start and end apart: 19, of which 11 were waited for; matrix products, arithmetic and copies ran while one was open for 4% of the time, Pallas kernels for 0%

profile of v2, /device:TPU:2, one launch (start us, length us, event | category | flops | bytes accessed | tf_op | source)
XLA Modules:
  0.0 162.9 jit_solution(5246723031939026243)
XLA Ops:
  0.0 1.0 copy-done.1
  1.0 1.0 copy-done.3
  2.1 1.0 copy-done.7
  3.5 39.2 %all_to_all.10.signal_ref = bf16[32,32,512]{2,1,0:T(8,128)(2,1)S(1)} all-to-all(bf16[32,32,512]{2,1,0:T(8,128)(2,1)S(1)} %pack.1), channel_id=1, replica_groups=mesh['ctx'=32,'tp'=8] {'ctx'}, dimensions={0} | all-to-all | bytes 2097152 | tf_op jit(solution)/shard_map/all_to_all | solution.py:215
  42.7 7.7 %conv.1 = bf16[32,16,512]{2,1,0:T(8,128)(2,1)} custom-call(bf16[32,32,512]{2,1,0:T(8,128)(2,1)S(1)} %all_to_all.10.signal_ref, bf16[512,1024]{1,0:T(8,128)(2,1)S(1)} %copy-done.5, bf16[1024,512]{1,0:T(8,128)(2,1)S(1)} %copy-done.6), custom_call_target="tpu_custom_call" | custom-call | tf_op jit(solution)/shard_map/conv/pallas_call | solution.py:218
  50.4 6.5 %all-to-all-start.1 = ((bf16[32,16,512]{2,1,0:T(8,128)(2,1)}), bf16[32,16,512]{2,1,0:T(8,128)(2,1)S(1)}, u32[]{:S(2)}, u32[]{:S(2)}) async-start(bf16[32,16,512]{2,1,0:T(8,128)(2,1)} %conv.1), calls=%async_computation.1 | async-start | bytes 1048576 | tf_op jit(solution)/shard_map/all_to_all | solution.py:221
  57.0 16.2 %all-to-all-done.1.conv_ref = bf16[32,16,512]{2,1,0:T(8,128)(2,1)S(1)} async-done(((bf16[32,16,512]{2,1,0:T(8,128)(2,1)}), bf16[32,16,512]{2,1,0:T(8,128)(2,1)S(1)}, u32[]{:S(2)}, u32[]{:S(2)}) %all-to-all-start.1) | async-done | bytes 524320 | tf_op jit(solution)/shard_map/all_to_all | solution.py:221
  73.2 2.2 %copy-done = bf16[512,4096]{1,0:T(8,128)(2,1)S(1)} copy-done((bf16[512,4096]{1,0:T(8,128)(2,1)S(1)}, bf16[512,4096]{1,0:T(8,128)(2,1)}, u32[]{:S(2)}) %copy-start) | copy-done | bytes 4194328
  75.4 3.4 %project.1 = (bf16[64,4096]{1,0:T(8,128)(2,1)S(1)}, bf16[64,4096]{1,0:T(8,128)(2,1)S(1)}, bf16[64,4096]{1,0:T(8,128)(2,1)S(1)}, bf16[64,4096]{1,0:T(8,128)(2,1)S...) custom-call(s32[8]{0:T(128)S(1)} %fusion.order_ref, ...), custom_call_target="tpu_custom_call" | custom-call | tf_op jit(solution)/shard_map/project/pallas_call | solution.py:227
  78.9 3.1 %collective-permute-start = (bf16[64,1280]{1,0:T(8,128)(2,1)S(1)}, bf16[64,1280]{1,0:T(8,128)(2,1)S(1)}, u32[]{:S(2)}, u32[]{:S(2)}) collective-permute-start(bf16[64,1280]{1,0:T(8,128)(2,1)S(1)} %slice.65), channel_id=1, source_target_pairs={{0,6},{1,7},{2,0},{3,1},{4,2},{5,3},{6,4},{7,5},{8,14},{9,15},{10,... | collective-permute-start | bytes 491528 | tf_op jit(solution)/shard_map/reduce/ppermute | solution.py:161
  82.3 4.2 %collective-permute-done = bf16[64,1280]{1,0:T(8,128)(2,1)S(1)} collective-permute-done((bf16[64,1280]{1,0:T(8,128)(2,1)S(1)}, bf16[64,1280]{1,0:T(8,128)(2,1)S(1)}, u32[]{:S(2)}, u32[]{:S(2)}) %collective-permute-start) | collective-permute-done | bytes 163872 | tf_op jit(solution)/shard_map/reduce/ppermute | solution.py:161
  86.6 3.8 %collective-permute-start.1 = (bf16[64,4096]{1,0:T(8,128)(2,1)S(1)}, bf16[64,4096]{1,0:T(8,128)(2,1)S(1)}, u32[]{:S(2)}, u32[]{:S(2)}) collective-permute-start(bf16[64,4096]{1,0:T(8,128)(2,1)S(1)} %pad_maximum_fusion), channel_id=1, source_target_pairs={{0,6},{1,7},{2,0},{3,1},{4,2},{5,3},{6,4},{7,5},{8,14},{9,15},{10,... | collective-permute-start | bytes 1572872 | tf_op jit(solution)/shard_map/reduce/ppermute | solution.py:161
  90.9 10.9 %collective-permute-done.1 = bf16[64,4096]{1,0:T(8,128)(2,1)S(1)} collective-permute-done((bf16[64,4096]{1,0:T(8,128)(2,1)S(1)}, bf16[64,4096]{1,0:T(8,128)(2,1)S(1)}, u32[]{:S(2)}, u32[]{:S(2)}) %collective-permute-start.1) | collective-permute-done | bytes 524320 | tf_op jit(solution)/shard_map/reduce/ppermute | solution.py:161
  102.0 4.0 %collective-permute-start.8 = (bf16[64,4096]{1,0:T(8,128)(2,1)S(1)}, bf16[64,4096]{1,0:T(8,128)(2,1)S(1)}, u32[]{:S(2)}, u32[]{:S(2)}) collective-permute-start(bf16[64,4096]{1,0:T(8,128)(2,1)S(1)} %get-tuple-element.24), channel_id=1, source_target_pairs={{0,6},{1,7},{2,0},{3,1},{4,2},{5,3},{6,4},{7,5},{8,14},{9,15},{10,... | collective-permute-start | bytes 1572872 | tf_op jit(solution)/shard_map/reduce/ppermute | solution.py:161
  106.0 1.0 add_convert_fusion.1
  108.3 7.4 %collective-permute-done.2 = bf16[64,4096]{1,0:T(8,128)(2,1)S(1)} collective-permute-done((bf16[64,4096]{1,0:T(8,128)(2,1)S(1)}, bf16[64,4096]{1,0:T(8,128)(2,1)S(1)}, u32[]{:S(2)}, u32[]{:S(2)}) %collective-permute-start.2) | collective-permute-done | bytes 524320 | tf_op jit(solution)/shard_map/reduce/ppermute | solution.py:153
  115.6 1.0 collective-permute-done.8
  116.6 4.6 %collective-permute-done.7 = bf16[64,4096]{1,0:T(8,128)(2,1)S(1)} collective-permute-done((bf16[64,4096]{1,0:T(8,128)(2,1)}, bf16[64,4096]{1,0:T(8,128)(2,1)S(1)}, u32[]{:S(2)}, u32[]{:S(2)}) %collective-permute-start.7) | collective-permute-done | bytes 524320 | tf_op jit(solution)/shard_map/reduce/ppermute | solution.py:157
  122.0 2.0 %copy-done.10 = bf16[512,4096]{1,0:T(8,128)(2,1)} copy-done((bf16[512,4096]{1,0:T(8,128)(2,1)}, bf16[512,4096]{1,0:T(8,128)(2,1)S(1)}, u32[]{:S(2)}) %copy-start.10) | copy-done | bytes 4194328
  124.0 1.5 collective-permute-start.9
  129.9 2.1 %collective-permute-start.17 = (bf16[64,4096]{1,0:T(8,128)(2,1)S(1)}, bf16[64,4096]{1,0:T(8,128)(2,1)S(1)}, u32[]{:S(2)}, u32[]{:S(2)}) collective-permute-start(bf16[64,4096]{1,0:T(8,128)(2,1)S(1)} %get-tuple-element.26), channel_id=1, source_target_pairs={{0,2},{1,3},{2,4},{3,5},{4,6},{5,7},{6,0},{7,1},{8,10},{9,11},{10,... | collective-permute-start | bytes 1572872 | tf_op jit(solution)/shard_map/gather/ppermute | solution.py:157
  132.0 4.0 %collective-permute-done.10 = bf16[64,4096]{1,0:T(8,128)(2,1)S(1)} collective-permute-done((bf16[64,4096]{1,0:T(8,128)(2,1)S(1)}, bf16[64,4096]{1,0:T(8,128)(2,1)S(1)}, u32[]{:S(2)}, u32[]{:S(2)}) %collective-permute-start.10) | collective-permute-done | bytes 524320 | tf_op jit(solution)/shard_map/gather/ppermute | solution.py:161
  135.9 1.2 collective-permute-start.11
  137.1 1.5 collective-permute-start.12
  138.6 1.3 collective-permute-start.14
  141.6 5.9 %collective-permute-done.12 = bf16[64,4096]{1,0:T(8,128)(2,1)S(1)} collective-permute-done((bf16[64,4096]{1,0:T(8,128)(2,1)S(1)}, bf16[64,4096]{1,0:T(8,128)(2,1)S(1)}, u32[]{:S(2)}, u32[]{:S(2)}) %collective-permute-start.12) | collective-permute-done | bytes 524320 | tf_op jit(solution)/shard_map/gather/ppermute | solution.py:161
  147.6 1.2 collective-permute-start.13
  148.8 3.1 %collective-permute-start.16 = (bf16[64,1408]{1,0:T(8,128)(2,1)S(1)}, bf16[64,1408]{1,0:T(8,128)(2,1)S(1)}, u32[]{:S(2)}, u32[]{:S(2)}) collective-permute-start(bf16[64,1408]{1,0:T(8,128)(2,1)S(1)} %slice.86), channel_id=1, source_target_pairs={{0,6},{1,7},{2,0},{3,1},{4,2},{5,3},{6,4},{7,5},{8,14},{9,15},{10,... | collective-permute-start | bytes 540680 | tf_op jit(solution)/shard_map/gather/ppermute | solution.py:161
  151.9 1.9 %collective-permute-done.14 = bf16[64,4096]{1,0:T(8,128)(2,1)S(1)} collective-permute-done((bf16[64,4096]{1,0:T(8,128)(2,1)S(1)}, bf16[64,4096]{1,0:T(8,128)(2,1)S(1)}, u32[]{:S(2)}, u32[]{:S(2)}) %collective-permute-start.14) | collective-permute-done | bytes 524320 | tf_op jit(solution)/shard_map/gather/ppermute | solution.py:157
  153.7 1.4 collective-permute-start.15
  156.8 3.6 %collective-permute-done.15 = bf16[64,1280]{1,0:T(8,128)(2,1)S(1)} collective-permute-done((bf16[64,1280]{1,0:T(8,128)(2,1)S(1)}, bf16[64,1280]{1,0:T(8,128)(2,1)S(1)}, u32[]{:S(2)}, u32[]{:S(2)}) %collective-permute-start.15) | collective-permute-done | bytes 163872 | tf_op jit(solution)/shard_map/gather/ppermute | solution.py:157
  160.4 0.8 maximum_dynamic-update-slice_fusion
  (59 shorter events, 7.9 us)
Async XLA Ops:
  0.0 1.0 copy-start.1
  1.0 1.0 copy-start.3
  2.1 1.0 copy-start.7
  3.1 39.6 %copy-start.5 = (bf16[512,1024]{1,0:T(8,128)(2,1)S(1)}, bf16[512,1024]{1,0:T(8,128)(2,1)}, u32[]{:S(2)}) copy-start(bf16[512,1024]{1,0:T(8,128)(2,1)} %constant.72.clone.forward_ref) | copy-start | bytes 3145732
  3.1 39.6 %copy-start.6 = (bf16[1024,512]{1,0:T(8,128)(2,1)S(1)}, bf16[1024,512]{1,0:T(8,128)(2,1)}, u32[]{:S(2)}) copy-start(bf16[1024,512]{1,0:T(8,128)(2,1)} %constant.73.clone.inverse_ref) | copy-start | bytes 3145732
  3.1 70.1 %copy-start.2 = (bf16[512,512]{1,0:T(8,128)(2,1)S(1)}, bf16[512,512]{1,0:T(8,128)(2,1)}, u32[]{:S(2)}) copy-start(bf16[512,512]{1,0:T(8,128)(2,1)} %key_ref.3) | copy-start | bytes 1572868
  3.1 70.1 %copy-start.4 = (bf16[512,512]{1,0:T(8,128)(2,1)S(1)}, bf16[512,512]{1,0:T(8,128)(2,1)}, u32[]{:S(2)}) copy-start(bf16[512,512]{1,0:T(8,128)(2,1)} %value_ref.3) | copy-start | bytes 1572868
  3.1 70.1 %copy-start.8 = (bf16[512,512]{1,0:T(8,128)(2,1)S(1)}, bf16[512,512]{1,0:T(8,128)(2,1)}, u32[]{:S(2)}) copy-start(bf16[512,512]{1,0:T(8,128)(2,1)} %query_ref.1) | copy-start | bytes 1572868
  3.1 70.1 %copy-start.9 = (f32[512]{0:T(512)S(1)}, f32[512]{0:T(512)}, u32[]{:S(2)}) copy-start(f32[512]{0:T(512)} %param.12) | copy-start | bytes 6148
  50.4 22.8 %all-to-all-start.1 = ((bf16[32,16,512]{2,1,0:T(8,128)(2,1)}), bf16[32,16,512]{2,1,0:T(8,128)(2,1)S(1)}, u32[]{:S(2)}, u32[]{:S(2)}) async-start(bf16[32,16,512]{2,1,0:T(8,128)(2,1)} %conv.1), calls=%async_computation.1 | async-start | bytes 1048576 | tf_op jit(solution)/shard_map/all_to_all | solution.py:221
  73.2 2.2 %copy-start = (bf16[512,4096]{1,0:T(8,128)(2,1)S(1)}, bf16[512,4096]{1,0:T(8,128)(2,1)}, u32[]{:S(2)}) copy-start(bf16[512,4096]{1,0:T(8,128)(2,1)} %weight_ref.1) | copy-start | bytes 12582916
  78.9 7.6 %collective-permute-start = (bf16[64,1280]{1,0:T(8,128)(2,1)S(1)}, bf16[64,1280]{1,0:T(8,128)(2,1)S(1)}, u32[]{:S(2)}, u32[]{:S(2)}) collective-permute-start(bf16[64,1280]{1,0:T(8,128)(2,1)S(1)} %slice.65), channel_id=1, source_target_pairs={{0,6},{1,7},{2,0},{3,1},{4,2},{5,3},{6,4},{7,5},{8,14},{9,15},{10,... | collective-permute-start | bytes 491528 | tf_op jit(solution)/shard_map/reduce/ppermute | solution.py:161
  82.0 8.5 %collective-permute-start.3 = (bf16[64,1408]{1,0:T(8,128)(2,1)S(1)}, bf16[64,1408]{1,0:T(8,128)(2,1)S(1)}, u32[]{:S(2)}, u32[]{:S(2)}) collective-permute-start(bf16[64,1408]{1,0:T(8,128)(2,1)S(1)} %get-tuple-element.27), channel_id=1, source_target_pairs={{0,2},{1,3},{2,4},{3,5},{4,6},{5,7},{6,0},{7,1},{8,10},{9,11},{10,... | collective-permute-start | bytes 540680 | tf_op jit(solution)/shard_map/reduce/ppermute | solution.py:157
  82.1 8.6 %collective-permute-start.5 = (bf16[64,1408]{1,0:T(8,128)(2,1)S(1)}, bf16[64,1408]{1,0:T(8,128)(2,1)S(1)}, u32[]{:S(2)}, u32[]{:S(2)}) collective-permute-start(bf16[64,1408]{1,0:T(8,128)(2,1)S(1)} %get-tuple-element.28), channel_id=1, source_target_pairs={{0,1},{1,0},{2,3},{3,2},{4,5},{5,4},{6,7},{7,6},{8,9},{9,8},{10,11... | collective-permute-start | bytes 540680 | tf_op jit(solution)/shard_map/reduce/ppermute | solution.py:153
  86.6 15.2 %collective-permute-start.1 = (bf16[64,4096]{1,0:T(8,128)(2,1)S(1)}, bf16[64,4096]{1,0:T(8,128)(2,1)S(1)}, u32[]{:S(2)}, u32[]{:S(2)}) collective-permute-start(bf16[64,4096]{1,0:T(8,128)(2,1)S(1)} %pad_maximum_fusion), channel_id=1, source_target_pairs={{0,6},{1,7},{2,0},{3,1},{4,2},{5,3},{6,4},{7,5},{8,14},{9,15},{10,... | collective-permute-start | bytes 1572872 | tf_op jit(solution)/shard_map/reduce/ppermute | solution.py:161
  90.6 15.4 %collective-permute-start.4 = (bf16[64,4096]{1,0:T(8,128)(2,1)S(1)}, bf16[64,4096]{1,0:T(8,128)(2,1)S(1)}, u32[]{:S(2)}, u32[]{:S(2)}) collective-permute-start(bf16[64,4096]{1,0:T(8,128)(2,1)S(1)} %pad_maximum_fusion.1), channel_id=1, source_target_pairs={{0,1},{1,0},{2,3},{3,2},{4,5},{5,4},{6,7},{7,6},{8,9},{9,8},{10,11... | collective-permute-start | bytes 1572872 | tf_op jit(solution)/shard_map/reduce/ppermute | solution.py:153
  90.8 15.2 %collective-permute-start.6 = (bf16[64,4096]{1,0:T(8,128)(2,1)S(1)}, bf16[64,4096]{1,0:T(8,128)(2,1)S(1)}, u32[]{:S(2)}, u32[]{:S(2)}) collective-permute-start(bf16[64,4096]{1,0:T(8,128)(2,1)S(1)} %pad_maximum_fusion.2), channel_id=1, source_target_pairs={{0,2},{1,3},{2,4},{3,5},{4,6},{5,7},{6,0},{7,1},{8,10},{9,11},{10,... | collective-permute-start | bytes 1572872 | tf_op jit(solution)/shard_map/reduce/ppermute | solution.py:157
  101.9 13.7 %collective-permute-start.2 = (bf16[64,4096]{1,0:T(8,128)(2,1)S(1)}, bf16[64,4096]{1,0:T(8,128)(2,1)S(1)}, u32[]{:S(2)}, u32[]{:S(2)}) collective-permute-start(bf16[64,4096]{1,0:T(8,128)(2,1)S(1)} %add_convert_fusion.2), channel_id=1, source_target_pairs={{0,1},{1,0},{2,3},{3,2},{4,5},{5,4},{6,7},{7,6},{8,9},{9,8},{10,11... | collective-permute-start | bytes 1572872 | tf_op jit(solution)/shard_map/reduce/ppermute | solution.py:153
  102.0 14.6 %collective-permute-start.8 = (bf16[64,4096]{1,0:T(8,128)(2,1)S(1)}, bf16[64,4096]{1,0:T(8,128)(2,1)S(1)}, u32[]{:S(2)}, u32[]{:S(2)}) collective-permute-start(bf16[64,4096]{1,0:T(8,128)(2,1)S(1)} %get-tuple-element.24), channel_id=1, source_target_pairs={{0,6},{1,7},{2,0},{3,1},{4,2},{5,3},{6,4},{7,5},{8,14},{9,15},{10,... | collective-permute-start | bytes 1572872 | tf_op jit(solution)/shard_map/reduce/ppermute | solution.py:161
  107.0 14.3 %collective-permute-start.7 = (bf16[64,4096]{1,0:T(8,128)(2,1)}, bf16[64,4096]{1,0:T(8,128)(2,1)S(1)}, u32[]{:S(2)}, u32[]{:S(2)}) collective-permute-start(bf16[64,4096]{1,0:T(8,128)(2,1)} %add_convert_fusion.1), channel_id=1, source_target_pairs={{0,2},{1,3},{2,4},{3,5},{4,6},{5,7},{6,0},{7,1},{8,10},{9,11},{10,... | collective-permute-start | bytes 1572872 | tf_op jit(solution)/shard_map/reduce/ppermute | solution.py:157
  122.0 2.0 %copy-start.10 = (bf16[512,4096]{1,0:T(8,128)(2,1)}, bf16[512,4096]{1,0:T(8,128)(2,1)S(1)}, u32[]{:S(2)}) copy-start(bf16[512,4096]{1,0:T(8,128)(2,1)S(1)} %get-tuple-element.25) | copy-start | bytes 12582916
  124.0 11.9 %collective-permute-start.10 = (bf16[64,4096]{1,0:T(8,128)(2,1)S(1)}, bf16[64,4096]{1,0:T(8,128)(2,1)S(1)}, u32[]{:S(2)}, u32[]{:S(2)}) collective-permute-start(bf16[64,4096]{1,0:T(8,128)(2,1)S(1)} %get-tuple-element.26), channel_id=1, source_target_pairs={{0,6},{1,7},{2,0},{3,1},{4,2},{5,3},{6,4},{7,5},{8,14},{9,15},{10,... | collective-permute-start | bytes 1572872 | tf_op jit(solution)/shard_map/gather/ppermute | solution.py:161
  124.0 14.6 %collective-permute-start.9 = (bf16[64,4096]{1,0:T(8,128)(2,1)S(1)}, bf16[64,4096]{1,0:T(8,128)(2,1)S(1)}, u32[]{:S(2)}, u32[]{:S(2)}) collective-permute-start(bf16[64,4096]{1,0:T(8,128)(2,1)S(1)} %get-tuple-element.26), channel_id=1, source_target_pairs={{0,1},{1,0},{2,3},{3,2},{4,5},{5,4},{6,7},{7,6},{8,9},{9,8},{10,11... | collective-permute-start | bytes 1572872 | tf_op jit(solution)/shard_map/gather/ppermute | solution.py:153
  129.9 31.3 %collective-permute-start.17 = (bf16[64,4096]{1,0:T(8,128)(2,1)S(1)}, bf16[64,4096]{1,0:T(8,128)(2,1)S(1)}, u32[]{:S(2)}, u32[]{:S(2)}) collective-permute-start(bf16[64,4096]{1,0:T(8,128)(2,1)S(1)} %get-tuple-element.26), channel_id=1, source_target_pairs={{0,2},{1,3},{2,4},{3,5},{4,6},{5,7},{6,0},{7,1},{8,10},{9,11},{10,... | collective-permute-start | bytes 1572872 | tf_op jit(solution)/shard_map/gather/ppermute | solution.py:157
  135.9 12.8 %collective-permute-start.11 = (bf16[64,4096]{1,0:T(8,128)(2,1)S(1)}, bf16[64,4096]{1,0:T(8,128)(2,1)S(1)}, u32[]{:S(2)}, u32[]{:S(2)}) collective-permute-start(bf16[64,4096]{1,0:T(8,128)(2,1)S(1)} %collective-permute-done.10), channel_id=1, source_target_pairs={{0,1},{1,0},{2,3},{3,2},{4,5},{5,4},{6,7},{7,6},{8,9},{9,8},{10,11... | collective-permute-start | bytes 1572872 | tf_op jit(solution)/shard_map/gather/ppermute | solution.py:153
  137.1 10.4 %collective-permute-start.12 = (bf16[64,4096]{1,0:T(8,128)(2,1)S(1)}, bf16[64,4096]{1,0:T(8,128)(2,1)S(1)}, u32[]{:S(2)}, u32[]{:S(2)}) collective-permute-start(bf16[64,4096]{1,0:T(8,128)(2,1)S(1)} %collective-permute-done.10), channel_id=1, source_target_pairs={{0,6},{1,7},{2,0},{3,1},{4,2},{5,3},{6,4},{7,5},{8,14},{9,15},{10,... | collective-permute-start | bytes 1572872 | tf_op jit(solution)/shard_map/gather/ppermute | solution.py:161
  138.6 15.1 %collective-permute-start.14 = (bf16[64,4096]{1,0:T(8,128)(2,1)S(1)}, bf16[64,4096]{1,0:T(8,128)(2,1)S(1)}, u32[]{:S(2)}, u32[]{:S(2)}) collective-permute-start(bf16[64,4096]{1,0:T(8,128)(2,1)S(1)} %collective-permute-done.9), channel_id=1, source_target_pairs={{0,2},{1,3},{2,4},{3,5},{4,6},{5,7},{6,0},{7,1},{8,10},{9,11},{10,... | collective-permute-start | bytes 1572872 | tf_op jit(solution)/shard_map/gather/ppermute | solution.py:157
  147.6 12.8 %collective-permute-start.13 = (bf16[64,1408]{1,0:T(8,128)(2,1)S(1)}, bf16[64,1408]{1,0:T(8,128)(2,1)S(1)}, u32[]{:S(2)}, u32[]{:S(2)}) collective-permute-start(bf16[64,1408]{1,0:T(8,128)(2,1)S(1)} %slice.84), channel_id=1, source_target_pairs={{0,1},{1,0},{2,3},{3,2},{4,5},{5,4},{6,7},{7,6},{8,9},{9,8},{10,11... | collective-permute-start | bytes 540680 | tf_op jit(solution)/shard_map/gather/ppermute | solution.py:153
  148.8 11.6 %collective-permute-start.16 = (bf16[64,1408]{1,0:T(8,128)(2,1)S(1)}, bf16[64,1408]{1,0:T(8,128)(2,1)S(1)}, u32[]{:S(2)}, u32[]{:S(2)}) collective-permute-start(bf16[64,1408]{1,0:T(8,128)(2,1)S(1)} %slice.86), channel_id=1, source_target_pairs={{0,6},{1,7},{2,0},{3,1},{4,2},{5,3},{6,4},{7,5},{8,14},{9,15},{10,... | collective-permute-start | bytes 540680 | tf_op jit(solution)/shard_map/gather/ppermute | solution.py:161
  153.7 6.6 %collective-permute-start.15 = (bf16[64,1280]{1,0:T(8,128)(2,1)S(1)}, bf16[64,1280]{1,0:T(8,128)(2,1)S(1)}, u32[]{:S(2)}, u32[]{:S(2)}) collective-permute-start(bf16[64,1280]{1,0:T(8,128)(2,1)S(1)} %slice.85), channel_id=1, source_target_pairs={{0,2},{1,3},{2,4},{3,5},{4,6},{5,7},{6,0},{7,1},{8,10},{9,11},{10,... | collective-permute-start | bytes 491528 | tf_op jit(solution)/shard_map/gather/ppermute | solution.py:157

commit v3 on v1

--- a/solution.py
+++ b/solution.py
@@ -1,3 +1,4 @@
+import functools
 import math
 
 import jax
@@ -7,10 +8,12 @@
 from jax import lax
 from jax.experimental import pallas as pl
 from jax.experimental.pallas import tpu as pltpu
-from jax.sharding import PartitionSpec as P
-
-VMEM_BYTES = 40 * 1024 * 1024
+from jax.sharding import Mesh, PartitionSpec as P
+
+MIB = 1024 * 1024
 GROUP = 4
+CUTS = (0, 1408, 2688, 4096)
+CTX_Y = ("block", "core", "y")
 
 
 def transform_tables(rows):
@@ -23,15 +26,48 @@
     return forward.astype(ml_dtypes.bfloat16), inverse.astype(ml_dtypes.bfloat16)
 
 
-def pack_kernel(key_ref, value_ref, filter_ref, out_ref):
+def pack_kernel(
+    key_hbm, value_hbm, filter_hbm, query_hbm, weight_hbm,
+    out_ref, half_hbm, up_hbm, down_hbm, far_hbm, key_ref, value_ref, filter_ref, sems,
+):
     parts, both, rows = out_ref.shape
     share = both // 2
+    half, quarter = half_hbm.shape[0], up_hbm.shape[0]
+
+    core, y = lax.axis_index("core"), lax.axis_index("y")
+
+    def rows_of(ref, index, count):
+        return ref.at[pl.ds(pl.multiple_of(index * count, count), count)]
+
+    copies = [
+        pltpu.make_async_copy(source, target, sems.at[i])
+        for i, (source, target) in enumerate(
+            (
+                (key_hbm, key_ref),
+                (value_hbm, value_ref),
+                (filter_hbm, filter_ref),
+                (rows_of(weight_hbm, core, half), half_hbm),
+                (rows_of(query_hbm, (y + 1) % 4, quarter), up_hbm),
+                (rows_of(query_hbm, (y + 3) % 4, quarter), down_hbm),
+                (rows_of(query_hbm, (y + 2) % 4, quarter), far_hbm),
+            )
+        )
+    ]
+    for copy in copies:
+        copy.start()
+    copies[0].wait()
+    copies[1].wait()
     mixer = key_ref[...].astype(jnp.float32) * value_ref[...].astype(jnp.float32)
     out_ref[:, :share, :] = mixer.astype(jnp.bfloat16).T.reshape(parts, share, rows)
+    copies[2].wait()
     out_ref[:, share:, :] = filter_ref[...].T.reshape(parts, share, rows)
-
-
-def conv_kernel(signal_ref, forward_ref, inverse_ref, out_ref, mixer_spec, filter_spec, product):
+    for copy in copies[3:]:
+        copy.wait()
+
+
+def conv_kernel(
+    signal_ref, gain_ref, forward_ref, inverse_ref, out_ref, mixer_spec, filter_spec, product
+):
     blocks, both, rows = signal_ref.shape
     share = both // 2
     forward = forward_ref[...]
@@ -101,70 +137,212 @@
     lax.fori_loop(0, (share // 8) * lane_tiles, tile, 0)
     flat = product[...].astype(jnp.bfloat16).reshape(blocks * share, 2 * rows)
     conv = jnp.dot(flat, inverse_ref[...], preferred_element_type=jnp.float32)
-    out_ref[...] = conv.astype(jnp.bfloat16).reshape(blocks, share, rows)
-
-
-def project_kernel(conv_ref, query_ref, key_ref, value_ref, gain_ref, weight_ref, out_ref):
-    rows, channels = query_ref.shape
-    conv = conv_ref[...].reshape(channels, rows).T.astype(jnp.float32)
-    mixer = key_ref[...].astype(jnp.float32) * value_ref[...].astype(jnp.float32)
-    mixer = mixer.astype(jnp.bfloat16).astype(jnp.float32)
-    gated = query_ref[...].astype(jnp.float32) * (conv + gain_ref[...] * mixer)
-    gated = gated.astype(jnp.bfloat16)
-    width = 1024
-    for start in range(0, out_ref.shape[1], width):
-        value = jnp.dot(
-            gated, weight_ref[:, start : start + width], preferred_element_type=jnp.float32
-        )
-        out_ref[:, start : start + width] = value.astype(jnp.bfloat16)
-
-
-def whole(kernel, out_shape, scratch=()):
+    mixer = signal_ref[:, :share, :].astype(jnp.float32)
+    total = (conv.reshape(blocks, share, rows) + gain_ref[...] * mixer).astype(jnp.bfloat16)
+    quarters, width = out_ref.shape[1], out_ref.shape[3]
+    for quarter in range(quarters):
+        out_ref[:, quarter] = total[:, :, quarter * width : (quarter + 1) * width]
+
+
+def gate(total_ref, query_ref, up_ref, down_ref, far_ref, out_ref, gated_ref):
+    blocks, groups, share, rows = total_ref.shape
+    half = blocks * share // 2
+    core, y, keep = lax.axis_index("core"), lax.axis_index("y"), lax.axis_index("z")
+    own = query_ref.at[pl.ds(pl.multiple_of(y * rows, rows), rows)]
+    sources = (own, y), (up_ref, (y + 3) % 4), (down_ref, (y + 1) % 4), (far_ref, (y + 2) % 4)
+    for group, (query, source) in enumerate(sources):
+        for part in range(2):
+            side = part if group == 0 else (core if part == 0 else 1 - core)
+            total = total_ref[pl.ds(side * (blocks // 2), blocks // 2), source]
+            total = total.reshape(half, rows).T.astype(jnp.float32)
+            channels = side * half if group == 0 else pl.multiple_of(side * half, half)
+            value = query[:, pl.ds(channels, half)].astype(jnp.float32) * total
+            start = (2 * group + part) * half
+            gated_ref[:, start : start + half] = value.astype(jnp.bfloat16)
+    piece = rows // 2
+    out_ref[:piece] = gated_ref[pl.ds(pl.multiple_of((1 - keep) * piece, piece), piece), :]
+    out_ref[piece:] = gated_ref[pl.ds(pl.multiple_of(keep * piece, piece), piece), :]
+
+
+def project_kernel(first, prepare, *refs):
+    count = 5 if prepare else 1
+    weights, rest = refs[count : count + 9], refs[count + 9 :]
+    if prepare:
+        other_ref, own_ref, gated_ref, _, buffer, sems, rows_ref = rest
+    else:
+        gated_ref = refs[0]
+        other_ref, own_ref, buffer, sems = rest
+    piece, columns = other_ref.shape
+    slots, _, width = buffer.shape
+    steps = columns // width
+
+    def copies(step):
+        start, made = 0, []
+        for i, weight in enumerate(weights):
+            depth = weight.shape[0]
+            source = weight.at[:, pl.ds(first + step * width, width)]
+            target = buffer.at[step % slots, pl.ds(start, depth)]
+            made.append(pltpu.make_async_copy(source, target, sems.at[step % slots, i]))
+            start += depth
+        return made
+
+    for step in range(min(slots, steps)):
+        for copy in copies(step):
+            copy.start()
+    if prepare:
+        gate(*refs[:5], gated_ref, rows_ref)
+    gated = gated_ref[...]
+    for step in range(steps):
+        for copy in copies(step):
+            copy.wait()
+        value = jnp.dot(gated, buffer[step % slots], preferred_element_type=jnp.float32)
+        value = value.astype(jnp.bfloat16)
+        other_ref[:, step * width : (step + 1) * width] = value[:piece]
+        own_ref[:, step * width : (step + 1) * width] = value[piece:]
+        if step + slots < steps:
+            for copy in copies(step + slots):
+                copy.start()
+
+
+VMEM = pl.BlockSpec(memory_space=pltpu.VMEM)
+HBM = pl.BlockSpec(memory_space=pltpu.HBM)
+
+
+def whole(kernel, shapes, in_specs, out_specs, scratch=(), limit=16):
     return pl.pallas_call(
         kernel,
-        out_shape=jax.ShapeDtypeStruct(out_shape, jnp.bfloat16),
+        out_shape=[jax.ShapeDtypeStruct(shape, jnp.bfloat16) for shape in shapes],
+        in_specs=in_specs,
+        out_specs=out_specs,
         scratch_shapes=list(scratch),
-        compiler_params=pltpu.CompilerParams(vmem_limit_bytes=VMEM_BYTES),
+        compiler_params=pltpu.CompilerParams(vmem_limit_bytes=limit * MIB),
     )
 
 
+def project(operands, weights, first, last, prepare, width=512, slots=3):
+    features = last - first
+    rows, depth = operands[0].shape[3] if prepare else operands[0].shape[0], 0
+    depth = sum(weight.shape[0] for weight in weights)
+    shapes = [(rows // 2, features)] * 2
+    scratch = [
+        pltpu.VMEM((slots, depth, width), jnp.bfloat16),
+        pltpu.SemaphoreType.DMA((slots, len(weights))),
+    ]
+    if prepare:
+        shapes += [(rows, depth), (rows * lax.axis_size("y"), features)]
+        scratch.append(pltpu.VMEM((rows, depth), jnp.bfloat16))
+    return whole(
+        functools.partial(project_kernel, first, prepare),
+        shapes,
+        [VMEM] * len(operands) + [HBM] * len(weights),
+        [VMEM] * 3 + [HBM] if prepare else [VMEM] * 2,
+        scratch,
+        limit=16,
+    )(*operands, *weights)
+
+
+def swap(axis):
+    return lambda value: lax.ppermute(value, axis, [(0, 1), (1, 0)])
+
+
+along_z, along_core = swap("z"), swap("core")
+
+
+def along_y(value, steps):
+    count = lax.axis_size("y")
+    return lax.ppermute(value, "y", [(i, (i + steps) % count) for i in range(count)])
+
+
+def add(*terms):
+    return sum(term.astype(jnp.float32) for term in terms).astype(jnp.bfloat16)
+
+
+def gather_pieces(own, order, out):
+    own_z, down, up = along_z(own), along_y(own, 1), along_y(own, -1)
+    up_z, down_z, far = along_z(up), along_y(own_z, 1), along_y(up, -1)
+    far_z = jnp.concatenate(
+        [
+            along_z(far[:, CUTS[0] : CUTS[1]]),
+            along_y(down_z[:, CUTS[1] : CUTS[2]], 1),
+            along_y(up_z[:, CUTS[2] : CUTS[3]], -1),
+        ],
+        1,
+    )
+    for slot, value in enumerate((own, own_z, up, up_z, far, far_z, down, down_z)):
+        out = lax.dynamic_update_slice(out, value, (order[slot] * own.shape[0], 0))
+    return out
+
+
 def body(query_branch, key_branch, value_branch, filters, skip_gain, out_weight):
-    ctx_count = lax.axis_size("ctx")
+    core, y, z = (lax.axis_index(name) for name in ("core", "y", "z"))
+    ctx = lax.axis_index("block") * 2 + core
+    ctx_count = lax.axis_size("block") * 2
+    y_count = lax.axis_size("y")
     rows, channels = query_branch.shape
     share = channels // ctx_count
+    features = out_weight.shape[1]
+    quarter = rows // y_count
     forward, inverse = (jnp.asarray(table) for table in transform_tables(rows))
+    gain = lax.dynamic_slice(skip_gain, (ctx * share,), (share,))[:, None]
 
     with jax.named_scope("pack"):
-        outgoing = whole(pack_kernel, (ctx_count, 2 * share, rows))(
-            key_branch, value_branch, filters
-        )
-    arrived = lax.all_to_all(outgoing, "ctx", split_axis=0, concat_axis=0, tiled=True)
+        square = pltpu.VMEM((rows, channels), jnp.bfloat16)
+        outgoing, weight_half, to_up, to_down, to_far = whole(
+            pack_kernel,
+            [(ctx_count, 2 * share, rows), (channels // 2, features)] + [(quarter, channels)] * 3,
+            [HBM] * 5,
+            [VMEM] + [HBM] * 4,
+            [square, square, square, pltpu.SemaphoreType.DMA((7,))],
+            limit=60,
+        )(key_branch, value_branch, filters, query_branch, out_weight)
+    with jax.named_scope("weights"):
+        weight_up, weight_down = along_y(weight_half, 1), along_y(weight_half, -1)
+        query_up, query_down = along_y(to_up, 1), along_y(to_down, -1)
+        query_far = along_y(to_far, 2)
+    arrived = lax.all_to_all(outgoing, ("block", "core"), split_axis=0, concat_axis=0, tiled=True)
     spec = pltpu.VMEM((ctx_count, share, 2 * rows), jnp.float32)
     with jax.named_scope("conv"):
-        conv = whole(conv_kernel, (ctx_count, share, rows), (spec, spec, spec))(
-            arrived, forward, inverse
+        (total,) = whole(
+            conv_kernel,
+            [(ctx_count, y_count, share, quarter)],
+            [VMEM] * 4,
+            [VMEM],
+            [spec] * 3,
+            limit=24,
+        )(arrived, gain, forward, inverse)
+    with jax.named_scope("weights"):
+        total, weight_up, weight_down, query_up, query_down, query_far = lax.optimization_barrier(
+            (total, weight_up, weight_down, query_up, query_down, query_far)
         )
-    conv = lax.all_to_all(conv, "ctx", split_axis=0, concat_axis=0, tiled=True)
+        cut = channels // 4
+        far_first, far_last = along_y(weight_up[:cut], 1), along_y(weight_down[cut:], -1)
+        swapped_up, swapped_down = along_core(weight_up), along_core(weight_down)
+    total = lax.all_to_all(
+        total.reshape(ctx_count * y_count, share, quarter), CTX_Y, split_axis=0, concat_axis=0,
+        tiled=True,
+    ).reshape(ctx_count, y_count, share, quarter)
+    with jax.named_scope("weights"):
+        total, far_first, far_last = lax.optimization_barrier((total, far_first, far_last))
+        swapped_first, swapped_last = along_core(far_first), along_core(far_last)
+    weights = (
+        out_weight, weight_up, swapped_up, weight_down, swapped_down,
+        far_first, far_last, swapped_first, swapped_last,
+    )
     with jax.named_scope("project"):
-        partial_value = whole(project_kernel, (rows, out_weight.shape[1]))(
-            conv, query_branch, key_branch, value_branch, skip_gain[None, :], out_weight
-        )
-    tp_count = lax.axis_size("tp")
-    pieces = lax.all_to_all(partial_value, "tp", split_axis=0, concat_axis=0, tiled=True)
-    pieces = pieces.reshape(tp_count, rows // tp_count, -1)
-    summed = pieces.astype(jnp.float32).sum(0).astype(jnp.bfloat16)
-    return lax.all_gather(summed, "tp", axis=0, tiled=True)
+        operands = (total, query_branch, query_up, query_down, query_far)
+        other, own, _, blank = project(operands, weights, 0, features, True)
+    with jax.named_scope("reduce"):
+        summed = add(own, along_z(other))
+    slots = jnp.arange(2 * y_count, dtype=jnp.int32)
+    order = (y + slots // 2) % y_count * 2 + (z + slots) % 2
+    with jax.named_scope("gather"):
+        return gather_pieces(summed, order, blank)
 
 
 def solution(mesh):
-    placed = (
-        P("ctx", "tp"),
-        P("ctx", "tp"),
-        P("ctx", "tp"),
-        P("ctx", "tp"),
-        P("tp"),
-        P("tp", None),
+    fine = Mesh(mesh.devices.reshape(-1, 2, 4, 2), ("block", "core", "y", "z"))
+    ctx, tp = ("block", "core"), ("y", "z")
+    placed = (P(ctx, tp), P(ctx, tp), P(ctx, tp), P(ctx, tp), P(tp), P(tp, None))
+    return jax.shard_map(
+        body, mesh=fine, in_specs=placed, out_specs=P(ctx, None), check_vma=False
     )
-    return jax.shard_map(
-        body, mesh=mesh, in_specs=placed, out_specs=P("ctx", None), check_vma=False
-    )

time: 244 us -> 239 us (0.980)
  blocking collectives: 117 us -> 33 us
  Pallas kernels: 9.74 us -> 91 us
  starting transfers between devices: 0.01 us -> 36.4 us
  waiting for transfers between devices: 88.9 us -> 61.3 us
  between operations: 13.4 us -> 5.15 us
    all_gather x1 -> x0, waiting for transfers between devices: 88.9 us -> none  [body(): return lax.all_gather(summed, 'tp', axis=0, tiled=True)]
    all_to_all x3 -> x1, blocking collectives: 117 us -> 33 us  [body(): lax.all_to_all(total.reshape(ctx_count * y_count, share, quarter), CTX_Y,...]
    pallas_call x3, Pallas kernels: 9.74 us -> 91 us  [the longest x1 77.6 us: body(): whole(pack_kernel, [(ctx_count, 2 * share, rows), (channels // 2, feature...]
    ppermute x0 -> x21, waiting for transfers between devices: none -> 37.8 us  [the longest x13 22.6 us: along_y(): lax.ppermute(value, 'y', [(i, (i + steps) % count) for i in range(count)])]
    ppermute x0 -> x21, starting transfers between devices: none -> 24.8 us  [the longest x13 19.4 us: along_y(): lax.ppermute(value, 'y', [(i, (i + steps) % count) for i in range(count)])]
    all_to_all x0 -> x1, waiting for transfers between devices: none -> 23.4 us  [body(): lax.all_to_all(outgoing, ('block', 'core'), split_axis=0, concat_axis=0,...]
    all_to_all x0 -> x1, starting transfers between devices: none -> 11.6 us  [body(): lax.all_to_all(outgoing, ('block', 'core'), split_axis=0, concat_axis=0,...]
    unnamed x21 -> x10, local copies, waits for them, and re-layouts: 10.3 us -> 2.46 us
  transfers between devices with their start and end apart: 1 -> 22, of which waited for: 1 -> 10; matrix products, arithmetic and copies ran while one was open for 0% -> 3% of each run, Pallas kernels for 0% -> 3%
where the time goes in v3:
time: 239 us; the launch traced here: 238 us
  Pallas kernels  91 us (38%)
  waiting for transfers between devices  61.3 us (26%)
  starting transfers between devices  36.4 us (15%)
  blocking collectives  33 us (14%)
  local copies, waits for them, and re-layouts  9.7 us (4%)
  between operations  5.15 us (2%)
    pallas_call x1, Pallas kernels, body(): whole(pack_kernel, [(ctx_count, 2 * share, rows), (channels // 2, feature...  77.6 us
    all_to_all x1, blocking collectives, body(): lax.all_to_all(total.reshape(ctx_count * y_count, share, quarter), CTX_Y,...  33 us
    all_to_all x1, waiting for transfers between devices, body(): lax.all_to_all(outgoing, ('block', 'core'), split_axis=0, concat_axis=0,...  23.4 us
    ppermute x13, waiting for transfers between devices, along_y(): lax.ppermute(value, 'y', [(i, (i + steps) % count) for i in range(count)])  22.6 us
    ppermute x13, starting transfers between devices, along_y(): lax.ppermute(value, 'y', [(i, (i + steps) % count) for i in range(count)])  19.4 us
    ppermute x8, waiting for transfers between devices, swap(): return lambda value: lax.ppermute(value, axis, [(0, 1), (1, 0)])  15.3 us
    all_to_all x1, starting transfers between devices, body(): lax.all_to_all(outgoing, ('block', 'core'), split_axis=0, concat_axis=0,...  11.6 us
    pallas_call x1, Pallas kernels, body(): whole(conv_kernel, [(ctx_count, y_count, share, quarter)], [VMEM] * 4, [V...  6.92 us
  transfers between devices with their start and end apart: 22, of which 10 were waited for; matrix products, arithmetic and copies ran while one was open for 3% of the time, Pallas kernels for 3%

profile of v3, /device:TPU:2, one launch (start us, length us, event | category | flops | bytes accessed | tf_op | source)
XLA Modules:
  0.0 238.3 jit_solution(9263410749384294431)
XLA Ops:
  0.0 77.6 %pack.1 = (bf16[32,32,512]{2,1,0:T(8,128)(2,1)}, bf16[256,4096]{1,0:T(8,128)(2,1)}, bf16[128,512]{1,0:T(8,128)(2,1)}, bf16[128,512]{1,0:T(8,128)(2,1)}, bf16[128,512]{1,0:T(8,128)(2,1)}) custom-call(bf16[512,512]{1,0:T(8,128)(2,1)} %key_hbm.1, bf16[512,512]{1,0:T(8,128)(2,1)} %value_hbm.1, bf16[512,512]{1,0:T(8,128)(2,1)} %filter_hbm.1, ...), custom_call_target="tpu_custom_call" | custom-call | tf_op jit(solution)/shard_map/pack/pallas_call | solution.py:290
  77.6 1.7 collective-permute-start
  79.3 1.7 collective-permute-start.1
  80.9 11.6 %all-to-all-start = ((bf16[32,32,512]{2,1,0:T(8,128)(2,1)}), bf16[32,32,512]{2,1,0:T(8,128)(2,1)S(1)}, u32[]{:S(2)}, u32[]{:S(2)}) async-start(bf16[32,32,512]{2,1,0:T(8,128)(2,1)} %get-tuple-element.22), calls=%async_computation | async-start | bytes 2097152 | tf_op jit(solution)/shard_map/all_to_all | solution.py:302
  93.0 2.9 %collective-permute-start.3 = (bf16[128,512]{1,0:T(8,128)(2,1)}, bf16[128,512]{1,0:T(8,128)(2,1)S(1)}, u32[]{:S(2)}, u32[]{:S(2)}) collective-permute-start(bf16[128,512]{1,0:T(8,128)(2,1)} %get-tuple-element.25), channel_id=1, source_target_pairs={{0,6},{2,0},{4,2},{6,4},{1,7},{3,1},{5,3},{7,5},{8,14},{10,8},{12,... | collective-permute-start | bytes 393224 | tf_op jit(solution)/shard_map/weights/ppermute | solution.py:253
  96.8 23.4 %all-to-all-done.signal_ref = bf16[32,32,512]{2,1,0:T(8,128)(2,1)S(1)} async-done(((bf16[32,32,512]{2,1,0:T(8,128)(2,1)}), bf16[32,32,512]{2,1,0:T(8,128)(2,1)S(1)}, u32[]{:S(2)}, u32[]{:S(2)}) %all-to-all-start) | async-done | bytes 1048608 | tf_op jit(solution)/shard_map/all_to_all | solution.py:302
  120.2 1.2 copy-done.3
  121.4 1.2 copy-done.4
  122.7 6.9 %conv.1 = bf16[32,4,16,128]{3,2,1,0:T(8,128)(2,1)S(1)} custom-call(bf16[32,32,512]{2,1,0:T(8,128)(2,1)S(1)} %all-to-all-done.signal_ref, f32[16,1]{1,0:T(8,128)S(1)} %copy.9.gain_ref, bf16[512,1024]{1,0:T(8,128)(2,1)S(1)} %copy-done.3, bf16[1024,512]{1,0:T(8,128)(2,1)S(1)} %copy-done.4), custom_call_target="tpu_custom_call" | custom-call | tf_op jit(solution)/shard_map/conv/pallas_call | solution.py:305
  129.6 2.0 collective-permute-done.3.refs_3_
  131.6 1.7 collective-permute-done.4.refs_4_
  133.4 1.2 collective-permute-start.5
  134.6 1.3 slice.40
  136.0 2.2 collective-permute-start.6
  138.6 33.0 %all_to_all.10 = bf16[128,16,128]{2,1,0:T(8,128)(2,1)S(1)} all-to-all(bf16[128,16,128]{2,1,0:T(8,128)(2,1)S(1)} %bitcast.13), channel_id=1, replica_groups=mesh['block'=16,'core'=2,'y'=4,'z'=2] {'block','core','y'}, dimensions={0} | all-to-all | bytes 1048576 | tf_op jit(solution)/shard_map/all_to_all | solution.py:320
  172.1 2.1 collective-permute-done.10.refs_13_
  174.3 1.5 collective-permute-done.9.refs_12_
  175.8 6.5 %project.1 = (bf16[64,4096]{1,0:T(8,128)(2,1)S(1)}, bf16[64,4096]{1,0:T(8,128)(2,1)S(1)}, bf16[128,2048]{1,0:T(8,128)(2,1)}, bf16[512,4096]{1,0:T(8,128)(2,1)}) custom-call(bf16[32,4,16,128]{3,2,1,0:T(8,128)(2,1)S(1)} %bitcast.12, bf16[512,512]{1,0:T(8,128)(2,1)S(1)} %copy-done.2, bf16[128,512]{1,0:T(8,128)(2,1)S(1)} %collective-permute-done.2.refs_2_, ...), custom_call_target="tpu_custom_call" | custom-call | tf_op jit(solution)/shard_map/project/pallas_call | solution.py:234
  182.3 1.2 collective-permute-start.11
  184.7 11.6 %collective-permute-done.11 = bf16[64,4096]{1,0:T(8,128)(2,1)S(1)} collective-permute-done((bf16[64,4096]{1,0:T(8,128)(2,1)S(1)}, bf16[64,4096]{1,0:T(8,128)(2,1)S(1)}, u32[]{:S(2)}, u32[]{:S(2)}) %collective-permute-start.11) | collective-permute-done | bytes 524320 | tf_op jit(solution)/shard_map/reduce/ppermute | solution.py:245
  196.3 0.9 constant_dynamic-update-slice_fusion.6
  197.3 1.2 collective-permute-start.13
  198.5 0.9 collective-permute-start.12
  203.8 1.1 collective-permute-start.20
  204.9 5.5 %collective-permute-done.13 = bf16[64,4096]{1,0:T(8,128)(2,1)S(1)} collective-permute-done((bf16[64,4096]{1,0:T(8,128)(2,1)S(1)}, bf16[64,4096]{1,0:T(8,128)(2,1)S(1)}, u32[]{:S(2)}, u32[]{:S(2)}) %collective-permute-start.13) | collective-permute-done | bytes 524320 | tf_op jit(solution)/shard_map/gather/ppermute | solution.py:253
  210.4 1.1 collective-permute-start.14
  211.5 2.5 %collective-permute-start.15 = (bf16[64,4096]{1,0:T(8,128)(2,1)S(1)}, bf16[64,4096]{1,0:T(8,128)(2,1)S(1)}, u32[]{:S(2)}, u32[]{:S(2)}) collective-permute-start(bf16[64,4096]{1,0:T(8,128)(2,1)S(1)} %collective-permute-done.13), channel_id=1, source_target_pairs={{0,6},{2,0},{4,2},{6,4},{1,7},{3,1},{5,3},{7,5},{8,14},{10,8},{12,... | collective-permute-start | bytes 1572872 | tf_op jit(solution)/shard_map/gather/ppermute | solution.py:253
  215.6 8.1 %collective-permute-done.15 = bf16[64,4096]{1,0:T(8,128)(2,1)S(1)} collective-permute-done((bf16[64,4096]{1,0:T(8,128)(2,1)S(1)}, bf16[64,4096]{1,0:T(8,128)(2,1)S(1)}, u32[]{:S(2)}, u32[]{:S(2)}) %collective-permute-start.15) | collective-permute-done | bytes 524320 | tf_op jit(solution)/shard_map/gather/ppermute | solution.py:253
  223.7 1.3 collective-permute-start.16
  225.0 3.8 %collective-permute-start.19 = (bf16[64,1408]{1,0:T(8,128)(2,1)S(1)}, bf16[64,1408]{1,0:T(8,128)(2,1)S(1)}, u32[]{:S(2)}, u32[]{:S(2)}) collective-permute-start(bf16[64,1408]{1,0:T(8,128)(2,1)S(1)} %slice.54), channel_id=1, source_target_pairs={{0,6},{2,0},{4,2},{6,4},{1,7},{3,1},{5,3},{7,5},{8,14},{10,8},{12,... | collective-permute-start | bytes 540680 | tf_op jit(solution)/shard_map/gather/ppermute | solution.py:253
  230.9 4.9 %collective-permute-done.18 = bf16[64,1280]{1,0:T(8,128)(2,1)S(1)} collective-permute-done((bf16[64,1280]{1,0:T(8,128)(2,1)S(1)}, bf16[64,1280]{1,0:T(8,128)(2,1)S(1)}, u32[]{:S(2)}, u32[]{:S(2)}) %collective-permute-start.18) | collective-permute-done | bytes 163872 | tf_op jit(solution)/shard_map/gather/ppermute | solution.py:253
  235.8 0.8 maximum_dynamic-update-slice_fusion
  (43 shorter events, 8.7 us)
Async XLA Ops:
  0.0 96.6 %copy-start = (f32[512]{0:T(512)S(1)}, f32[512]{0:T(512)}, u32[]{:S(2)}) copy-start(f32[512]{0:T(512)} %param.12) | copy-start | bytes 6148
  77.6 55.7 %collective-permute-start = (bf16[256,4096]{1,0:T(8,128)(2,1)}, bf16[256,4096]{1,0:T(8,128)(2,1)S(1)}, u32[]{:S(2)}, u32[]{:S(2)}) collective-permute-start(bf16[256,4096]{1,0:T(8,128)(2,1)} %get-tuple-element.23), channel_id=1, source_target_pairs={{0,2},{2,4},{4,6},{6,0},{1,3},{3,5},{5,7},{7,1},{8,10},{10,12},{12... | collective-permute-start | bytes 6291464 | tf_op jit(solution)/shard_map/weights/ppermute | solution.py:253
  79.3 54.1 %collective-permute-start.1 = (bf16[256,4096]{1,0:T(8,128)(2,1)}, bf16[256,4096]{1,0:T(8,128)(2,1)}, u32[]{:S(2)}, u32[]{:S(2)}) collective-permute-start(bf16[256,4096]{1,0:T(8,128)(2,1)} %get-tuple-element.23), channel_id=1, source_target_pairs={{0,6},{2,0},{4,2},{6,4},{1,7},{3,1},{5,3},{7,5},{8,14},{10,8},{12,... | collective-permute-start | bytes 6291464 | tf_op jit(solution)/shard_map/weights/ppermute | solution.py:253
  80.9 39.3 %all-to-all-start = ((bf16[32,32,512]{2,1,0:T(8,128)(2,1)}), bf16[32,32,512]{2,1,0:T(8,128)(2,1)S(1)}, u32[]{:S(2)}, u32[]{:S(2)}) async-start(bf16[32,32,512]{2,1,0:T(8,128)(2,1)} %get-tuple-element.22), calls=%async_computation | async-start | bytes 2097152 | tf_op jit(solution)/shard_map/all_to_all | solution.py:302
  92.5 37.1 %collective-permute-start.2 = (bf16[128,512]{1,0:T(8,128)(2,1)}, bf16[128,512]{1,0:T(8,128)(2,1)S(1)}, u32[]{:S(2)}, u32[]{:S(2)}) collective-permute-start(bf16[128,512]{1,0:T(8,128)(2,1)} %get-tuple-element.24), channel_id=1, source_target_pairs={{0,2},{2,4},{4,6},{6,0},{1,3},{3,5},{5,7},{7,1},{8,10},{10,12},{12... | collective-permute-start | bytes 393224 | tf_op jit(solution)/shard_map/weights/ppermute | solution.py:253
  93.0 38.7 %collective-permute-start.3 = (bf16[128,512]{1,0:T(8,128)(2,1)}, bf16[128,512]{1,0:T(8,128)(2,1)S(1)}, u32[]{:S(2)}, u32[]{:S(2)}) collective-permute-start(bf16[128,512]{1,0:T(8,128)(2,1)} %get-tuple-element.25), channel_id=1, source_target_pairs={{0,6},{2,0},{4,2},{6,4},{1,7},{3,1},{5,3},{7,5},{8,14},{10,8},{12,... | collective-permute-start | bytes 393224 | tf_op jit(solution)/shard_map/weights/ppermute | solution.py:253
  95.9 37.5 %collective-permute-start.4 = (bf16[128,512]{1,0:T(8,128)(2,1)}, bf16[128,512]{1,0:T(8,128)(2,1)S(1)}, u32[]{:S(2)}, u32[]{:S(2)}) collective-permute-start(bf16[128,512]{1,0:T(8,128)(2,1)} %get-tuple-element.26), channel_id=1, source_target_pairs={{0,4},{2,6},{4,0},{6,2},{1,5},{3,7},{5,1},{7,3},{8,12},{10,14},{12... | collective-permute-start | bytes 393224 | tf_op jit(solution)/shard_map/weights/ppermute | solution.py:253
  120.2 1.2 copy-start.3
  121.4 1.2 copy-start.4
  122.7 53.1 %copy-start.1 = (bf16[512,4096]{1,0:T(8,128)(2,1)S(1)}, bf16[512,4096]{1,0:T(8,128)(2,1)}, u32[]{:S(2)}) copy-start(bf16[512,4096]{1,0:T(8,128)(2,1)} %refs_5_.1) | copy-start | bytes 12582916
  122.7 53.1 %copy-start.2 = (bf16[512,512]{1,0:T(8,128)(2,1)S(1)}, bf16[512,512]{1,0:T(8,128)(2,1)}, u32[]{:S(2)}) copy-start(bf16[512,512]{1,0:T(8,128)(2,1)} %refs_1_.1) | copy-start | bytes 1572868
  133.4 38.2 %collective-permute-start.5 = (bf16[128,4096]{1,0:T(8,128)(2,1)S(1)}, bf16[128,4096]{1,0:T(8,128)(2,1)S(1)}, u32[]{:S(2)}, u32[]{:S(2)}) collective-permute-start(bf16[128,4096]{1,0:T(8,128)(2,1)S(1)} %slice.39), channel_id=1, source_target_pairs={{0,2},{2,4},{4,6},{6,0},{1,3},{3,5},{5,7},{7,1},{8,10},{10,12},{12... | collective-permute-start | bytes 3145736 | tf_op jit(solution)/shard_map/weights/ppermute | solution.py:253
  136.0 35.7 %collective-permute-start.6 = (bf16[128,4096]{1,0:T(8,128)(2,1)S(1)}, bf16[128,4096]{1,0:T(8,128)(2,1)S(1)}, u32[]{:S(2)}, u32[]{:S(2)}) collective-permute-start(bf16[128,4096]{1,0:T(8,128)(2,1)S(1)} %slice.40), channel_id=1, source_target_pairs={{0,6},{2,0},{4,2},{6,4},{1,7},{3,1},{5,3},{7,5},{8,14},{10,8},{12,... | collective-permute-start | bytes 3145736 | tf_op jit(solution)/shard_map/weights/ppermute | solution.py:253
  138.1 37.7 %collective-permute-start.7 = (bf16[256,4096]{1,0:T(8,128)(2,1)S(1)}, bf16[256,4096]{1,0:T(8,128)(2,1)S(1)}, u32[]{:S(2)}, u32[]{:S(2)}) collective-permute-start(bf16[256,4096]{1,0:T(8,128)(2,1)S(1)} %collective-permute-done.refs_6_), channel_id=1, source_target_pairs={{0,8},{8,0},{1,9},{9,1},{2,10},{10,2},{3,11},{11,3},{4,12},{12,4},... | collective-permute-start | bytes 6291464 | tf_op jit(solution)/shard_map/weights/ppermute | solution.py:245
  138.1 37.7 %collective-permute-start.8 = (bf16[256,4096]{1,0:T(8,128)(2,1)}, bf16[256,4096]{1,0:T(8,128)(2,1)S(1)}, u32[]{:S(2)}, u32[]{:S(2)}) collective-permute-start(bf16[256,4096]{1,0:T(8,128)(2,1)} %collective-permute-done.1.refs_8_), channel_id=1, source_target_pairs={{0,8},{8,0},{1,9},{9,1},{2,10},{10,2},{3,11},{11,3},{4,12},{12,4},... | collective-permute-start | bytes 6291464 | tf_op jit(solution)/shard_map/weights/ppermute | solution.py:245
  171.6 2.7 %collective-permute-start.10 = (bf16[128,4096]{1,0:T(8,128)(2,1)S(1)}, bf16[128,4096]{1,0:T(8,128)(2,1)S(1)}, u32[]{:S(2)}, u32[]{:S(2)}) collective-permute-start(bf16[128,4096]{1,0:T(8,128)(2,1)S(1)} %collective-permute-done.6.refs_11_), channel_id=1, source_target_pairs={{0,8},{8,0},{1,9},{9,1},{2,10},{10,2},{3,11},{11,3},{4,12},{12,4},... | collective-permute-start | bytes 3145736 | tf_op jit(solution)/shard_map/weights/ppermute | solution.py:245
  171.6 4.2 %collective-permute-start.9 = (bf16[128,4096]{1,0:T(8,128)(2,1)S(1)}, bf16[128,4096]{1,0:T(8,128)(2,1)S(1)}, u32[]{:S(2)}, u32[]{:S(2)}) collective-permute-start(bf16[128,4096]{1,0:T(8,128)(2,1)S(1)} %collective-permute-done.5.refs_10_), channel_id=1, source_target_pairs={{0,8},{8,0},{1,9},{9,1},{2,10},{10,2},{3,11},{11,3},{4,12},{12,4},... | collective-permute-start | bytes 3145736 | tf_op jit(solution)/shard_map/weights/ppermute | solution.py:245
  182.3 14.0 %collective-permute-start.11 = (bf16[64,4096]{1,0:T(8,128)(2,1)S(1)}, bf16[64,4096]{1,0:T(8,128)(2,1)S(1)}, u32[]{:S(2)}, u32[]{:S(2)}) collective-permute-start(bf16[64,4096]{1,0:T(8,128)(2,1)S(1)} %get-tuple-element.38), channel_id=1, source_target_pairs={{0,1},{1,0},{2,3},{3,2},{4,5},{5,4},{6,7},{7,6},{8,9},{9,8},{10,11... | collective-permute-start | bytes 1572872 | tf_op jit(solution)/shard_map/reduce/ppermute | solution.py:245
  197.3 13.1 %collective-permute-start.13 = (bf16[64,4096]{1,0:T(8,128)(2,1)S(1)}, bf16[64,4096]{1,0:T(8,128)(2,1)S(1)}, u32[]{:S(2)}, u32[]{:S(2)}) collective-permute-start(bf16[64,4096]{1,0:T(8,128)(2,1)S(1)} %get-tuple-element.40), channel_id=1, source_target_pairs={{0,6},{2,0},{4,2},{6,4},{1,7},{3,1},{5,3},{7,5},{8,14},{10,8},{12,... | collective-permute-start | bytes 1572872 | tf_op jit(solution)/shard_map/gather/ppermute | solution.py:253
  198.5 15.5 %collective-permute-start.12 = (bf16[64,4096]{1,0:T(8,128)(2,1)S(1)}, bf16[64,4096]{1,0:T(8,128)(2,1)S(1)}, u32[]{:S(2)}, u32[]{:S(2)}) collective-permute-start(bf16[64,4096]{1,0:T(8,128)(2,1)S(1)} %get-tuple-element.40), channel_id=1, source_target_pairs={{0,1},{1,0},{2,3},{3,2},{4,5},{5,4},{6,7},{7,6},{8,9},{9,8},{10,11... | collective-permute-start | bytes 1572872 | tf_op jit(solution)/shard_map/gather/ppermute | solution.py:245
  203.8 32.8 %collective-permute-start.20 = (bf16[64,4096]{1,0:T(8,128)(2,1)S(1)}, bf16[64,4096]{1,0:T(8,128)(2,1)S(1)}, u32[]{:S(2)}, u32[]{:S(2)}) collective-permute-start(bf16[64,4096]{1,0:T(8,128)(2,1)S(1)} %get-tuple-element.40), channel_id=1, source_target_pairs={{0,2},{2,4},{4,6},{6,0},{1,3},{3,5},{5,7},{7,1},{8,10},{10,12},{12... | collective-permute-start | bytes 1572872 | tf_op jit(solution)/shard_map/gather/ppermute | solution.py:253
  210.4 14.5 %collective-permute-start.14 = (bf16[64,4096]{1,0:T(8,128)(2,1)S(1)}, bf16[64,4096]{1,0:T(8,128)(2,1)S(1)}, u32[]{:S(2)}, u32[]{:S(2)}) collective-permute-start(bf16[64,4096]{1,0:T(8,128)(2,1)S(1)} %collective-permute-done.13), channel_id=1, source_target_pairs={{0,1},{1,0},{2,3},{3,2},{4,5},{5,4},{6,7},{7,6},{8,9},{9,8},{10,11... | collective-permute-start | bytes 1572872 | tf_op jit(solution)/shard_map/gather/ppermute | solution.py:245
  211.5 12.2 %collective-permute-start.15 = (bf16[64,4096]{1,0:T(8,128)(2,1)S(1)}, bf16[64,4096]{1,0:T(8,128)(2,1)S(1)}, u32[]{:S(2)}, u32[]{:S(2)}) collective-permute-start(bf16[64,4096]{1,0:T(8,128)(2,1)S(1)} %collective-permute-done.13), channel_id=1, source_target_pairs={{0,6},{2,0},{4,2},{6,4},{1,7},{3,1},{5,3},{7,5},{8,14},{10,8},{12,... | collective-permute-start | bytes 1572872 | tf_op jit(solution)/shard_map/gather/ppermute | solution.py:253
  213.9 15.2 %collective-permute-start.17 = (bf16[64,4096]{1,0:T(8,128)(2,1)S(1)}, bf16[64,4096]{1,0:T(8,128)(2,1)S(1)}, u32[]{:S(2)}, u32[]{:S(2)}) collective-permute-start(bf16[64,4096]{1,0:T(8,128)(2,1)S(1)} %collective-permute-done.12), channel_id=1, source_target_pairs={{0,2},{2,4},{4,6},{6,0},{1,3},{3,5},{5,7},{7,1},{8,10},{10,12},{12... | collective-permute-start | bytes 1572872 | tf_op jit(solution)/shard_map/gather/ppermute | solution.py:253
  223.7 12.1 %collective-permute-start.16 = (bf16[64,1408]{1,0:T(8,128)(2,1)S(1)}, bf16[64,1408]{1,0:T(8,128)(2,1)S(1)}, u32[]{:S(2)}, u32[]{:S(2)}) collective-permute-start(bf16[64,1408]{1,0:T(8,128)(2,1)S(1)} %slice.52), channel_id=1, source_target_pairs={{0,1},{1,0},{2,3},{3,2},{4,5},{5,4},{6,7},{7,6},{8,9},{9,8},{10,11... | collective-permute-start | bytes 540680 | tf_op jit(solution)/shard_map/gather/ppermute | solution.py:245
  225.0 10.8 %collective-permute-start.19 = (bf16[64,1408]{1,0:T(8,128)(2,1)S(1)}, bf16[64,1408]{1,0:T(8,128)(2,1)S(1)}, u32[]{:S(2)}, u32[]{:S(2)}) collective-permute-start(bf16[64,1408]{1,0:T(8,128)(2,1)S(1)} %slice.54), channel_id=1, source_target_pairs={{0,6},{2,0},{4,2},{6,4},{1,7},{3,1},{5,3},{7,5},{8,14},{10,8},{12,... | collective-permute-start | bytes 540680 | tf_op jit(solution)/shard_map/gather/ppermute | solution.py:253
  229.2 6.6 %collective-permute-start.18 = (bf16[64,1280]{1,0:T(8,128)(2,1)S(1)}, bf16[64,1280]{1,0:T(8,128)(2,1)S(1)}, u32[]{:S(2)}, u32[]{:S(2)}) collective-permute-start(bf16[64,1280]{1,0:T(8,128)(2,1)S(1)} %slice.53), channel_id=1, source_target_pairs={{0,2},{2,4},{4,6},{6,0},{1,3},{3,5},{5,7},{7,1},{8,10},{10,12},{12... | collective-permute-start | bytes 491528 | tf_op jit(solution)/shard_map/gather/ppermute | solution.py:253

commit v4 on v3

v4 whole, which is shorter than its diff:
```python
import functools
import math

import jax
import jax.numpy as jnp
import ml_dtypes
import numpy as np
from jax import lax
from jax.experimental import pallas as pl
from jax.experimental.pallas import tpu as pltpu
from jax.sharding import Mesh, PartitionSpec as P

MIB = 1024 * 1024
GROUP = 4
STEPS = (0, 1, -1, 2)
STREAMS = 2
WIDTH = 512


def transform_tables(rows):
    j = np.arange(rows, dtype=np.int64)[:, None]
    f = np.arange(rows, dtype=np.int64)[None, :]
    angle = (j * (2 * f + 1) % (4 * rows)) * (2.0 * math.pi / (4 * rows))
    cos, sin = np.cos(angle), np.sin(angle)
    forward = np.concatenate([cos, -sin], 1)
    inverse = np.concatenate([cos.T, -sin.T], 0) / rows
    return forward.astype(ml_dtypes.bfloat16), inverse.astype(ml_dtypes.bfloat16)


def pack_kernel(
    key_hbm, value_hbm, filter_hbm, query_hbm, weight_hbm,
    out_ref, half_ref, up_ref, down_ref, far_ref, key_ref, value_ref, filter_ref, sems,
):
    parts, both, rows = out_ref.shape
    share = both // 2
    half, quarter = half_ref.shape[0], up_ref.shape[0]

    core, y = lax.axis_index("core"), lax.axis_index("y")

    def rows_of(ref, index, count):
        return ref.at[pl.ds(pl.multiple_of(index * count, count), count)]

    copies = [
        pltpu.make_async_copy(source, target, sems.at[i])
        for i, (source, target) in enumerate(
            (
                (key_hbm, key_ref),
                (value_hbm, value_ref),
                (filter_hbm, filter_ref),
                (rows_of(weight_hbm, core, half), half_ref),
                (rows_of(query_hbm, (y + 1) % 4, quarter), up_ref),
                (rows_of(query_hbm, (y + 3) % 4, quarter), down_ref),
                (rows_of(query_hbm, (y + 2) % 4, quarter), far_ref),
            )
        )
    ]
    for copy in copies:
        copy.start()
    copies[0].wait()
    copies[1].wait()
    mixer = key_ref[...].astype(jnp.float32) * value_ref[...].astype(jnp.float32)
    out_ref[:, :share, :] = mixer.astype(jnp.bfloat16).T.reshape(parts, share, rows)
    copies[2].wait()
    out_ref[:, share:, :] = filter_ref[...].T.reshape(parts, share, rows)
    for copy in copies[3:]:
        copy.wait()


def conv_kernel(
    signal_ref, gain_ref, forward_hbm, inverse_hbm, out_ref, mixer_spec, filter_spec, product,
    sum_ref, forward_ref, inverse_ref, sems,
):
    blocks, both, rows = signal_ref.shape
    share = both // 2
    copies = []
    for source, target in ((forward_hbm, forward_ref), (inverse_hbm, inverse_ref)):
        count = source.shape[0] // 4
        for part in range(4):
            here = pl.ds(part * count, count)
            copies.append(
                pltpu.make_async_copy(source.at[here], target.at[here], sems.at[len(copies)])
            )
    for copy in copies:
        copy.start()
    for copy in copies[:4]:
        copy.wait()
    forward = forward_ref[...]

    def spectrum(signal):
        flat = signal.reshape(blocks * share, rows)
        value = jnp.dot(flat, forward, preferred_element_type=jnp.float32)
        return value.reshape(blocks, share, 2 * rows)

    mixer_spec[...] = spectrum(signal_ref[:, :share, :])
    filter_spec[...] = spectrum(signal_ref[:, share:, :])

    lane = lax.broadcasted_iota(jnp.int32, (8, 128), 1)
    sign = jnp.where(lane % 2 == 0, 1.0, -1.0).astype(jnp.float32)
    lane_tiles = rows // 128

    def tile(step, carry):
        row = pl.multiple_of((step // lane_tiles) * 8, 8)
        real = pl.multiple_of((step % lane_tiles) * 128, 128)
        imag = pl.multiple_of(rows + (step % lane_tiles) * 128, 128)

        def load(ref, block):
            return (
                ref[block, pl.ds(row, 8), pl.ds(real, 128)],
                ref[block, pl.ds(row, 8), pl.ds(imag, 128)],
            )

        def window(block):
            now_real, now_imag = load(mixer_spec, block)
            if block > 0:
                last_real, last_imag = load(mixer_spec, block - 1)
                now_real, now_imag = now_real - sign * last_imag, now_imag + sign * last_real
            return now_real, now_imag

        for block in reversed(range(blocks)):
            now_real, now_imag = window(block)
            mixer_spec[block, pl.ds(row, 8), pl.ds(real, 128)] = now_real
            mixer_spec[block, pl.ds(row, 8), pl.ds(imag, 128)] = now_imag

        for first in range(0, blocks, GROUP):
            sums = [[None] * 3 for _ in range(GROUP)]
            held = {}
            for lag in range(first + GROUP):
                filter_real, filter_imag = load(filter_spec, lag)
                filter_both = filter_real + filter_imag
                for i in range(GROUP):
                    block = first + i - lag
                    if block < 0:
                        continue
                    if block not in held:
                        real_part, imag_part = load(mixer_spec, block)
                        held[block] = (real_part, imag_part, real_part + imag_part)
                    terms = (
                        filter_real * held[block][0],
                        filter_imag * held[block][1],
                        filter_both * held[block][2],
                    )
                    for s in range(3):
                        sums[i][s] = terms[s] if sums[i][s] is None else sums[i][s] + terms[s]
                held.pop(first + GROUP - 1 - lag, None)
            for i in range(GROUP):
                one, two, three = sums[i]
                product[first + i, pl.ds(row, 8), pl.ds(real, 128)] = one - two
                product[first + i, pl.ds(row, 8), pl.ds(imag, 128)] = three - one - two
        return carry

    lax.fori_loop(0, (share // 8) * lane_tiles, tile, 0)
    flat = product[...].astype(jnp.bfloat16).reshape(blocks * share, 2 * rows)
    for copy in copies[4:]:
        copy.wait()
    conv = jnp.dot(flat, inverse_ref[...], preferred_element_type=jnp.float32)
    mixer = signal_ref[:, :share, :].astype(jnp.float32)
    total = conv.reshape(blocks, share, rows) + gain_ref[...] * mixer
    sum_ref[...] = total.astype(jnp.bfloat16)
    quarters, width = out_ref.shape[1], out_ref.shape[3]
    for slot in range(quarters):
        start = (lax.axis_index("y") + STEPS[slot]) % quarters * width
        out_ref[:, slot] = sum_ref[:, :, pl.ds(pl.multiple_of(start, width), width)]


def gate(total, query, sides, out_ref, gated_ref):
    blocks, share, rows = total.shape
    half = blocks * share // 2
    for part, side in enumerate(sides):
        value = total[pl.ds(side * (blocks // 2), blocks // 2)].reshape(half, rows)
        channels = side * half if isinstance(side, int) else pl.multiple_of(side * half, half)
        value = query[:, pl.ds(channels, half)].astype(jnp.float32) * value.T.astype(jnp.float32)
        gated_ref[:, part * half : (part + 1) * half] = value.astype(jnp.bfloat16)
    piece = rows // 2
    keep = lax.axis_index("z")
    out_ref[:piece] = gated_ref[pl.ds(pl.multiple_of((1 - keep) * piece, piece), piece), :]
    out_ref[piece:] = gated_ref[pl.ds(pl.multiple_of(keep * piece, piece), piece), :]


def own_kernel(total_ref, query_ref, weight_ref, out_ref, blank_ref, gated_ref, rows_ref):
    del blank_ref
    rows = total_ref.shape[2]
    start = pl.multiple_of(lax.axis_index("y") * rows, rows)
    gate(total_ref, query_ref.at[pl.ds(start, rows)], (0, 1), rows_ref, gated_ref)
    for start in range(0, out_ref.shape[1], WIDTH):
        columns = slice(start, start + WIDTH)
        out_ref[:, columns] = jnp.dot(
            rows_ref[...], weight_ref[:, columns], preferred_element_type=jnp.float32
        )


def gate_kernel(*refs):
    totals, queries, out_ref, gated_ref = refs[:3], refs[3:6], refs[6], refs[7]
    core = lax.axis_index("core")
    depth = gated_ref.shape[1]
    for group in range(3):
        out = out_ref.at[:, pl.ds(group * depth, depth)]
        gate(totals[group], queries[group], (core, 1 - core), out, gated_ref)


def rest_kernel(first, gated_ref, partial_ref, *refs):
    weights, (other_ref, own_ref) = refs[:-2], refs[-2:]
    piece, columns = other_ref.shape
    for column in range(0, columns, WIDTH):
        here = slice(first + column, first + column + WIDTH)
        value, start = partial_ref[:, here], 0
        for weight in weights:
            depth = weight.shape[0]
            value = value + jnp.dot(
                gated_ref[:, start : start + depth],
                weight[:, here],
                preferred_element_type=jnp.float32,
            )
            start += depth
        value = value.astype(jnp.bfloat16)
        other_ref[:, column : column + WIDTH] = value[:piece]
        own_ref[:, column : column + WIDTH] = value[piece:]


VMEM = pl.BlockSpec(memory_space=pltpu.VMEM)
HBM = pl.BlockSpec(memory_space=pltpu.HBM)


def whole(kernel, shapes, in_specs, out_specs, scratch=(), limit=16, dtype=jnp.bfloat16, cost=0):
    return pl.pallas_call(
        kernel,
        out_shape=[
            jax.ShapeDtypeStruct(shape, dtype if i == 0 else jnp.bfloat16)
            for i, shape in enumerate(shapes)
        ],
        in_specs=in_specs,
        out_specs=out_specs,
        scratch_shapes=list(scratch),
        compiler_params=pltpu.CompilerParams(vmem_limit_bytes=limit * MIB),
        cost_estimate=pl.CostEstimate(flops=2 * cost, bytes_accessed=8 * MIB, transcendentals=0),
    )


def swap(axis):
    return lambda value: lax.ppermute(value, axis, [(0, 1), (1, 0)])


along_z, along_core = swap("z"), swap("core")


def along_y(value, steps):
    count = lax.axis_size("y")
    return lax.ppermute(value, "y", [(i, (i + steps) % count) for i in range(count)])


def add(*terms):
    return sum(term.astype(jnp.float32) for term in terms).astype(jnp.bfloat16)


def reduce_and_gather(halves):
    found, first, last = [], [], []
    arrived = [along_z(other) for other, _ in halves]
    for (_, own), from_z in zip(halves, arrived):
        own = add(own, from_z)
        first.append((own, along_z(own), along_y(own, 1), along_y(own, -1)))
    for stream, (own, own_z, down, up) in enumerate(first):
        own_z, down, up = lax.optimization_barrier((own_z, down, up))
        found += [(stream, 0, 0, own), (stream, 1, 0, own_z), (stream, 6, 0, down)]
        found.append((stream, 2, 0, up))
        last.append((along_z(up), along_y(up, -1), along_y(own_z, 1)))
    for stream, (up_z, far, down_z) in enumerate(last):
        up_z, far, down_z = lax.optimization_barrier((up_z, far, down_z))
        found += [(stream, 3, 0, up_z), (stream, 4, 0, far), (stream, 7, 0, down_z)]
        middle = up_z.shape[1] // 2
        found.append((stream, 5, 0, along_y(down_z[:, :middle], 1)))
        found.append((stream, 5, 1, along_y(up_z[:, middle:], -1)))
    return found


def body(query_branch, key_branch, value_branch, filters, skip_gain, out_weight):
    core, y, z = (lax.axis_index(name) for name in ("core", "y", "z"))
    ctx = lax.axis_index("block") * 2 + core
    ctx_count = lax.axis_size("block") * 2
    y_count = lax.axis_size("y")
    rows, channels = query_branch.shape
    share = channels // ctx_count
    features = out_weight.shape[1]
    quarter = rows // y_count
    forward, inverse = (jnp.asarray(table) for table in transform_tables(rows))
    gain = lax.dynamic_slice(skip_gain, (ctx * share,), (share,))[:, None]

    with jax.named_scope("pack"):
        square = pltpu.VMEM((rows, channels), jnp.bfloat16)
        outgoing, weight_half, to_up, to_down, to_far = whole(
            pack_kernel,
            [(ctx_count, 2 * share, rows), (channels // 2, features)] + [(quarter, channels)] * 3,
            [HBM] * 5,
            [VMEM] * 5,
            [square, square, square, pltpu.SemaphoreType.DMA((7,))],
            limit=60,
        )(key_branch, value_branch, filters, query_branch, out_weight)
    with jax.named_scope("weights"):
        weight_up, weight_down = along_y(weight_half, 1), along_y(weight_half, -1)
        query_up, query_down = along_y(to_up, 1), along_y(to_down, -1)
        query_far = along_y(to_far, 2)
    arrived = lax.all_to_all(outgoing, ("block", "core"), split_axis=0, concat_axis=0, tiled=True)
    spec = pltpu.VMEM((ctx_count, share, 2 * rows), jnp.float32)
    with jax.named_scope("conv"):
        (total,) = whole(
            conv_kernel,
            [(ctx_count, y_count, share, quarter)],
            [VMEM] * 2 + [HBM] * 2,
            [VMEM],
            [spec] * 3
            + [
                pltpu.VMEM(shape, jnp.bfloat16)
                for shape in ((ctx_count, share, rows), forward.shape, inverse.shape)
            ]
            + [pltpu.SemaphoreType.DMA((8,))],
            limit=24,
        )(arrived, gain, forward, inverse)
    with jax.named_scope("weights"):
        total, weight_up, weight_down, query_up, query_down, query_far = lax.optimization_barrier(
            (total, weight_up, weight_down, query_up, query_down, query_far)
        )
        cut = channels // 4
        far_first, far_last = along_y(weight_up[:cut], 1), along_y(weight_down[cut:], -1)
        swapped_up, swapped_down = along_core(weight_up), along_core(weight_down)
    total = lax.all_to_all(total, ("block", "core"), split_axis=0, concat_axis=0, tiled=True)
    with jax.named_scope("weights"):
        total, far_first, far_last, swapped_up, swapped_down = lax.optimization_barrier(
            (total, far_first, far_last, swapped_up, swapped_down)
        )
        swapped_first, swapped_last = along_core(far_first), along_core(far_last)
    with jax.named_scope("quarters"):
        total_up, total_down = along_y(total[:, 1], 1), along_y(total[:, 2], -1)
        total_far = along_y(total[:, 3], 2)
    with jax.named_scope("own"):
        gated = pltpu.VMEM((quarter, channels), jnp.bfloat16)
        partial_value, out = whole(
            own_kernel, [(quarter, features), (rows, features)], [VMEM] * 3, [VMEM, HBM],
            [gated, gated], limit=12, dtype=jnp.float32, cost=rows * channels * features,
        )(total[:, 0], query_branch, out_weight)
    with jax.named_scope("rest"):
        (rest,) = whole(gate_kernel, [(quarter, 3 * channels)], [VMEM] * 6, [VMEM], [gated])(
            total_up, total_down, total_far, query_up, query_down, query_far
        )
        weights = (
            weight_up, swapped_up, weight_down, swapped_down,
            far_first, far_last, swapped_first, swapped_last,
        )
        width = features // STREAMS
        halves = [
            whole(
                functools.partial(rest_kernel, stream * width),
                [(quarter // 2, width)] * 2,
                [VMEM] * (2 + len(weights)),
                [VMEM] * 2,
                limit=20,
                cost=rows * channels * features,
            )(rest, partial_value, *weights)
            for stream in range(STREAMS)
        ]
    slots = jnp.arange(2 * y_count, dtype=jnp.int32)
    order = ((y + slots // 2) % y_count * 2 + (z + slots) % 2) * (quarter // 2)
    with jax.named_scope("gather"):
        for stream, slot, part, value in reduce_and_gather(halves):
            column = stream * width + part * value.shape[1]
            out = lax.dynamic_update_slice(out, value, (order[slot], column))
    return out


def solution(mesh):
    fine = Mesh(mesh.devices.reshape(-1, 2, 4, 2), ("block", "core", "y", "z"))
    ctx, tp = ("block", "core"), ("y", "z")
    placed = (P(ctx, tp), P(ctx, tp), P(ctx, tp), P(ctx, tp), P(tp), P(tp, None))
    return jax.shard_map(
        body, mesh=fine, in_specs=placed, out_specs=P(ctx, None), check_vma=False
    )
```

time: 239 us -> 238 us (level)
  Pallas kernels: 91 us -> 18 us
  local copies, waits for them, and re-layouts: 9.7 us -> 76.1 us
  starting transfers between devices: 36.4 us -> 51.8 us
  waiting for transfers between devices: 61.3 us -> 46.8 us
  between operations: 5.15 us -> 15.1 us
  blocking collectives: 33 us -> 27.9 us
    pallas_call x1, Pallas kernels: 77.6 us -> 3.93 us  [body(): whole(pack_kernel, [(ctx_count, 2 * share, rows), (channels // 2, feature...]
    dynamic_update_slice x6 -> x18, local copies, waits for them, and re-layouts: 4.97 us -> 69.4 us  [body(): out = lax.dynamic_update_slice(out, value, (order[slot], column))]
    ppermute x13 -> x22, starting transfers between devices: 19.4 us -> 29.9 us  [along_y(): lax.ppermute(value, 'y', [(i, (i + steps) % count) for i in range(count)])]
    ppermute x13 -> x22, waiting for transfers between devices: 22.6 us -> 14.8 us  [along_y(): lax.ppermute(value, 'y', [(i, (i + steps) % count) for i in range(count)])]
    ppermute x8 -> x10, waiting for transfers between devices: 15.3 us -> 9.18 us  [swap(): return lambda value: lax.ppermute(value, axis, [(0, 1), (1, 0)])]
    all_to_all x1, blocking collectives: 33 us -> 27.9 us  [body(): lax.all_to_all(total, ('block', 'core'), split_axis=0, concat_axis=0, til...]
    ppermute x8 -> x10, starting transfers between devices: 5.35 us -> 10.2 us  [swap(): return lambda value: lax.ppermute(value, axis, [(0, 1), (1, 0)])]
    pallas_call x2 -> x5, Pallas kernels: 13.4 us -> 14 us  [the longest x1 7.32 us: body(): whole(conv_kernel, [(ctx_count, y_count, share, quarter)], [VMEM] * 2 + [...]
  transfers between devices with their start and end apart: 22 -> 33, of which waited for: 10 -> 11; matrix products, arithmetic and copies ran while one was open for 3% -> 30% of each run, Pallas kernels for 3% -> 5%
where the time goes in v4:
time: 238 us; the launch traced here: 236 us
  local copies, waits for them, and re-layouts  76.1 us (32%)
  starting transfers between devices  51.8 us (22%)
  waiting for transfers between devices  46.8 us (20%)
  blocking collectives  27.9 us (12%)
  Pallas kernels  18 us (8%)
  between operations  15.1 us (6%)
    dynamic_update_slice x18, local copies, waits for them, and re-layouts, body(): out = lax.dynamic_update_slice(out, value, (order[slot], column))  69.4 us
    ppermute x22, starting transfers between devices, along_y(): lax.ppermute(value, 'y', [(i, (i + steps) % count) for i in range(count)])  29.9 us
    all_to_all x1, blocking collectives, body(): lax.all_to_all(total, ('block', 'core'), split_axis=0, concat_axis=0, til...  27.9 us
    all_to_all x1, waiting for transfers between devices, body(): lax.all_to_all(outgoing, ('block', 'core'), split_axis=0, concat_axis=0,...  22.7 us
    ppermute x22, waiting for transfers between devices, along_y(): lax.ppermute(value, 'y', [(i, (i + steps) % count) for i in range(count)])  14.8 us
    all_to_all x1, starting transfers between devices, body(): lax.all_to_all(outgoing, ('block', 'core'), split_axis=0, concat_axis=0,...  11.6 us
    ppermute x10, starting transfers between devices, swap(): return lambda value: lax.ppermute(value, axis, [(0, 1), (1, 0)])  10.2 us
    ppermute x10, waiting for transfers between devices, swap(): return lambda value: lax.ppermute(value, axis, [(0, 1), (1, 0)])  9.18 us
  transfers between devices with their start and end apart: 33, of which 11 were waited for; matrix products, arithmetic and copies ran while one was open for 30% of the time, Pallas kernels for 5%

profile of v4, /device:TPU:2, one launch (start us, length us, event | category | flops | bytes accessed | tf_op | source)
XLA Modules:
  0.0 235.7 jit_solution(17611237150413848309)
XLA Ops:
  0.0 3.9 %pack.1 = (bf16[32,32,512]{2,1,0:T(8,128)(2,1)}, bf16[256,4096]{1,0:T(8,128)(2,1)}, bf16[128,512]{1,0:T(8,128)(2,1)}, bf16[128,512]{1,0:T(8,128)(2,1)}, bf16[128,512]{1,0:T(8,128)(2,1)}) custom-call(bf16[512,512]{1,0:T(8,128)(2,1)} %key_hbm.1, bf16[512,512]{1,0:T(8,128)(2,1)} %value_hbm.1, bf16[512,512]{1,0:T(8,128)(2,1)} %filter_hbm.1, ...), custom_call_target="tpu_custom_call" | custom-call | bytes 8388608 | tf_op jit(solution)/shard_map/pack/pallas_call | solution.py:288
  3.9 3.1 %collective-permute-start.1 = (bf16[256,4096]{1,0:T(8,128)(2,1)}, bf16[256,4096]{1,0:T(8,128)(2,1)S(1)}, u32[]{:S(2)}, u32[]{:S(2)}) collective-permute-start(bf16[256,4096]{1,0:T(8,128)(2,1)} %get-tuple-element.40), channel_id=1, source_target_pairs={{0,6},{2,0},{4,2},{6,4},{1,7},{3,1},{5,3},{7,5},{8,14},{10,8},{12,... | collective-permute-start | bytes 6291464 | tf_op jit(solution)/shard_map/weights/ppermute | solution.py:247
  7.0 11.6 %all-to-all-start = ((bf16[32,32,512]{2,1,0:T(8,128)(2,1)}), bf16[32,32,512]{2,1,0:T(8,128)(2,1)S(1)}, u32[]{:S(2)}, u32[]{:S(2)}) async-start(bf16[32,32,512]{2,1,0:T(8,128)(2,1)} %get-tuple-element.39), calls=%async_computation | async-start | bytes 2097152 | tf_op jit(solution)/shard_map/all_to_all | solution.py:300
  23.6 22.7 %all-to-all-done.signal_ref = bf16[32,32,512]{2,1,0:T(8,128)(2,1)S(1)} async-done(((bf16[32,32,512]{2,1,0:T(8,128)(2,1)}), bf16[32,32,512]{2,1,0:T(8,128)(2,1)S(1)}, u32[]{:S(2)}, u32[]{:S(2)}) %all-to-all-start) | async-done | bytes 1048608 | tf_op jit(solution)/shard_map/all_to_all | solution.py:300
  48.8 7.3 %conv.1 = bf16[32,4,16,128]{3,2,1,0:T(8,128)(2,1)S(1)} custom-call(bf16[32,32,512]{2,1,0:T(8,128)(2,1)S(1)} %all-to-all-done.signal_ref, f32[16,1]{1,0:T(8,128)S(1)} %copy.11.gain_ref, bf16[512,1024]{1,0:T(8,128)(2,1)S(1)} %copy-done.3, bf16[1024,512]{1,0:T(8,128)(2,1)S(1)} %copy-done.2), custom_call_target="tpu_custom_call" | custom-call | bytes 8388608 | tf_op jit(solution)/shard_map/conv/pallas_call | solution.py:303
  56.1 5.0 %collective-permute-done.2.refs_3_ = bf16[128,512]{1,0:T(8,128)(2,1)S(1)} collective-permute-done((bf16[128,512]{1,0:T(8,128)(2,1)}, bf16[128,512]{1,0:T(8,128)(2,1)S(1)}, u32[]{:S(2)}, u32[]{:S(2)}) %collective-permute-start.2) | collective-permute-done | bytes 131104 | tf_op jit(solution)/shard_map/weights/ppermute | solution.py:247
  65.3 27.9 %all_to_all.10 = bf16[32,4,16,128]{3,2,1,0:T(8,128)(2,1)S(1)} all-to-all(bf16[32,4,16,128]{3,2,1,0:T(8,128)(2,1)S(1)} %conv.1), channel_id=1, replica_groups=mesh['block'=16,'core'=2,'y'=4,'z'=2] {'block','core'}, dimensions={0} | all-to-all | bytes 1048576 | tf_op jit(solution)/shard_map/all_to_all | solution.py:323
  98.2 4.4 %collective-permute-done.11.refs_2_ = bf16[32,16,128]{2,1,0:T(8,128)(2,1)S(1)} collective-permute-done((bf16[32,16,128]{2,1,0:T(8,128)(2,1)S(1)}, bf16[32,16,128]{2,1,0:T(8,128)(2,1)S(1)}, u32[]{:S(2)}, u32[]{:S(2)}) %collective-permute-start.11) | collective-permute-done | bytes 131104 | tf_op jit(solution)/shard_map/quarters/ppermute | solution.py:247
  105.1 2.9 %rest.5 = (bf16[64,2048]{1,0:T(8,128)(2,1)S(1)}, bf16[64,2048]{1,0:T(8,128)(2,1)S(1)}) custom-call(bf16[128,1536]{1,0:T(8,128)(2,1)S(1)} %rest.3.gated_ref, f32[128,4096]{1,0:T(8,128)S(1)} %get-tuple-element.52.partial_ref, bf16[256,4096]{1,0:T(8,128)(2,1)} %collective-permute-done.refs_0_, bf16[256,4096]{1,0:T(8,128)(2,1)S(1)} %collective-permute-done.7.refs_1_, ...), custom_call_target="tpu_custom_call" | custom-call | flops 2147483648 | bytes 8388608 | tf_op jit(solution)/shard_map/rest/pallas_call | solution.py:348
  109.6 2.9 %rest.4 = (bf16[64,2048]{1,0:T(8,128)(2,1)S(1)}, bf16[64,2048]{1,0:T(8,128)(2,1)S(1)}) custom-call(bf16[128,1536]{1,0:T(8,128)(2,1)S(1)} %rest.3.gated_ref, f32[128,4096]{1,0:T(8,128)S(1)} %get-tuple-element.52.partial_ref, bf16[256,4096]{1,0:T(8,128)(2,1)} %collective-permute-done.refs_0_, bf16[256,4096]{1,0:T(8,128)(2,1)S(1)} %collective-permute-done.7.refs_1_, ...), custom_call_target="tpu_custom_call" | custom-call | flops 2147483648 | bytes 8388608 | tf_op jit(solution)/shard_map/rest/pallas_call | solution.py:348
  113.1 4.2 %collective-permute-done.18 = bf16[64,2048]{1,0:T(8,128)(2,1)S(1)} collective-permute-done((bf16[64,2048]{1,0:T(8,128)(2,1)S(1)}, bf16[64,2048]{1,0:T(8,128)(2,1)S(1)}, u32[]{:S(2)}, u32[]{:S(2)}) %collective-permute-start.18) | collective-permute-done | bytes 262176 | tf_op jit(solution)/shard_map/gather/ppermute | solution.py:239
  128.7 3.2 %collective-permute-start.28 = (bf16[64,2048]{1,0:T(8,128)(2,1)S(1)}, bf16[64,2048]{1,0:T(8,128)(2,1)S(1)}, u32[]{:S(2)}, u32[]{:S(2)}) collective-permute-start(bf16[64,2048]{1,0:T(8,128)(2,1)S(1)} %collective-permute-done.21), channel_id=1, source_target_pairs={{0,6},{2,0},{4,2},{6,4},{1,7},{3,1},{5,3},{7,5},{8,14},{10,8},{12,... | collective-permute-start | bytes 786440 | tf_op jit(solution)/shard_map/gather/ppermute | solution.py:247
  134.3 3.2 %collective-permute-start.23 = (bf16[64,2048]{1,0:T(8,128)(2,1)S(1)}, bf16[64,2048]{1,0:T(8,128)(2,1)}, u32[]{:S(2)}, u32[]{:S(2)}) collective-permute-start(bf16[64,2048]{1,0:T(8,128)(2,1)S(1)} %collective-permute-done.17), channel_id=1, source_target_pairs={{0,6},{2,0},{4,2},{6,4},{1,7},{3,1},{5,3},{7,5},{8,14},{10,8},{12,... | collective-permute-start | bytes 786440 | tf_op jit(solution)/shard_map/gather/ppermute | solution.py:247
  142.0 3.2 %collective-permute-start.31 = (bf16[64,1024]{1,0:T(8,128)(2,1)S(1)}, bf16[64,1024]{1,0:T(8,128)(2,1)}, u32[]{:S(2)}, u32[]{:S(2)}) collective-permute-start(bf16[64,1024]{1,0:T(8,128)(2,1)S(1)} %slice.81), channel_id=1, source_target_pairs={{0,6},{2,0},{4,2},{6,4},{1,7},{3,1},{5,3},{7,5},{8,14},{10,8},{12,... | collective-permute-start | bytes 393224 | tf_op jit(solution)/shard_map/gather/ppermute | solution.py:247
  147.5 3.2 %collective-permute-start.26 = (bf16[64,1024]{1,0:T(8,128)(2,1)}, bf16[64,1024]{1,0:T(8,128)(2,1)}, u32[]{:S(2)}, u32[]{:S(2)}) collective-permute-start(bf16[64,1024]{1,0:T(8,128)(2,1)} %slice.79), channel_id=1, source_target_pairs={{0,6},{2,0},{4,2},{6,4},{1,7},{3,1},{5,3},{7,5},{8,14},{10,8},{12,... | collective-permute-start | bytes 393224 | tf_op jit(solution)/shard_map/gather/ppermute | solution.py:247
  166.3 4.5 %dynamic_update_slice.54 = bf16[512,4096]{1,0:T(8,128)(2,1)} dynamic-update-slice(bf16[512,4096]{1,0:T(8,128)(2,1)} %get-tuple-element.48, bf16[64,2048]{1,0:T(8,128)(2,1)S(1)} %add_convert_fusion.1, s32[]{:T(128)S(6)} %select_n.57, s32[]{:T(128)} %constant.63.clone.1) | dynamic-update-slice | bytes 524292 | tf_op jit(solution)/shard_map/gather/dynamic_update_slice | solution.py:363
  170.8 4.4 %dynamic_update_slice.55 = bf16[512,4096]{1,0:T(8,128)(2,1)} dynamic-update-slice(bf16[512,4096]{1,0:T(8,128)(2,1)} %dynamic_update_slice.54, bf16[64,2048]{1,0:T(8,128)(2,1)S(1)} %collective-permute-done.15, s32[]{:T(128)S(6)} %select_n.58, s32[]{:T(128)} %constant.63.clone.1) | dynamic-update-slice | bytes 524292 | tf_op jit(solution)/shard_map/gather/dynamic_update_slice | solution.py:363
  175.2 4.4 %dynamic_update_slice.56 = bf16[512,4096]{1,0:T(8,128)(2,1)} dynamic-update-slice(bf16[512,4096]{1,0:T(8,128)(2,1)} %dynamic_update_slice.55, bf16[64,2048]{1,0:T(8,128)(2,1)S(1)} %collective-permute-done.16, s32[]{:T(128)S(6)} %select_n.59, s32[]{:T(128)} %constant.63.clone.1) | dynamic-update-slice | bytes 524292 | tf_op jit(solution)/shard_map/gather/dynamic_update_slice | solution.py:363
  179.7 4.4 %dynamic_update_slice.57 = bf16[512,4096]{1,0:T(8,128)(2,1)} dynamic-update-slice(bf16[512,4096]{1,0:T(8,128)(2,1)} %dynamic_update_slice.56, bf16[64,2048]{1,0:T(8,128)(2,1)S(1)} %collective-permute-done.17, s32[]{:T(128)S(6)} %select_n.60, s32[]{:T(128)} %constant.63.clone.1) | dynamic-update-slice | bytes 524292 | tf_op jit(solution)/shard_map/gather/dynamic_update_slice | solution.py:363
  184.1 3.8 %dynamic_update_slice.58 = bf16[512,4096]{1,0:T(8,128)(2,1)} dynamic-update-slice(bf16[512,4096]{1,0:T(8,128)(2,1)} %dynamic_update_slice.57, bf16[64,2048]{1,0:T(8,128)(2,1)S(1)} %add_convert_fusion, s32[]{:T(128)S(6)} %select_n.57, s32[]{:T(128)} %constant.70.clone.1) | dynamic-update-slice | bytes 524292 | tf_op jit(solution)/shard_map/gather/dynamic_update_slice | solution.py:363
  187.9 3.8 %dynamic_update_slice.59 = bf16[512,4096]{1,0:T(8,128)(2,1)} dynamic-update-slice(bf16[512,4096]{1,0:T(8,128)(2,1)} %dynamic_update_slice.58, bf16[64,2048]{1,0:T(8,128)(2,1)S(1)} %collective-permute-done.19, s32[]{:T(128)S(6)} %select_n.58, s32[]{:T(128)} %constant.70.clone.1) | dynamic-update-slice | bytes 524292 | tf_op jit(solution)/shard_map/gather/dynamic_update_slice | solution.py:363
  191.8 3.8 %dynamic_update_slice.60 = bf16[512,4096]{1,0:T(8,128)(2,1)} dynamic-update-slice(bf16[512,4096]{1,0:T(8,128)(2,1)} %dynamic_update_slice.59, bf16[64,2048]{1,0:T(8,128)(2,1)S(1)} %collective-permute-done.20, s32[]{:T(128)S(6)} %select_n.59, s32[]{:T(128)} %constant.70.clone.1) | dynamic-update-slice | bytes 524292 | tf_op jit(solution)/shard_map/gather/dynamic_update_slice | solution.py:363
  195.6 3.8 %dynamic_update_slice.61 = bf16[512,4096]{1,0:T(8,128)(2,1)} dynamic-update-slice(bf16[512,4096]{1,0:T(8,128)(2,1)} %dynamic_update_slice.60, bf16[64,2048]{1,0:T(8,128)(2,1)S(1)} %collective-permute-done.21, s32[]{:T(128)S(6)} %select_n.60, s32[]{:T(128)} %constant.70.clone.1) | dynamic-update-slice | bytes 524292 | tf_op jit(solution)/shard_map/gather/dynamic_update_slice | solution.py:363
  199.4 4.4 %dynamic_update_slice.62 = bf16[512,4096]{1,0:T(8,128)(2,1)} dynamic-update-slice(bf16[512,4096]{1,0:T(8,128)(2,1)} %dynamic_update_slice.61, bf16[64,2048]{1,0:T(8,128)(2,1)S(1)} %collective-permute-done.22, s32[]{:T(128)S(6)} %select_n.61, s32[]{:T(128)} %constant.63.clone.1) | dynamic-update-slice | bytes 524292 | tf_op jit(solution)/shard_map/gather/dynamic_update_slice | solution.py:363
  203.8 4.6 %dynamic_update_slice.63 = bf16[512,4096]{1,0:T(8,128)(2,1)} dynamic-update-slice(bf16[512,4096]{1,0:T(8,128)(2,1)} %dynamic_update_slice.62, bf16[64,2048]{1,0:T(8,128)(2,1)} %collective-permute-done.23, s32[]{:T(128)S(6)} %select_n.62, s32[]{:T(128)} %constant.63.clone.1) | dynamic-update-slice | bytes 524292 | tf_op jit(solution)/shard_map/gather/dynamic_update_slice | solution.py:363
  208.5 3.5 %dynamic_update_slice.64 = bf16[512,4096]{1,0:T(8,128)(2,1)} dynamic-update-slice(bf16[512,4096]{1,0:T(8,128)(2,1)} %dynamic_update_slice.63, bf16[64,2048]{1,0:T(8,128)(2,1)S(1)} %collective-permute-done.24, s32[]{:T(128)S(6)} %select_n.63, s32[]{:T(128)} %constant.63.clone.1) | dynamic-update-slice | bytes 524292 | tf_op jit(solution)/shard_map/gather/dynamic_update_slice | solution.py:363
  211.9 3.4 %dynamic_update_slice.65 = bf16[512,4096]{1,0:T(8,128)(2,1)} dynamic-update-slice(bf16[512,4096]{1,0:T(8,128)(2,1)} %dynamic_update_slice.64, bf16[64,1024]{1,0:T(8,128)(2,1)} %collective-permute-done.25, s32[]{:T(128)S(6)} %select_n.64, s32[]{:T(128)} %constant.63.clone.1) | dynamic-update-slice | bytes 262148 | tf_op jit(solution)/shard_map/gather/dynamic_update_slice | solution.py:363
  215.4 3.4 %dynamic_update_slice.66 = bf16[512,4096]{1,0:T(8,128)(2,1)} dynamic-update-slice(bf16[512,4096]{1,0:T(8,128)(2,1)} %dynamic_update_slice.65, bf16[64,1024]{1,0:T(8,128)(2,1)} %collective-permute-done.26, s32[]{:T(128)S(6)} %select_n.64, s32[]{:T(128)} %constant.71.clone.1) | dynamic-update-slice | bytes 262148 | tf_op jit(solution)/shard_map/gather/dynamic_update_slice | solution.py:363
  218.8 3.8 %dynamic_update_slice.67 = bf16[512,4096]{1,0:T(8,128)(2,1)} dynamic-update-slice(bf16[512,4096]{1,0:T(8,128)(2,1)} %dynamic_update_slice.66, bf16[64,2048]{1,0:T(8,128)(2,1)S(1)} %collective-permute-done.27, s32[]{:T(128)S(6)} %select_n.61, s32[]{:T(128)} %constant.70.clone.1) | dynamic-update-slice | bytes 524292 | tf_op jit(solution)/shard_map/gather/dynamic_update_slice | solution.py:363
  222.6 3.8 %dynamic_update_slice.68 = bf16[512,4096]{1,0:T(8,128)(2,1)} dynamic-update-slice(bf16[512,4096]{1,0:T(8,128)(2,1)} %dynamic_update_slice.67, bf16[64,2048]{1,0:T(8,128)(2,1)S(1)} %collective-permute-done.28, s32[]{:T(128)S(6)} %select_n.62, s32[]{:T(128)} %constant.70.clone.1) | dynamic-update-slice | bytes 524292 | tf_op jit(solution)/shard_map/gather/dynamic_update_slice | solution.py:363
  226.5 3.0 %dynamic_update_slice.69 = bf16[512,4096]{1,0:T(8,128)(2,1)} dynamic-update-slice(bf16[512,4096]{1,0:T(8,128)(2,1)} %dynamic_update_slice.68, bf16[64,2048]{1,0:T(8,128)(2,1)S(1)} %collective-permute-done.29, s32[]{:T(128)S(6)} %select_n.63, s32[]{:T(128)} %constant.70.clone.1) | dynamic-update-slice | bytes 524292 | tf_op jit(solution)/shard_map/gather/dynamic_update_slice | solution.py:363
  229.5 3.4 %dynamic_update_slice.70 = bf16[512,4096]{1,0:T(8,128)(2,1)} dynamic-update-slice(bf16[512,4096]{1,0:T(8,128)(2,1)} %dynamic_update_slice.69, bf16[64,1024]{1,0:T(8,128)(2,1)} %collective-permute-done.30, s32[]{:T(128)S(6)} %select_n.64, s32[]{:T(128)} %constant.70.clone.1) | dynamic-update-slice | bytes 262148 | tf_op jit(solution)/shard_map/gather/dynamic_update_slice | solution.py:363
  (82 shorter events, 45.2 us)
Async XLA Ops:
  3.9 57.2 %collective-permute-start.1 = (bf16[256,4096]{1,0:T(8,128)(2,1)}, bf16[256,4096]{1,0:T(8,128)(2,1)S(1)}, u32[]{:S(2)}, u32[]{:S(2)}) collective-permute-start(bf16[256,4096]{1,0:T(8,128)(2,1)} %get-tuple-element.40), channel_id=1, source_target_pairs={{0,6},{2,0},{4,2},{6,4},{1,7},{3,1},{5,3},{7,5},{8,14},{10,8},{12,... | collective-permute-start | bytes 6291464 | tf_op jit(solution)/shard_map/weights/ppermute | solution.py:247
  7.0 54.1 %collective-permute-start = (bf16[256,4096]{1,0:T(8,128)(2,1)}, bf16[256,4096]{1,0:T(8,128)(2,1)}, u32[]{:S(2)}, u32[]{:S(2)}) collective-permute-start(bf16[256,4096]{1,0:T(8,128)(2,1)} %get-tuple-element.40), channel_id=1, source_target_pairs={{0,2},{2,4},{4,6},{6,0},{1,3},{3,5},{5,7},{7,1},{8,10},{10,12},{12... | collective-permute-start | bytes 6291464 | tf_op jit(solution)/shard_map/weights/ppermute | solution.py:247
  7.0 39.3 %all-to-all-start = ((bf16[32,32,512]{2,1,0:T(8,128)(2,1)}), bf16[32,32,512]{2,1,0:T(8,128)(2,1)S(1)}, u32[]{:S(2)}, u32[]{:S(2)}) async-start(bf16[32,32,512]{2,1,0:T(8,128)(2,1)} %get-tuple-element.39), calls=%async_computation | async-start | bytes 2097152 | tf_op jit(solution)/shard_map/all_to_all | solution.py:300
  18.7 42.5 %collective-permute-start.2 = (bf16[128,512]{1,0:T(8,128)(2,1)}, bf16[128,512]{1,0:T(8,128)(2,1)S(1)}, u32[]{:S(2)}, u32[]{:S(2)}) collective-permute-start(bf16[128,512]{1,0:T(8,128)(2,1)} %get-tuple-element.41), channel_id=1, source_target_pairs={{0,2},{2,4},{4,6},{6,0},{1,3},{3,5},{5,7},{7,1},{8,10},{10,12},{12... | collective-permute-start | bytes 393224 | tf_op jit(solution)/shard_map/weights/ppermute | solution.py:247
  19.3 41.8 %collective-permute-start.3 = (bf16[128,512]{1,0:T(8,128)(2,1)}, bf16[128,512]{1,0:T(8,128)(2,1)S(1)}, u32[]{:S(2)}, u32[]{:S(2)}) collective-permute-start(bf16[128,512]{1,0:T(8,128)(2,1)} %get-tuple-element.42), channel_id=1, source_target_pairs={{0,6},{2,0},{4,2},{6,4},{1,7},{3,1},{5,3},{7,5},{8,14},{10,8},{12,... | collective-permute-start | bytes 393224 | tf_op jit(solution)/shard_map/weights/ppermute | solution.py:247
  22.1 39.1 %collective-permute-start.4 = (bf16[128,512]{1,0:T(8,128)(2,1)}, bf16[128,512]{1,0:T(8,128)(2,1)S(1)}, u32[]{:S(2)}, u32[]{:S(2)}) collective-permute-start(bf16[128,512]{1,0:T(8,128)(2,1)} %get-tuple-element.43), channel_id=1, source_target_pairs={{0,4},{2,6},{4,0},{6,2},{1,5},{3,7},{5,1},{7,3},{8,12},{10,14},{12... | collective-permute-start | bytes 393224 | tf_op jit(solution)/shard_map/weights/ppermute | solution.py:247
  61.2 32.0 %collective-permute-start.7 = (bf16[256,4096]{1,0:T(8,128)(2,1)}, bf16[256,4096]{1,0:T(8,128)(2,1)S(1)}, u32[]{:S(2)}, u32[]{:S(2)}) collective-permute-start(bf16[256,4096]{1,0:T(8,128)(2,1)} %collective-permute-done.refs_0_), channel_id=1, source_target_pairs={{0,8},{8,0},{1,9},{9,1},{2,10},{10,2},{3,11},{11,3},{4,12},{12,4},... | collective-permute-start | bytes 6291464 | tf_op jit(solution)/shard_map/weights/ppermute | solution.py:239
  61.3 32.0 %collective-permute-start.8 = (bf16[256,4096]{1,0:T(8,128)(2,1)S(1)}, bf16[256,4096]{1,0:T(8,128)(2,1)S(1)}, u32[]{:S(2)}, u32[]{:S(2)}) collective-permute-start(bf16[256,4096]{1,0:T(8,128)(2,1)S(1)} %collective-permute-done.1.refs_2_), channel_id=1, source_target_pairs={{0,8},{8,0},{1,9},{9,1},{2,10},{10,2},{3,11},{11,3},{4,12},{12,4},... | collective-permute-start | bytes 6291464 | tf_op jit(solution)/shard_map/weights/ppermute | solution.py:239
  63.2 30.1 %collective-permute-start.6 = (bf16[128,4096]{1,0:T(8,128)(2,1)S(1)}, bf16[128,4096]{1,0:T(8,128)(2,1)S(1)}, u32[]{:S(2)}, u32[]{:S(2)}) collective-permute-start(bf16[128,4096]{1,0:T(8,128)(2,1)S(1)} %slice.65), channel_id=1, source_target_pairs={{0,6},{2,0},{4,2},{6,4},{1,7},{3,1},{5,3},{7,5},{8,14},{10,8},{12,... | collective-permute-start | bytes 3145736 | tf_op jit(solution)/shard_map/weights/ppermute | solution.py:247
  63.5 29.7 %collective-permute-start.5 = (bf16[128,4096]{1,0:T(8,128)(2,1)S(1)}, bf16[128,4096]{1,0:T(8,128)(2,1)S(1)}, u32[]{:S(2)}, u32[]{:S(2)}) collective-permute-start(bf16[128,4096]{1,0:T(8,128)(2,1)S(1)} %slice.64), channel_id=1, source_target_pairs={{0,2},{2,4},{4,6},{6,0},{1,3},{3,5},{5,7},{7,1},{8,10},{10,12},{12... | collective-permute-start | bytes 3145736 | tf_op jit(solution)/shard_map/weights/ppermute | solution.py:247
  93.2 11.9 %collective-permute-start.12 = (bf16[128,4096]{1,0:T(8,128)(2,1)S(1)}, bf16[128,4096]{1,0:T(8,128)(2,1)S(1)}, u32[]{:S(2)}, u32[]{:S(2)}) collective-permute-start(bf16[128,4096]{1,0:T(8,128)(2,1)S(1)} %collective-permute-done.5.refs_4_), channel_id=1, source_target_pairs={{0,8},{8,0},{1,9},{9,1},{2,10},{10,2},{3,11},{11,3},{4,12},{12,4},... | collective-permute-start | bytes 3145736 | tf_op jit(solution)/shard_map/weights/ppermute | solution.py:239
  94.5 10.6 %collective-permute-start.13 = (bf16[128,4096]{1,0:T(8,128)(2,1)S(1)}, bf16[128,4096]{1,0:T(8,128)(2,1)S(1)}, u32[]{:S(2)}, u32[]{:S(2)}) collective-permute-start(bf16[128,4096]{1,0:T(8,128)(2,1)S(1)} %collective-permute-done.6.refs_5_), channel_id=1, source_target_pairs={{0,8},{8,0},{1,9},{9,1},{2,10},{10,2},{3,11},{11,3},{4,12},{12,4},... | collective-permute-start | bytes 3145736 | tf_op jit(solution)/shard_map/weights/ppermute | solution.py:239
  94.7 7.9 %collective-permute-start.11 = (bf16[32,16,128]{2,1,0:T(8,128)(2,1)S(1)}, bf16[32,16,128]{2,1,0:T(8,128)(2,1)S(1)}, u32[]{:S(2)}, u32[]{:S(2)}) collective-permute-start(bf16[32,16,128]{2,1,0:T(8,128)(2,1)S(1)} %get-tuple-element.73), channel_id=1, source_target_pairs={{0,4},{2,6},{4,0},{6,2},{1,5},{3,7},{5,1},{7,3},{8,12},{10,14},{12... | collective-permute-start | bytes 393224 | tf_op jit(solution)/shard_map/quarters/ppermute | solution.py:247
  95.3 8.5 %collective-permute-start.10 = (bf16[32,16,128]{2,1,0:T(8,128)(2,1)S(1)}, bf16[32,16,128]{2,1,0:T(8,128)(2,1)S(1)}, u32[]{:S(2)}, u32[]{:S(2)}) collective-permute-start(bf16[32,16,128]{2,1,0:T(8,128)(2,1)S(1)} %get-tuple-element.74), channel_id=1, source_target_pairs={{0,6},{2,0},{4,2},{6,4},{1,7},{3,1},{5,3},{7,5},{8,14},{10,8},{12,... | collective-permute-start | bytes 393224 | tf_op jit(solution)/shard_map/quarters/ppermute | solution.py:247
  97.4 7.5 %collective-permute-start.9 = (bf16[32,16,128]{2,1,0:T(8,128)(2,1)S(1)}, bf16[32,16,128]{2,1,0:T(8,128)(2,1)S(1)}, u32[]{:S(2)}, u32[]{:S(2)}) collective-permute-start(bf16[32,16,128]{2,1,0:T(8,128)(2,1)S(1)} %get-tuple-element.75), channel_id=1, source_target_pairs={{0,2},{2,4},{4,6},{6,0},{1,3},{3,5},{5,7},{7,1},{8,10},{10,12},{12... | collective-permute-start | bytes 393224 | tf_op jit(solution)/shard_map/quarters/ppermute | solution.py:247
  108.0 9.3 %collective-permute-start.18 = (bf16[64,2048]{1,0:T(8,128)(2,1)S(1)}, bf16[64,2048]{1,0:T(8,128)(2,1)S(1)}, u32[]{:S(2)}, u32[]{:S(2)}) collective-permute-start(bf16[64,2048]{1,0:T(8,128)(2,1)S(1)} %get-tuple-element.63), channel_id=1, source_target_pairs={{0,1},{1,0},{2,3},{3,2},{4,5},{5,4},{6,7},{7,6},{8,9},{9,8},{10,11... | collective-permute-start | bytes 786440 | tf_op jit(solution)/shard_map/gather/ppermute | solution.py:239
  112.5 10.4 %collective-permute-start.14 = (bf16[64,2048]{1,0:T(8,128)(2,1)S(1)}, bf16[64,2048]{1,0:T(8,128)(2,1)S(1)}, u32[]{:S(2)}, u32[]{:S(2)}) collective-permute-start(bf16[64,2048]{1,0:T(8,128)(2,1)S(1)} %get-tuple-element.58), channel_id=1, source_target_pairs={{0,1},{1,0},{2,3},{3,2},{4,5},{5,4},{6,7},{7,6},{8,9},{9,8},{10,11... | collective-permute-start | bytes 786440 | tf_op jit(solution)/shard_map/gather/ppermute | solution.py:239
  117.4 7.7 %collective-permute-start.21 = (bf16[64,2048]{1,0:T(8,128)(2,1)S(1)}, bf16[64,2048]{1,0:T(8,128)(2,1)S(1)}, u32[]{:S(2)}, u32[]{:S(2)}) collective-permute-start(bf16[64,2048]{1,0:T(8,128)(2,1)S(1)} %add_convert_fusion), channel_id=1, source_target_pairs={{0,6},{2,0},{4,2},{6,4},{1,7},{3,1},{5,3},{7,5},{8,14},{10,8},{12,... | collective-permute-start | bytes 786440 | tf_op jit(solution)/shard_map/gather/ppermute | solution.py:247
  118.9 7.7 %collective-permute-start.20 = (bf16[64,2048]{1,0:T(8,128)(2,1)S(1)}, bf16[64,2048]{1,0:T(8,128)(2,1)S(1)}, u32[]{:S(2)}, u32[]{:S(2)}) collective-permute-start(bf16[64,2048]{1,0:T(8,128)(2,1)S(1)} %add_convert_fusion), channel_id=1, source_target_pairs={{0,2},{2,4},{4,6},{6,0},{1,3},{3,5},{5,7},{7,1},{8,10},{10,12},{12... | collective-permute-start | bytes 786440 | tf_op jit(solution)/shard_map/gather/ppermute | solution.py:247
  119.5 9.2 %collective-permute-start.19 = (bf16[64,2048]{1,0:T(8,128)(2,1)S(1)}, bf16[64,2048]{1,0:T(8,128)(2,1)S(1)}, u32[]{:S(2)}, u32[]{:S(2)}) collective-permute-start(bf16[64,2048]{1,0:T(8,128)(2,1)S(1)} %add_convert_fusion), channel_id=1, source_target_pairs={{0,1},{1,0},{2,3},{3,2},{4,5},{5,4},{6,7},{7,6},{8,9},{9,8},{10,11... | collective-permute-start | bytes 786440 | tf_op jit(solution)/shard_map/gather/ppermute | solution.py:239
  123.0 9.0 %collective-permute-start.17 = (bf16[64,2048]{1,0:T(8,128)(2,1)S(1)}, bf16[64,2048]{1,0:T(8,128)(2,1)S(1)}, u32[]{:S(2)}, u32[]{:S(2)}) collective-permute-start(bf16[64,2048]{1,0:T(8,128)(2,1)S(1)} %add_convert_fusion.1), channel_id=1, source_target_pairs={{0,6},{2,0},{4,2},{6,4},{1,7},{3,1},{5,3},{7,5},{8,14},{10,8},{12,... | collective-permute-start | bytes 786440 | tf_op jit(solution)/shard_map/gather/ppermute | solution.py:247
  124.5 9.8 %collective-permute-start.16 = (bf16[64,2048]{1,0:T(8,128)(2,1)S(1)}, bf16[64,2048]{1,0:T(8,128)(2,1)S(1)}, u32[]{:S(2)}, u32[]{:S(2)}) collective-permute-start(bf16[64,2048]{1,0:T(8,128)(2,1)S(1)} %add_convert_fusion.1), channel_id=1, source_target_pairs={{0,2},{2,4},{4,6},{6,0},{1,3},{3,5},{5,7},{7,1},{8,10},{10,12},{12... | collective-permute-start | bytes 786440 | tf_op jit(solution)/shard_map/gather/ppermute | solution.py:247
  125.1 9.2 %collective-permute-start.15 = (bf16[64,2048]{1,0:T(8,128)(2,1)S(1)}, bf16[64,2048]{1,0:T(8,128)(2,1)S(1)}, u32[]{:S(2)}, u32[]{:S(2)}) collective-permute-start(bf16[64,2048]{1,0:T(8,128)(2,1)S(1)} %add_convert_fusion.1), channel_id=1, source_target_pairs={{0,1},{1,0},{2,3},{3,2},{4,5},{5,4},{6,7},{7,6},{8,9},{9,8},{10,11... | collective-permute-start | bytes 786440 | tf_op jit(solution)/shard_map/gather/ppermute | solution.py:239
  128.7 11.1 %collective-permute-start.29 = (bf16[64,2048]{1,0:T(8,128)(2,1)S(1)}, bf16[64,2048]{1,0:T(8,128)(2,1)S(1)}, u32[]{:S(2)}, u32[]{:S(2)}) collective-permute-start(bf16[64,2048]{1,0:T(8,128)(2,1)S(1)} %collective-permute-done.19), channel_id=1, source_target_pairs={{0,2},{2,4},{4,6},{6,0},{1,3},{3,5},{5,7},{7,1},{8,10},{10,12},{12... | collective-permute-start | bytes 786440 | tf_op jit(solution)/shard_map/gather/ppermute | solution.py:247
  128.7 12.6 %collective-permute-start.28 = (bf16[64,2048]{1,0:T(8,128)(2,1)S(1)}, bf16[64,2048]{1,0:T(8,128)(2,1)S(1)}, u32[]{:S(2)}, u32[]{:S(2)}) collective-permute-start(bf16[64,2048]{1,0:T(8,128)(2,1)S(1)} %collective-permute-done.21), channel_id=1, source_target_pairs={{0,6},{2,0},{4,2},{6,4},{1,7},{3,1},{5,3},{7,5},{8,14},{10,8},{12,... | collective-permute-start | bytes 786440 | tf_op jit(solution)/shard_map/gather/ppermute | solution.py:247
  132.0 9.4 %collective-permute-start.27 = (bf16[64,2048]{1,0:T(8,128)(2,1)S(1)}, bf16[64,2048]{1,0:T(8,128)(2,1)S(1)}, u32[]{:S(2)}, u32[]{:S(2)}) collective-permute-start(bf16[64,2048]{1,0:T(8,128)(2,1)S(1)} %collective-permute-done.21), channel_id=1, source_target_pairs={{0,1},{1,0},{2,3},{3,2},{4,5},{5,4},{6,7},{7,6},{8,9},{9,8},{10,11... | collective-permute-start | bytes 786440 | tf_op jit(solution)/shard_map/gather/ppermute | solution.py:239
  134.3 10.9 %collective-permute-start.24 = (bf16[64,2048]{1,0:T(8,128)(2,1)S(1)}, bf16[64,2048]{1,0:T(8,128)(2,1)S(1)}, u32[]{:S(2)}, u32[]{:S(2)}) collective-permute-start(bf16[64,2048]{1,0:T(8,128)(2,1)S(1)} %collective-permute-done.15), channel_id=1, source_target_pairs={{0,2},{2,4},{4,6},{6,0},{1,3},{3,5},{5,7},{7,1},{8,10},{10,12},{12... | collective-permute-start | bytes 786440 | tf_op jit(solution)/shard_map/gather/ppermute | solution.py:247
  134.3 10.9 %collective-permute-start.23 = (bf16[64,2048]{1,0:T(8,128)(2,1)S(1)}, bf16[64,2048]{1,0:T(8,128)(2,1)}, u32[]{:S(2)}, u32[]{:S(2)}) collective-permute-start(bf16[64,2048]{1,0:T(8,128)(2,1)S(1)} %collective-permute-done.17), channel_id=1, source_target_pairs={{0,6},{2,0},{4,2},{6,4},{1,7},{3,1},{5,3},{7,5},{8,14},{10,8},{12,... | collective-permute-start | bytes 786440 | tf_op jit(solution)/shard_map/gather/ppermute | solution.py:247
  142.0 87.5 %collective-permute-start.30 = (bf16[64,1024]{1,0:T(8,128)(2,1)}, bf16[64,1024]{1,0:T(8,128)(2,1)}, u32[]{:S(2)}, u32[]{:S(2)}) collective-permute-start(bf16[64,1024]{1,0:T(8,128)(2,1)} %slice.80), channel_id=1, source_target_pairs={{0,2},{2,4},{4,6},{6,0},{1,3},{3,5},{5,7},{7,1},{8,10},{10,12},{12... | collective-permute-start | bytes 393224 | tf_op jit(solution)/shard_map/gather/ppermute | solution.py:247
  142.0 90.9 %collective-permute-start.31 = (bf16[64,1024]{1,0:T(8,128)(2,1)S(1)}, bf16[64,1024]{1,0:T(8,128)(2,1)}, u32[]{:S(2)}, u32[]{:S(2)}) collective-permute-start(bf16[64,1024]{1,0:T(8,128)(2,1)S(1)} %slice.81), channel_id=1, source_target_pairs={{0,6},{2,0},{4,2},{6,4},{1,7},{3,1},{5,3},{7,5},{8,14},{10,8},{12,... | collective-permute-start | bytes 393224 | tf_op jit(solution)/shard_map/gather/ppermute | solution.py:247
  147.5 64.4 %collective-permute-start.25 = (bf16[64,1024]{1,0:T(8,128)(2,1)}, bf16[64,1024]{1,0:T(8,128)(2,1)}, u32[]{:S(2)}, u32[]{:S(2)}) collective-permute-start(bf16[64,1024]{1,0:T(8,128)(2,1)} %slice.77), channel_id=1, source_target_pairs={{0,2},{2,4},{4,6},{6,0},{1,3},{3,5},{5,7},{7,1},{8,10},{10,12},{12... | collective-permute-start | bytes 393224 | tf_op jit(solution)/shard_map/gather/ppermute | solution.py:247
  147.5 67.9 %collective-permute-start.26 = (bf16[64,1024]{1,0:T(8,128)(2,1)}, bf16[64,1024]{1,0:T(8,128)(2,1)}, u32[]{:S(2)}, u32[]{:S(2)}) collective-permute-start(bf16[64,1024]{1,0:T(8,128)(2,1)} %slice.79), channel_id=1, source_target_pairs={{0,6},{2,0},{4,2},{6,4},{1,7},{3,1},{5,3},{7,5},{8,14},{10,8},{12,... | collective-permute-start | bytes 393224 | tf_op jit(solution)/shard_map/gather/ppermute | solution.py:247
  (6 other events, 129.6 us)

commit v5 on v1

v5 whole, which is shorter than its diff:
```python
import functools
import math

import jax
import jax.numpy as jnp
import ml_dtypes
import numpy as np
from jax import lax
from jax.experimental import pallas as pl
from jax.experimental.pallas import tpu as pltpu
from jax.sharding import Mesh, PartitionSpec as P

MIB = 1024 * 1024
GROUP = 4
STREAMS = 2
WIDTH = 512


def transform_table(rows):
    j = np.arange(rows, dtype=np.int64)[:, None]
    f = np.arange(rows, dtype=np.int64)[None, :]
    angle = (j * (2 * f + 1) % (4 * rows)) * (2.0 * math.pi / (4 * rows))
    return np.concatenate([np.cos(angle), -np.sin(angle)], 1).astype(ml_dtypes.bfloat16)


def pack_kernel(
    key_hbm, value_hbm, filter_hbm, weight_hbm, out_ref, half_ref, key_ref, value_ref, filter_ref, sems
):
    parts, both, rows = out_ref.shape
    share, half = both // 2, half_ref.shape[0]
    start = pl.multiple_of(lax.axis_index("core") * half, half)
    moves = (
        (key_hbm, key_ref),
        (value_hbm, value_ref),
        (filter_hbm, filter_ref),
        (weight_hbm.at[pl.ds(start, half)], half_ref),
    )
    copies = [pltpu.make_async_copy(*move, sems.at[i]) for i, move in enumerate(moves)]
    for copy in copies:
        copy.start()
    copies[0].wait()
    copies[1].wait()
    mixer = key_ref[...].astype(jnp.float32) * value_ref[...].astype(jnp.float32)
    out_ref[:, :share, :] = mixer.astype(jnp.bfloat16).T.reshape(parts, share, rows)
    copies[2].wait()
    out_ref[:, share:, :] = filter_ref[...].T.reshape(parts, share, rows)
    copies[3].wait()


def conv_kernel(
    signal_ref, gain_ref, table_ref, out_ref, mixer_spec, filter_spec, product
):
    blocks, both, rows = signal_ref.shape
    share = both // 2
    table = table_ref[...]

    def spectrum(signal):
        flat = signal.reshape(blocks * share, rows)
        value = jnp.dot(flat, table, preferred_element_type=jnp.float32)
        return value.reshape(blocks, share, 2 * rows)

    mixer_spec[...] = spectrum(signal_ref[:, :share, :])
    filter_spec[...] = spectrum(signal_ref[:, share:, :])

    lane = lax.broadcasted_iota(jnp.int32, (8, 128), 1)
    sign = jnp.where(lane % 2 == 0, 1.0, -1.0).astype(jnp.float32)
    lane_tiles = rows // 128

    def tile(step, carry):
        row = pl.multiple_of((step // lane_tiles) * 8, 8)
        real = pl.multiple_of((step % lane_tiles) * 128, 128)
        imag = pl.multiple_of(rows + (step % lane_tiles) * 128, 128)

        def load(ref, block):
            return (
                ref[block, pl.ds(row, 8), pl.ds(real, 128)],
                ref[block, pl.ds(row, 8), pl.ds(imag, 128)],
            )

        def window(block):
            now_real, now_imag = load(mixer_spec, block)
            if block > 0:
                last_real, last_imag = load(mixer_spec, block - 1)
                now_real, now_imag = now_real - sign * last_imag, now_imag + sign * last_real
            return now_real, now_imag

        for block in reversed(range(blocks)):
            now_real, now_imag = window(block)
            mixer_spec[block, pl.ds(row, 8), pl.ds(real, 128)] = now_real
            mixer_spec[block, pl.ds(row, 8), pl.ds(imag, 128)] = now_imag

        for first in range(0, blocks, GROUP):
            sums = [[None] * 3 for _ in range(GROUP)]
            held = {}
            for lag in range(first + GROUP):
                filter_real, filter_imag = load(filter_spec, lag)
                filter_both = filter_real + filter_imag
                for i in range(GROUP):
                    block = first + i - lag
                    if block < 0:
                        continue
                    if block not in held:
                        real_part, imag_part = load(mixer_spec, block)
                        held[block] = (real_part, imag_part, real_part + imag_part)
                    terms = (
                        filter_real * held[block][0],
                        filter_imag * held[block][1],
                        filter_both * held[block][2],
                    )
                    for s in range(3):
                        sums[i][s] = terms[s] if sums[i][s] is None else sums[i][s] + terms[s]
                held.pop(first + GROUP - 1 - lag, None)
            for i in range(GROUP):
                one, two, three = sums[i]
                product[first + i, pl.ds(row, 8), pl.ds(real, 128)] = one - two
                product[first + i, pl.ds(row, 8), pl.ds(imag, 128)] = three - one - two
        return carry

    lax.fori_loop(0, (share // 8) * lane_tiles, tile, 0)
    flat = product[...].astype(jnp.bfloat16).reshape(blocks * share, 2 * rows)
    conv = lax.dot_general(
        flat, table, (((1,), (1,)), ((), ())), preferred_element_type=jnp.float32
    ) * (1.0 / rows)
    mixer = signal_ref[:, :share, :].astype(jnp.float32)
    total = conv.reshape(blocks, share, rows) + gain_ref[...] * mixer
    out_ref[...] = total.astype(jnp.bfloat16)


def gate_kernel(total_ref, query_ref, own_ref, toward_ref, back_ref, far_ref, gated_ref):
    rows, channels = query_ref.shape
    core, y, keep = lax.axis_index("core"), lax.axis_index("y"), lax.axis_index("z")
    total = total_ref[...].reshape(channels, rows).T.astype(jnp.float32)
    gated_ref[...] = (query_ref[...].astype(jnp.float32) * total).astype(jnp.bfloat16)
    half, piece = channels // 2, own_ref.shape[0] // 2
    steps = (own_ref, y), (toward_ref, y + 1 - 2 * core), (back_ref, y + 3 + 2 * core)
    for out_ref, place in steps + ((far_ref, y + 2),):
        for part, side in enumerate((1 - keep, keep)):
            start = pl.multiple_of((place % 4 * 2 + side) * piece, piece)
            rows_out = slice(part * piece, (part + 1) * piece)
            if out_ref is own_ref:
                out_ref[rows_out, :] = gated_ref[pl.ds(start, piece), :]
                continue
            for column, sender in enumerate((core, 1 - core)):
                columns = pl.ds(pl.multiple_of(sender * half, half), half)
                here = slice(column * half, (column + 1) * half)
                out_ref[rows_out, here] = gated_ref[pl.ds(start, piece), columns]


def own_kernel(gated_ref, weight_ref, out_ref):
    for start in range(0, out_ref.shape[1], WIDTH):
        columns = slice(start, start + WIDTH)
        out_ref[:, columns] = jnp.dot(
            gated_ref[...], weight_ref[:, columns], preferred_element_type=jnp.float32
        )


def rest_kernel(first, partial_ref, *refs):
    gated, weights, (other_ref, own_ref) = refs[:3], refs[3:-2], refs[-2:]
    piece, columns = other_ref.shape
    depth = weights[0].shape[0]
    for column in range(0, columns, WIDTH):
        here = slice(first + column, first + column + WIDTH)
        value = partial_ref[:, here]
        for i, weight in enumerate(weights):
            half = slice(i % 2 * depth, (i % 2 + 1) * depth)
            value = value + jnp.dot(
                gated[i // 2][:, half], weight[:, here], preferred_element_type=jnp.float32
            )
        value = value.astype(jnp.bfloat16)
        other_ref[:, column : column + WIDTH] = value[:piece]
        own_ref[:, column : column + WIDTH] = value[piece:]


def place_kernel(layout, fresh, *refs):
    pieces, (out_ref, sems) = refs[0 if fresh else 1 : -2], refs[-2:]
    y, z = lax.axis_index("y"), lax.axis_index("z")
    copies = []
    for i, (piece, (slot, column)) in enumerate(zip(pieces, layout)):
        count, width = piece.shape
        row = ((y + slot // 2) % 4 * 2 + (z + slot) % 2) * count
        target = out_ref.at[pl.ds(pl.multiple_of(row, count), count), pl.ds(column, width)]
        copies.append(pltpu.make_async_copy(piece, target, sems.at[i]))
    for copy in copies:
        copy.start()
    for copy in copies:
        copy.wait()


VMEM = pl.BlockSpec(memory_space=pltpu.VMEM)
HBM = pl.BlockSpec(memory_space=pltpu.HBM)


def whole(kernel, shapes, in_specs, out_specs, scratch=(), limit=16, cost=0, **rest):
    return pl.pallas_call(
        kernel,
        out_shape=[jax.ShapeDtypeStruct(*shape) for shape in shapes],
        in_specs=in_specs,
        out_specs=out_specs,
        scratch_shapes=list(scratch),
        compiler_params=pltpu.CompilerParams(vmem_limit_bytes=limit * MIB),
        cost_estimate=pl.CostEstimate(flops=2 * cost, bytes_accessed=8 * MIB, transcendentals=0),
        **rest,
    )


def place_pieces(out, shape, found):
    fresh = out is None
    layout, values = [item[:2] for item in found], [item[2] for item in found]
    return whole(
        functools.partial(place_kernel, layout, fresh),
        [(shape, jnp.bfloat16)],
        [HBM] * (not fresh) + [VMEM] * len(values),
        [HBM],
        [pltpu.SemaphoreType.DMA((len(values),))],
        input_output_aliases={} if fresh else {0: 0},
    )(*([] if fresh else [out]), *values)[0]


def swap(axis):
    return lambda value: lax.ppermute(value, axis, [(0, 1), (1, 0)])


along_z, along_core = swap("z"), swap("core")


def along_y(value, steps):
    count = lax.axis_size("y")
    return lax.ppermute(value, "y", [(i, (i + steps) % count) for i in range(count)])


def mirrored(value, steps):
    count = lax.axis_size("y")
    pairs = [
        (core * count + i, core * count + (i + (steps, -steps)[core]) % count)
        for core in range(2)
        for i in range(count)
    ]
    return lax.ppermute(value, ("core", "y"), pairs)


def add(*terms):
    return sum(term.astype(jnp.float32) for term in terms).astype(jnp.bfloat16)


def reduce_and_gather(halves, shape):
    first, last, early, late = [], [], [], []
    width = halves[0][1].shape[1]
    arrived = [along_z(other) for other, _ in halves]
    for (_, own), from_z in zip(halves, arrived):
        own = add(own, from_z)
        first.append((own, along_z(own), along_y(own, 1), along_y(own, -1)))
    for stream, (own, own_z, down, up) in enumerate(first):
        column = stream * width
        own_z, down, up = lax.optimization_barrier((own_z, down, up))
        early += [(slot, column, value) for slot, value in ((0, own), (1, own_z), (6, down), (2, up))]
        last.append((along_z(up), along_y(up, -1), along_y(own_z, 1)))
    out = place_pieces(None, shape, early)
    for stream, (up_z, far, down_z) in enumerate(last):
        column = stream * width
        up_z, far, down_z = lax.optimization_barrier((up_z, far, down_z))
        late += [(3, column, up_z), (4, column, far), (7, column, down_z)]
        middle = width // 2
        late.append((5, column, along_y(down_z[:, :middle], 1)))
        late.append((5, column + middle, along_y(up_z[:, middle:], -1)))
    return place_pieces(out, shape, late)


def body(query_branch, key_branch, value_branch, filters, skip_gain, out_weight):
    ctx = lax.axis_index("block") * 2 + lax.axis_index("core")
    ctx_count = lax.axis_size("block") * 2
    rows, channels = query_branch.shape
    share = channels // ctx_count
    features = out_weight.shape[1]
    quarter = rows // lax.axis_size("y")
    half16, full32 = jnp.bfloat16, jnp.float32
    table = jnp.asarray(transform_table(rows))
    gain = lax.dynamic_slice(skip_gain, (ctx * share,), (share,))[:, None]

    with jax.named_scope("pack"):
        square = pltpu.VMEM((rows, channels), half16)
        outgoing, weight_half = whole(
            pack_kernel,
            [((ctx_count, 2 * share, rows), half16), ((channels // 2, features), half16)],
            [HBM] * 4,
            [VMEM] * 2,
            [square, square, square, pltpu.SemaphoreType.DMA((4,))],
            limit=60,
        )(key_branch, value_branch, filters, out_weight)
    with jax.named_scope("weights"):
        toward, back = mirrored(weight_half, 1), mirrored(weight_half, -1)
    arrived = lax.all_to_all(outgoing, ("block", "core"), split_axis=0, concat_axis=0, tiled=True)
    spec = pltpu.VMEM((ctx_count, share, 2 * rows), full32)
    with jax.named_scope("conv"):
        (total,) = whole(
            conv_kernel,
            [((ctx_count, share, rows), half16)],
            [VMEM] * 3,
            [VMEM],
            [spec] * 3,
            limit=24,
        )(arrived, gain, table)
    with jax.named_scope("weights"):
        total, toward, back = lax.optimization_barrier((total, toward, back))
        far = mirrored(toward, 1)
        swapped = [along_core(toward), along_core(back)]
    total = lax.all_to_all(total, ("block", "core"), split_axis=0, concat_axis=0, tiled=True)
    with jax.named_scope("weights"):
        total, far, *swapped = lax.optimization_barrier((total, far, *swapped))
        weights = (toward, swapped[1], back, swapped[0], far, along_core(far))
    with jax.named_scope("gate"):
        gated = whole(
            gate_kernel, [((quarter, channels), half16)] * 4, [VMEM] * 2, [VMEM] * 4, [square]
        )(total, query_branch)
    with jax.named_scope("quarters"):
        others = mirrored(gated[1], 1), mirrored(gated[2], -1), along_y(gated[3], 2)
    cost = quarter * channels * features
    with jax.named_scope("own"):
        (partial_value,) = whole(
            own_kernel, [((quarter, features), full32)], [VMEM] * 2, [VMEM], limit=12, cost=cost
        )(gated[0], out_weight)
    with jax.named_scope("rest"):
        width = features // STREAMS
        halves = [
            whole(
                functools.partial(rest_kernel, stream * width),
                [((quarter // 2, width), half16)] * 2,
                [VMEM] * (4 + len(weights)),
                [VMEM] * 2,
                limit=20,
                cost=cost,
            )(partial_value, *others, *weights)
            for stream in range(STREAMS)
        ]
    with jax.named_scope("gather"):
        return reduce_and_gather(halves, (rows, features))


def solution(mesh):
    fine = Mesh(mesh.devices.reshape(-1, 2, 4, 2), ("block", "core", "y", "z"))
    ctx, tp = ("block", "core"), ("y", "z")
    placed = (P(ctx, tp), P(ctx, tp), P(ctx, tp), P(ctx, tp), P(tp), P(tp, None))
    return jax.shard_map(
        body, mesh=fine, in_specs=placed, out_specs=P(ctx, None), check_vma=False
    )
```

time: 244 us -> 148 us (0.61)
  blocking collectives: 117 us -> 27.5 us
  starting transfers between devices: 0.01 us -> 49.8 us
  waiting for transfers between devices: 88.9 us -> 45.5 us
  between operations: 13.4 us -> 0.35 us
  Pallas kernels: 9.74 us -> 19.7 us
  local copies, waits for them, and re-layouts: 10.3 us -> 2.48 us
  other arithmetic: 3.84 us -> 0.13 us
    all_to_all x3 -> x1, blocking collectives: 117 us -> 27.5 us  [body(): lax.all_to_all(total, ('block', 'core'), split_axis=0, concat_axis=0, til...]
    all_gather x1 -> x0, waiting for transfers between devices: 88.9 us -> none  [body(): return lax.all_gather(summed, 'tp', axis=0, tiled=True)]
    ppermute x0 -> x27, starting transfers between devices: none -> 38.2 us  [the longest x13 18.2 us: along_y(): lax.ppermute(value, 'y', [(i, (i + steps) % count) for i in range(count)])]
    all_to_all x0 -> x1, waiting for transfers between devices: none -> 27.5 us  [body(): lax.all_to_all(outgoing, ('block', 'core'), split_axis=0, concat_axis=0,...]
    ppermute x0 -> x27, waiting for transfers between devices: none -> 18 us  [the longest x9 8.6 us: swap(): return lambda value: lax.ppermute(value, axis, [(0, 1), (1, 0)])]
    all_to_all x0 -> x1, starting transfers between devices: none -> 11.6 us  [body(): lax.all_to_all(outgoing, ('block', 'core'), split_axis=0, concat_axis=0,...]
    pallas_call x3 -> x8, Pallas kernels: 9.74 us -> 19.7 us  [the longest x1 6.92 us: body(): whole(conv_kernel, [((ctx_count, share, rows), half16)], [VMEM] * 3, [VME...]
    unnamed x21 -> x8, local copies, waits for them, and re-layouts: 10.3 us -> 2.27 us
  transfers between devices with their start and end apart: 1 -> 28, of which waited for: 1 -> 10; matrix products, arithmetic and copies ran while one was open for 0% -> 0% of each run, Pallas kernels for 0% -> 8%
where the time goes in v5:
time: 148 us; the launch traced here: 145 us
  starting transfers between devices  49.8 us (34%)
  waiting for transfers between devices  45.5 us (31%)
  blocking collectives  27.5 us (19%)
  Pallas kernels  19.7 us (13%)
  local copies, waits for them, and re-layouts  2.48 us (2%)
    all_to_all x1, blocking collectives, body(): lax.all_to_all(total, ('block', 'core'), split_axis=0, concat_axis=0, til...  27.5 us
    all_to_all x1, waiting for transfers between devices, body(): lax.all_to_all(outgoing, ('block', 'core'), split_axis=0, concat_axis=0,...  27.5 us
    ppermute x13, starting transfers between devices, along_y(): lax.ppermute(value, 'y', [(i, (i + steps) % count) for i in range(count)])  18.2 us
    ppermute x9, starting transfers between devices, swap(): return lambda value: lax.ppermute(value, axis, [(0, 1), (1, 0)])  13 us
    all_to_all x1, starting transfers between devices, body(): lax.all_to_all(outgoing, ('block', 'core'), split_axis=0, concat_axis=0,...  11.6 us
    ppermute x9, waiting for transfers between devices, swap(): return lambda value: lax.ppermute(value, axis, [(0, 1), (1, 0)])  8.6 us
    ppermute x5, starting transfers between devices, mirrored(): return lax.ppermute(value, ('core', 'y'), pairs)  6.99 us
    pallas_call x1, Pallas kernels, body(): whole(conv_kernel, [((ctx_count, share, rows), half16)], [VMEM] * 3, [VME...  6.92 us
  transfers between devices with their start and end apart: 28, of which 10 were waited for; matrix products, arithmetic and copies ran while one was open for 0% of the time, Pallas kernels for 8%

profile of v5, /device:TPU:2, one launch (start us, length us, event | category | flops | bytes accessed | tf_op | source)
XLA Modules:
  0.0 145.5 jit_solution(9566199071046475190)
XLA Ops:
  0.0 3.8 %pack.1 = (bf16[32,32,512]{2,1,0:T(8,128)(2,1)}, bf16[256,4096]{1,0:T(8,128)(2,1)}) custom-call(bf16[512,512]{1,0:T(8,128)(2,1)} %key_hbm.1, bf16[512,512]{1,0:T(8,128)(2,1)} %value_hbm.1, bf16[512,512]{1,0:T(8,128)(2,1)} %filter_hbm.1, bf16[512,4096]{1,0:T(8,128)(2,1)} %weight_ref.1), custom_call_target="tpu_custom_call" | custom-call | bytes 8388608 | tf_op jit(solution)/shard_map/pack/pallas_call | solution.py:281
  3.8 3.1 %collective-permute-start.1 = (bf16[256,4096]{1,0:T(8,128)(2,1)}, bf16[256,4096]{1,0:T(8,128)(2,1)S(1)}, u32[]{:S(2)}, u32[]{:S(2)}) collective-permute-start(bf16[256,4096]{1,0:T(8,128)(2,1)} %get-tuple-element.35), channel_id=1, source_target_pairs={{0,6},{2,0},{4,2},{6,4},{8,10},{10,12},{12,14},{14,8},{1,7},{3,1},... | collective-permute-start | bytes 6291464 | tf_op jit(solution)/shard_map/weights/ppermute | solution.py:238
  6.9 11.6 %all-to-all-start = ((bf16[32,32,512]{2,1,0:T(8,128)(2,1)}), bf16[32,32,512]{2,1,0:T(8,128)(2,1)S(1)}, u32[]{:S(2)}, u32[]{:S(2)}) async-start(bf16[32,32,512]{2,1,0:T(8,128)(2,1)} %get-tuple-element.34), calls=%async_computation | async-start | bytes 2097152 | tf_op jit(solution)/shard_map/all_to_all | solution.py:291
  18.7 27.5 %all-to-all-done.signal_ref = bf16[32,32,512]{2,1,0:T(8,128)(2,1)S(1)} async-done(((bf16[32,32,512]{2,1,0:T(8,128)(2,1)}), bf16[32,32,512]{2,1,0:T(8,128)(2,1)S(1)}, u32[]{:S(2)}, u32[]{:S(2)}) %all-to-all-start) | async-done | bytes 1048608 | tf_op jit(solution)/shard_map/all_to_all | solution.py:291
  46.2 1.2 copy-done.2
  47.4 6.9 %conv.1 = bf16[32,16,512]{2,1,0:T(8,128)(2,1)S(1)} custom-call(bf16[32,32,512]{2,1,0:T(8,128)(2,1)S(1)} %all-to-all-done.signal_ref, f32[16,1]{1,0:T(8,128)S(1)} %copy.9.gain_ref, bf16[512,1024]{1,0:T(8,128)(2,1)S(1)} %copy-done.2), custom_call_target="tpu_custom_call" | custom-call | bytes 8388608 | tf_op jit(solution)/shard_map/conv/pallas_call | solution.py:294
  54.4 1.0 collective-permute-start.4
  56.1 27.5 %all_to_all.10.total_ref = bf16[32,16,512]{2,1,0:T(8,128)(2,1)S(1)} all-to-all(bf16[32,16,512]{2,1,0:T(8,128)(2,1)S(1)} %conv.1), channel_id=1, replica_groups=mesh['block'=16,'core'=2,'y'=4,'z'=2] {'block','core'}, dimensions={0} | all-to-all | bytes 1048576 | tf_op jit(solution)/shard_map/all_to_all | solution.py:306
  83.6 1.3 collective-permute-start.8
  84.9 1.0 copy-done.3
  86.8 2.7 %collective-permute-start.6 = (bf16[128,512]{1,0:T(8,128)(2,1)S(1)}, bf16[128,512]{1,0:T(8,128)(2,1)S(1)}, u32[]{:S(2)}, u32[]{:S(2)}) collective-permute-start(bf16[128,512]{1,0:T(8,128)(2,1)S(1)} %get-tuple-element.42), channel_id=1, source_target_pairs={{0,6},{2,0},{4,2},{6,4},{8,10},{10,12},{12,14},{14,8},{1,7},{3,1},... | collective-permute-start | bytes 393224 | tf_op jit(solution)/shard_map/quarters/ppermute | solution.py:238
  91.1 5.2 %collective-permute-done.5.refs_0_ = bf16[128,512]{1,0:T(8,128)(2,1)S(1)} collective-permute-done((bf16[128,512]{1,0:T(8,128)(2,1)S(1)}, bf16[128,512]{1,0:T(8,128)(2,1)S(1)}, u32[]{:S(2)}, u32[]{:S(2)}) %collective-permute-start.5) | collective-permute-done | bytes 131104 | tf_op jit(solution)/shard_map/quarters/ppermute | solution.py:238
  96.4 2.6 %rest.3 = (bf16[64,2048]{1,0:T(8,128)(2,1)S(1)}, bf16[64,2048]{1,0:T(8,128)(2,1)S(1)}) custom-call(f32[128,4096]{1,0:T(8,128)S(1)} %own.1.partial_ref, bf16[128,512]{1,0:T(8,128)(2,1)S(1)} %collective-permute-done.5.refs_0_, bf16[128,512]{1,0:T(8,128)(2,1)S(1)} %collective-permute-done.6.refs_1_, bf16[128,512]{1,0:T(8,128)(2,1)S(1)} %collective-permute-done.7.refs_2_, ...), custom_call_target="tpu_custom_call" | custom-call | flops 536870912 | bytes 8388608 | tf_op jit(solution)/shard_map/rest/pallas_call | solution.py:324
  99.0 1.8 %collective-permute-start.13 = (bf16[64,2048]{1,0:T(8,128)(2,1)S(1)}, bf16[64,2048]{1,0:T(8,128)(2,1)S(1)}, u32[]{:S(2)}, u32[]{:S(2)}) collective-permute-start(bf16[64,2048]{1,0:T(8,128)(2,1)S(1)} %get-tuple-element.53), channel_id=1, source_target_pairs={{0,1},{1,0},{2,3},{3,2},{4,5},{5,4},{6,7},{7,6},{8,9},{9,8},{10,11... | collective-permute-start | bytes 786440 | tf_op jit(solution)/shard_map/gather/ppermute | solution.py:220
  100.8 2.6 %rest.2 = (bf16[64,2048]{1,0:T(8,128)(2,1)S(1)}, bf16[64,2048]{1,0:T(8,128)(2,1)S(1)}) custom-call(f32[128,4096]{1,0:T(8,128)S(1)} %own.1.partial_ref, bf16[128,512]{1,0:T(8,128)(2,1)S(1)} %collective-permute-done.5.refs_0_, bf16[128,512]{1,0:T(8,128)(2,1)S(1)} %collective-permute-done.6.refs_1_, bf16[128,512]{1,0:T(8,128)(2,1)S(1)} %collective-permute-done.7.refs_2_, ...), custom_call_target="tpu_custom_call" | custom-call | flops 536870912 | bytes 8388608 | tf_op jit(solution)/shard_map/rest/pallas_call | solution.py:324
  104.0 4.5 %collective-permute-done.13 = bf16[64,2048]{1,0:T(8,128)(2,1)S(1)} collective-permute-done((bf16[64,2048]{1,0:T(8,128)(2,1)S(1)}, bf16[64,2048]{1,0:T(8,128)(2,1)S(1)}, u32[]{:S(2)}, u32[]{:S(2)}) %collective-permute-start.13) | collective-permute-done | bytes 262176 | tf_op jit(solution)/shard_map/gather/ppermute | solution.py:220
  108.5 1.3 collective-permute-start.16
  110.6 1.5 %collective-permute-start.14 = (bf16[64,2048]{1,0:T(8,128)(2,1)S(1)}, bf16[64,2048]{1,0:T(8,128)(2,1)S(1)}, u32[]{:S(2)}, u32[]{:S(2)}) collective-permute-start(bf16[64,2048]{1,0:T(8,128)(2,1)S(1)} %add_convert_fusion.refs_4_), channel_id=1, source_target_pairs={{0,1},{1,0},{2,3},{3,2},{4,5},{5,4},{6,7},{7,6},{8,9},{9,8},{10,11... | collective-permute-start | bytes 786440 | tf_op jit(solution)/shard_map/gather/ppermute | solution.py:220
  112.2 1.9 %collective-permute-done.9 = bf16[64,2048]{1,0:T(8,128)(2,1)S(1)} collective-permute-done((bf16[64,2048]{1,0:T(8,128)(2,1)S(1)}, bf16[64,2048]{1,0:T(8,128)(2,1)S(1)}, u32[]{:S(2)}, u32[]{:S(2)}) %collective-permute-start.9) | collective-permute-done | bytes 262176 | tf_op jit(solution)/shard_map/gather/ppermute | solution.py:220
  114.2 1.4 collective-permute-start.12
  116.3 1.9 %collective-permute-start.10 = (bf16[64,2048]{1,0:T(8,128)(2,1)S(1)}, bf16[64,2048]{1,0:T(8,128)(2,1)S(1)}, u32[]{:S(2)}, u32[]{:S(2)}) collective-permute-start(bf16[64,2048]{1,0:T(8,128)(2,1)S(1)} %add_convert_fusion.1.refs_0_), channel_id=1, source_target_pairs={{0,1},{1,0},{2,3},{3,2},{4,5},{5,4},{6,7},{7,6},{8,9},{9,8},{10,11... | collective-permute-start | bytes 786440 | tf_op jit(solution)/shard_map/gather/ppermute | solution.py:220
  118.9 1.0 collective-permute-done.14.refs_5_
  119.9 3.2 %collective-permute-start.23 = (bf16[64,2048]{1,0:T(8,128)(2,1)S(1)}, bf16[64,2048]{1,0:T(8,128)(2,1)S(1)}, u32[]{:S(2)}, u32[]{:S(2)}) collective-permute-start(bf16[64,2048]{1,0:T(8,128)(2,1)S(1)} %collective-permute-done.16.refs_7_), channel_id=1, source_target_pairs={{0,6},{2,0},{4,2},{6,4},{1,7},{3,1},{5,3},{7,5},{8,14},{10,8},{12,... | collective-permute-start | bytes 786440 | tf_op jit(solution)/shard_map/gather/ppermute | solution.py:228
  123.1 2.2 %collective-permute-start.22 = (bf16[64,2048]{1,0:T(8,128)(2,1)S(1)}, bf16[64,2048]{1,0:T(8,128)(2,1)S(1)}, u32[]{:S(2)}, u32[]{:S(2)}) collective-permute-start(bf16[64,2048]{1,0:T(8,128)(2,1)S(1)} %collective-permute-done.16.refs_7_), channel_id=1, source_target_pairs={{0,1},{1,0},{2,3},{3,2},{4,5},{5,4},{6,7},{7,6},{8,9},{9,8},{10,11... | collective-permute-start | bytes 786440 | tf_op jit(solution)/shard_map/gather/ppermute | solution.py:220
  125.5 3.2 %collective-permute-start.18 = (bf16[64,2048]{1,0:T(8,128)(2,1)S(1)}, bf16[64,2048]{1,0:T(8,128)(2,1)S(1)}, u32[]{:S(2)}, u32[]{:S(2)}) collective-permute-start(bf16[64,2048]{1,0:T(8,128)(2,1)S(1)} %collective-permute-done.12.refs_3_), channel_id=1, source_target_pairs={{0,6},{2,0},{4,2},{6,4},{1,7},{3,1},{5,3},{7,5},{8,14},{10,8},{12,... | collective-permute-start | bytes 786440 | tf_op jit(solution)/shard_map/gather/ppermute | solution.py:228
  128.7 1.9 %collective-permute-done.24.refs_8_ = bf16[64,2048]{1,0:T(8,128)(2,1)S(1)} collective-permute-done((bf16[64,2048]{1,0:T(8,128)(2,1)S(1)}, bf16[64,2048]{1,0:T(8,128)(2,1)S(1)}, u32[]{:S(2)}, u32[]{:S(2)}) %collective-permute-start.24) | collective-permute-done | bytes 262176 | tf_op jit(solution)/shard_map/gather/ppermute | solution.py:228
  130.7 2.7 %collective-permute-start.17 = (bf16[64,2048]{1,0:T(8,128)(2,1)S(1)}, bf16[64,2048]{1,0:T(8,128)(2,1)S(1)}, u32[]{:S(2)}, u32[]{:S(2)}) collective-permute-start(bf16[64,2048]{1,0:T(8,128)(2,1)S(1)} %collective-permute-done.12.refs_3_), channel_id=1, source_target_pairs={{0,1},{1,0},{2,3},{3,2},{4,5},{5,4},{6,7},{7,6},{8,9},{9,8},{10,11... | collective-permute-start | bytes 786440 | tf_op jit(solution)/shard_map/gather/ppermute | solution.py:220
  133.4 3.2 %collective-permute-start.26 = (bf16[64,1024]{1,0:T(8,128)(2,1)S(1)}, bf16[64,1024]{1,0:T(8,128)(2,1)S(1)}, u32[]{:S(2)}, u32[]{:S(2)}) collective-permute-start(bf16[64,1024]{1,0:T(8,128)(2,1)S(1)} %slice.15), channel_id=1, source_target_pairs={{0,6},{2,0},{4,2},{6,4},{1,7},{3,1},{5,3},{7,5},{8,14},{10,8},{12,... | collective-permute-start | bytes 393224 | tf_op jit(solution)/shard_map/gather/ppermute | solution.py:228
  137.8 3.2 %collective-permute-start.21 = (bf16[64,1024]{1,0:T(8,128)(2,1)S(1)}, bf16[64,1024]{1,0:T(8,128)(2,1)S(1)}, u32[]{:S(2)}, u32[]{:S(2)}) collective-permute-start(bf16[64,1024]{1,0:T(8,128)(2,1)S(1)} %slice.13), channel_id=1, source_target_pairs={{0,6},{2,0},{4,2},{6,4},{1,7},{3,1},{5,3},{7,5},{8,14},{10,8},{12,... | collective-permute-start | bytes 393224 | tf_op jit(solution)/shard_map/gather/ppermute | solution.py:228
  141.0 1.4 gather.2.refs_0_
  142.4 1.5 %collective-permute-done.20.refs_4_ = bf16[64,1024]{1,0:T(8,128)(2,1)S(1)} collective-permute-done((bf16[64,1024]{1,0:T(8,128)(2,1)S(1)}, bf16[64,1024]{1,0:T(8,128)(2,1)S(1)}, u32[]{:S(2)}, u32[]{:S(2)}) %collective-permute-start.20) | collective-permute-done | bytes 131104 | tf_op jit(solution)/shard_map/gather/ppermute | solution.py:228
  143.9 1.4 gather.3
  (49 shorter events, 7.7 us)
Async XLA Ops:
  0.0 18.5 %copy-start = (f32[512]{0:T(512)S(1)}, f32[512]{0:T(512)}, u32[]{:S(2)}) copy-start(f32[512]{0:T(512)} %param.11) | copy-start | bytes 6148
  3.8 50.6 %collective-permute-start.1 = (bf16[256,4096]{1,0:T(8,128)(2,1)}, bf16[256,4096]{1,0:T(8,128)(2,1)S(1)}, u32[]{:S(2)}, u32[]{:S(2)}) collective-permute-start(bf16[256,4096]{1,0:T(8,128)(2,1)} %get-tuple-element.35), channel_id=1, source_target_pairs={{0,6},{2,0},{4,2},{6,4},{8,10},{10,12},{12,14},{14,8},{1,7},{3,1},... | collective-permute-start | bytes 6291464 | tf_op jit(solution)/shard_map/weights/ppermute | solution.py:238
  6.9 47.5 %collective-permute-start = (bf16[256,4096]{1,0:T(8,128)(2,1)}, bf16[256,4096]{1,0:T(8,128)(2,1)}, u32[]{:S(2)}, u32[]{:S(2)}) collective-permute-start(bf16[256,4096]{1,0:T(8,128)(2,1)} %get-tuple-element.35), channel_id=1, source_target_pairs={{0,2},{2,4},{4,6},{6,0},{8,14},{10,8},{12,10},{14,12},{1,3},{3,5},... | collective-permute-start | bytes 6291464 | tf_op jit(solution)/shard_map/weights/ppermute | solution.py:238
  6.9 39.3 %all-to-all-start = ((bf16[32,32,512]{2,1,0:T(8,128)(2,1)}), bf16[32,32,512]{2,1,0:T(8,128)(2,1)S(1)}, u32[]{:S(2)}, u32[]{:S(2)}) async-start(bf16[32,32,512]{2,1,0:T(8,128)(2,1)} %get-tuple-element.34), calls=%async_computation | async-start | bytes 2097152 | tf_op jit(solution)/shard_map/all_to_all | solution.py:291
  46.2 1.2 copy-start.2
  47.4 43.0 %copy-start.1 = (bf16[512,4096]{1,0:T(8,128)(2,1)S(1)}, bf16[512,4096]{1,0:T(8,128)(2,1)}, u32[]{:S(2)}) copy-start(bf16[512,4096]{1,0:T(8,128)(2,1)} %weight_ref.1) | copy-start | bytes 12582916
  54.4 29.2 %collective-permute-start.4 = (bf16[256,4096]{1,0:T(8,128)(2,1)S(1)}, bf16[256,4096]{1,0:T(8,128)(2,1)S(1)}, u32[]{:S(2)}, u32[]{:S(2)}) collective-permute-start(bf16[256,4096]{1,0:T(8,128)(2,1)S(1)} %collective-permute-done.1.refs_5_), channel_id=1, source_target_pairs={{0,8},{8,0},{1,9},{9,1},{2,10},{10,2},{3,11},{11,3},{4,12},{12,4},... | collective-permute-start | bytes 6291464 | tf_op jit(solution)/shard_map/weights/ppermute | solution.py:220
  55.4 28.2 %collective-permute-start.3 = (bf16[256,4096]{1,0:T(8,128)(2,1)}, bf16[256,4096]{1,0:T(8,128)(2,1)S(1)}, u32[]{:S(2)}, u32[]{:S(2)}) collective-permute-start(bf16[256,4096]{1,0:T(8,128)(2,1)} %collective-permute-done.refs_3_), channel_id=1, source_target_pairs={{0,8},{8,0},{1,9},{9,1},{2,10},{10,2},{3,11},{11,3},{4,12},{12,4},... | collective-permute-start | bytes 6291464 | tf_op jit(solution)/shard_map/weights/ppermute | solution.py:220
  55.5 28.1 %collective-permute-start.2 = (bf16[256,4096]{1,0:T(8,128)(2,1)}, bf16[256,4096]{1,0:T(8,128)(2,1)S(1)}, u32[]{:S(2)}, u32[]{:S(2)}) collective-permute-start(bf16[256,4096]{1,0:T(8,128)(2,1)} %collective-permute-done.refs_3_), channel_id=1, source_target_pairs={{0,2},{2,4},{4,6},{6,0},{8,14},{10,8},{12,10},{14,12},{1,3},{3,5},... | collective-permute-start | bytes 6291464 | tf_op jit(solution)/shard_map/weights/ppermute | solution.py:238
  83.6 12.8 %collective-permute-start.8 = (bf16[256,4096]{1,0:T(8,128)(2,1)S(1)}, bf16[256,4096]{1,0:T(8,128)(2,1)S(1)}, u32[]{:S(2)}, u32[]{:S(2)}) collective-permute-start(bf16[256,4096]{1,0:T(8,128)(2,1)S(1)} %collective-permute-done.2.refs_7_), channel_id=1, source_target_pairs={{0,8},{8,0},{1,9},{9,1},{2,10},{10,2},{3,11},{11,3},{4,12},{12,4},... | collective-permute-start | bytes 6291464 | tf_op jit(solution)/shard_map/weights/ppermute | solution.py:220
  84.9 1.0 copy-start.3
  86.2 10.2 %collective-permute-start.5 = (bf16[128,512]{1,0:T(8,128)(2,1)S(1)}, bf16[128,512]{1,0:T(8,128)(2,1)S(1)}, u32[]{:S(2)}, u32[]{:S(2)}) collective-permute-start(bf16[128,512]{1,0:T(8,128)(2,1)S(1)} %get-tuple-element.41), channel_id=1, source_target_pairs={{0,2},{2,4},{4,6},{6,0},{8,14},{10,8},{12,10},{14,12},{1,3},{3,5},... | collective-permute-start | bytes 393224 | tf_op jit(solution)/shard_map/quarters/ppermute | solution.py:238
  86.8 9.6 %collective-permute-start.6 = (bf16[128,512]{1,0:T(8,128)(2,1)S(1)}, bf16[128,512]{1,0:T(8,128)(2,1)S(1)}, u32[]{:S(2)}, u32[]{:S(2)}) collective-permute-start(bf16[128,512]{1,0:T(8,128)(2,1)S(1)} %get-tuple-element.42), channel_id=1, source_target_pairs={{0,6},{2,0},{4,2},{6,4},{8,10},{10,12},{12,14},{14,8},{1,7},{3,1},... | collective-permute-start | bytes 393224 | tf_op jit(solution)/shard_map/quarters/ppermute | solution.py:238
  89.5 6.9 %collective-permute-start.7 = (bf16[128,512]{1,0:T(8,128)(2,1)S(1)}, bf16[128,512]{1,0:T(8,128)(2,1)S(1)}, u32[]{:S(2)}, u32[]{:S(2)}) collective-permute-start(bf16[128,512]{1,0:T(8,128)(2,1)S(1)} %get-tuple-element.43), channel_id=1, source_target_pairs={{0,4},{2,6},{4,0},{6,2},{1,5},{3,7},{5,1},{7,3},{8,12},{10,14},{12... | collective-permute-start | bytes 393224 | tf_op jit(solution)/shard_map/quarters/ppermute | solution.py:228
  99.0 9.5 %collective-permute-start.13 = (bf16[64,2048]{1,0:T(8,128)(2,1)S(1)}, bf16[64,2048]{1,0:T(8,128)(2,1)S(1)}, u32[]{:S(2)}, u32[]{:S(2)}) collective-permute-start(bf16[64,2048]{1,0:T(8,128)(2,1)S(1)} %get-tuple-element.53), channel_id=1, source_target_pairs={{0,1},{1,0},{2,3},{3,2},{4,5},{5,4},{6,7},{7,6},{8,9},{9,8},{10,11... | collective-permute-start | bytes 786440 | tf_op jit(solution)/shard_map/gather/ppermute | solution.py:220
  103.4 10.7 %collective-permute-start.9 = (bf16[64,2048]{1,0:T(8,128)(2,1)S(1)}, bf16[64,2048]{1,0:T(8,128)(2,1)S(1)}, u32[]{:S(2)}, u32[]{:S(2)}) collective-permute-start(bf16[64,2048]{1,0:T(8,128)(2,1)S(1)} %get-tuple-element.48), channel_id=1, source_target_pairs={{0,1},{1,0},{2,3},{3,2},{4,5},{5,4},{6,7},{7,6},{8,9},{9,8},{10,11... | collective-permute-start | bytes 786440 | tf_op jit(solution)/shard_map/gather/ppermute | solution.py:220
  108.5 7.7 %collective-permute-start.16 = (bf16[64,2048]{1,0:T(8,128)(2,1)S(1)}, bf16[64,2048]{1,0:T(8,128)(2,1)S(1)}, u32[]{:S(2)}, u32[]{:S(2)}) collective-permute-start(bf16[64,2048]{1,0:T(8,128)(2,1)S(1)} %add_convert_fusion.refs_4_), channel_id=1, source_target_pairs={{0,6},{2,0},{4,2},{6,4},{1,7},{3,1},{5,3},{7,5},{8,14},{10,8},{12,... | collective-permute-start | bytes 786440 | tf_op jit(solution)/shard_map/gather/ppermute | solution.py:228
  109.8 9.0 %collective-permute-start.15 = (bf16[64,2048]{1,0:T(8,128)(2,1)S(1)}, bf16[64,2048]{1,0:T(8,128)(2,1)S(1)}, u32[]{:S(2)}, u32[]{:S(2)}) collective-permute-start(bf16[64,2048]{1,0:T(8,128)(2,1)S(1)} %add_convert_fusion.refs_4_), channel_id=1, source_target_pairs={{0,2},{2,4},{4,6},{6,0},{1,3},{3,5},{5,7},{7,1},{8,10},{10,12},{12... | collective-permute-start | bytes 786440 | tf_op jit(solution)/shard_map/gather/ppermute | solution.py:228
  110.6 9.2 %collective-permute-start.14 = (bf16[64,2048]{1,0:T(8,128)(2,1)S(1)}, bf16[64,2048]{1,0:T(8,128)(2,1)S(1)}, u32[]{:S(2)}, u32[]{:S(2)}) collective-permute-start(bf16[64,2048]{1,0:T(8,128)(2,1)S(1)} %add_convert_fusion.refs_4_), channel_id=1, source_target_pairs={{0,1},{1,0},{2,3},{3,2},{4,5},{5,4},{6,7},{7,6},{8,9},{9,8},{10,11... | collective-permute-start | bytes 786440 | tf_op jit(solution)/shard_map/gather/ppermute | solution.py:220
  114.2 9.0 %collective-permute-start.12 = (bf16[64,2048]{1,0:T(8,128)(2,1)S(1)}, bf16[64,2048]{1,0:T(8,128)(2,1)S(1)}, u32[]{:S(2)}, u32[]{:S(2)}) collective-permute-start(bf16[64,2048]{1,0:T(8,128)(2,1)S(1)} %add_convert_fusion.1.refs_0_), channel_id=1, source_target_pairs={{0,6},{2,0},{4,2},{6,4},{1,7},{3,1},{5,3},{7,5},{8,14},{10,8},{12,... | collective-permute-start | bytes 786440 | tf_op jit(solution)/shard_map/gather/ppermute | solution.py:228
  115.5 9.8 %collective-permute-start.11 = (bf16[64,2048]{1,0:T(8,128)(2,1)S(1)}, bf16[64,2048]{1,0:T(8,128)(2,1)S(1)}, u32[]{:S(2)}, u32[]{:S(2)}) collective-permute-start(bf16[64,2048]{1,0:T(8,128)(2,1)S(1)} %add_convert_fusion.1.refs_0_), channel_id=1, source_target_pairs={{0,2},{2,4},{4,6},{6,0},{1,3},{3,5},{5,7},{7,1},{8,10},{10,12},{12... | collective-permute-start | bytes 786440 | tf_op jit(solution)/shard_map/gather/ppermute | solution.py:228
  116.3 9.2 %collective-permute-start.10 = (bf16[64,2048]{1,0:T(8,128)(2,1)S(1)}, bf16[64,2048]{1,0:T(8,128)(2,1)S(1)}, u32[]{:S(2)}, u32[]{:S(2)}) collective-permute-start(bf16[64,2048]{1,0:T(8,128)(2,1)S(1)} %add_convert_fusion.1.refs_0_), channel_id=1, source_target_pairs={{0,1},{1,0},{2,3},{3,2},{4,5},{5,4},{6,7},{7,6},{8,9},{9,8},{10,11... | collective-permute-start | bytes 786440 | tf_op jit(solution)/shard_map/gather/ppermute | solution.py:220
  119.9 10.8 %collective-permute-start.24 = (bf16[64,2048]{1,0:T(8,128)(2,1)S(1)}, bf16[64,2048]{1,0:T(8,128)(2,1)S(1)}, u32[]{:S(2)}, u32[]{:S(2)}) collective-permute-start(bf16[64,2048]{1,0:T(8,128)(2,1)S(1)} %collective-permute-done.14.refs_5_), channel_id=1, source_target_pairs={{0,2},{2,4},{4,6},{6,0},{1,3},{3,5},{5,7},{7,1},{8,10},{10,12},{12... | collective-permute-start | bytes 786440 | tf_op jit(solution)/shard_map/gather/ppermute | solution.py:228
  119.9 13.4 %collective-permute-start.23 = (bf16[64,2048]{1,0:T(8,128)(2,1)S(1)}, bf16[64,2048]{1,0:T(8,128)(2,1)S(1)}, u32[]{:S(2)}, u32[]{:S(2)}) collective-permute-start(bf16[64,2048]{1,0:T(8,128)(2,1)S(1)} %collective-permute-done.16.refs_7_), channel_id=1, source_target_pairs={{0,6},{2,0},{4,2},{6,4},{1,7},{3,1},{5,3},{7,5},{8,14},{10,8},{12,... | collective-permute-start | bytes 786440 | tf_op jit(solution)/shard_map/gather/ppermute | solution.py:228
  123.1 10.2 %collective-permute-start.22 = (bf16[64,2048]{1,0:T(8,128)(2,1)S(1)}, bf16[64,2048]{1,0:T(8,128)(2,1)S(1)}, u32[]{:S(2)}, u32[]{:S(2)}) collective-permute-start(bf16[64,2048]{1,0:T(8,128)(2,1)S(1)} %collective-permute-done.16.refs_7_), channel_id=1, source_target_pairs={{0,1},{1,0},{2,3},{3,2},{4,5},{5,4},{6,7},{7,6},{8,9},{9,8},{10,11... | collective-permute-start | bytes 786440 | tf_op jit(solution)/shard_map/gather/ppermute | solution.py:220
  125.5 11.2 %collective-permute-start.19 = (bf16[64,2048]{1,0:T(8,128)(2,1)S(1)}, bf16[64,2048]{1,0:T(8,128)(2,1)S(1)}, u32[]{:S(2)}, u32[]{:S(2)}) collective-permute-start(bf16[64,2048]{1,0:T(8,128)(2,1)S(1)} %collective-permute-done.10.refs_1_), channel_id=1, source_target_pairs={{0,2},{2,4},{4,6},{6,0},{1,3},{3,5},{5,7},{7,1},{8,10},{10,12},{12... | collective-permute-start | bytes 786440 | tf_op jit(solution)/shard_map/gather/ppermute | solution.py:228
  125.5 11.2 %collective-permute-start.18 = (bf16[64,2048]{1,0:T(8,128)(2,1)S(1)}, bf16[64,2048]{1,0:T(8,128)(2,1)S(1)}, u32[]{:S(2)}, u32[]{:S(2)}) collective-permute-start(bf16[64,2048]{1,0:T(8,128)(2,1)S(1)} %collective-permute-done.12.refs_3_), channel_id=1, source_target_pairs={{0,6},{2,0},{4,2},{6,4},{1,7},{3,1},{5,3},{7,5},{8,14},{10,8},{12,... | collective-permute-start | bytes 786440 | tf_op jit(solution)/shard_map/gather/ppermute | solution.py:228
  130.7 7.0 %collective-permute-start.17 = (bf16[64,2048]{1,0:T(8,128)(2,1)S(1)}, bf16[64,2048]{1,0:T(8,128)(2,1)S(1)}, u32[]{:S(2)}, u32[]{:S(2)}) collective-permute-start(bf16[64,2048]{1,0:T(8,128)(2,1)S(1)} %collective-permute-done.12.refs_3_), channel_id=1, source_target_pairs={{0,1},{1,0},{2,3},{3,2},{4,5},{5,4},{6,7},{7,6},{8,9},{9,8},{10,11... | collective-permute-start | bytes 786440 | tf_op jit(solution)/shard_map/gather/ppermute | solution.py:220
  133.3 9.0 %collective-permute-start.25 = (bf16[64,1024]{1,0:T(8,128)(2,1)S(1)}, bf16[64,1024]{1,0:T(8,128)(2,1)S(1)}, u32[]{:S(2)}, u32[]{:S(2)}) collective-permute-start(bf16[64,1024]{1,0:T(8,128)(2,1)S(1)} %slice.14), channel_id=1, source_target_pairs={{0,2},{2,4},{4,6},{6,0},{1,3},{3,5},{5,7},{7,1},{8,10},{10,12},{12... | collective-permute-start | bytes 393224 | tf_op jit(solution)/shard_map/gather/ppermute | solution.py:228
  133.4 9.0 %collective-permute-start.26 = (bf16[64,1024]{1,0:T(8,128)(2,1)S(1)}, bf16[64,1024]{1,0:T(8,128)(2,1)S(1)}, u32[]{:S(2)}, u32[]{:S(2)}) collective-permute-start(bf16[64,1024]{1,0:T(8,128)(2,1)S(1)} %slice.15), channel_id=1, source_target_pairs={{0,6},{2,0},{4,2},{6,4},{1,7},{3,1},{5,3},{7,5},{8,14},{10,8},{12,... | collective-permute-start | bytes 393224 | tf_op jit(solution)/shard_map/gather/ppermute | solution.py:228
  137.7 6.3 %collective-permute-start.20 = (bf16[64,1024]{1,0:T(8,128)(2,1)S(1)}, bf16[64,1024]{1,0:T(8,128)(2,1)S(1)}, u32[]{:S(2)}, u32[]{:S(2)}) collective-permute-start(bf16[64,1024]{1,0:T(8,128)(2,1)S(1)} %slice.12), channel_id=1, source_target_pairs={{0,2},{2,4},{4,6},{6,0},{1,3},{3,5},{5,7},{7,1},{8,10},{10,12},{12... | collective-permute-start | bytes 393224 | tf_op jit(solution)/shard_map/gather/ppermute | solution.py:228
  137.8 6.2 %collective-permute-start.21 = (bf16[64,1024]{1,0:T(8,128)(2,1)S(1)}, bf16[64,1024]{1,0:T(8,128)(2,1)S(1)}, u32[]{:S(2)}, u32[]{:S(2)}) collective-permute-start(bf16[64,1024]{1,0:T(8,128)(2,1)S(1)} %slice.13), channel_id=1, source_target_pairs={{0,6},{2,0},{4,2},{6,4},{1,7},{3,1},{5,3},{7,5},{8,14},{10,8},{12,... | collective-permute-start | bytes 393224 | tf_op jit(solution)/shard_map/gather/ppermute | solution.py:228

commit v6 on v5

--- a/solution.py
+++ b/solution.py
@@ -12,6 +12,7 @@
 
 MIB = 1024 * 1024
 GROUP = 4
+PIECES = 4
 STREAMS = 2
 WIDTH = 512
 
@@ -24,99 +25,93 @@
 
 
 def pack_kernel(
-    key_hbm, value_hbm, filter_hbm, weight_hbm, out_ref, half_ref, key_ref, value_ref, filter_ref, sems
+    key_hbm, value_hbm, filter_hbm, weight_hbm, out_hbm, half_hbm,
+    key_ref, value_ref, filter_ref, half_ref, out_ref, sems,
 ):
-    parts, both, rows = out_ref.shape
-    share, half = both // 2, half_ref.shape[0]
+    parts, both, rows = out_hbm.shape
+    share, half = both // 2, half_hbm.shape[0]
     start = pl.multiple_of(lax.axis_index("core") * half, half)
-    moves = (
-        (key_hbm, key_ref),
-        (value_hbm, value_ref),
-        (filter_hbm, filter_ref),
-        (weight_hbm.at[pl.ds(start, half)], half_ref),
-    )
-    copies = [pltpu.make_async_copy(*move, sems.at[i]) for i, move in enumerate(moves)]
-    for copy in copies:
+    piece = half // PIECES
+    moves = [(key_hbm, key_ref), (value_hbm, value_ref), (filter_hbm, filter_ref)]
+    for i in range(PIECES):
+        here = pl.ds(i * piece, piece)
+        moves.append((weight_hbm.at[pl.ds(start + i * piece, piece)], half_ref.at[here]))
+    arriving = [pltpu.make_async_copy(*move, sems.at[i]) for i, move in enumerate(moves)]
+    leaving = []
+
+    def send(source, target):
+        leaving.append(pltpu.make_async_copy(source, target, sems.at[len(moves) + len(leaving)]))
+        leaving[-1].start()
+
+    for copy in arriving:
         copy.start()
-    copies[0].wait()
-    copies[1].wait()
+    arriving[0].wait()
+    arriving[1].wait()
     mixer = key_ref[...].astype(jnp.float32) * value_ref[...].astype(jnp.float32)
     out_ref[:, :share, :] = mixer.astype(jnp.bfloat16).T.reshape(parts, share, rows)
-    copies[2].wait()
+    send(out_ref.at[:, pl.ds(0, share)], out_hbm.at[:, pl.ds(0, share)])
+    arriving[2].wait()
     out_ref[:, share:, :] = filter_ref[...].T.reshape(parts, share, rows)
-    copies[3].wait()
-
-
-def conv_kernel(
-    signal_ref, gain_ref, table_ref, out_ref, mixer_spec, filter_spec, product
-):
+    send(out_ref.at[:, pl.ds(share, share)], out_hbm.at[:, pl.ds(share, share)])
+    for i in range(PIECES):
+        arriving[3 + i].wait()
+        here = pl.ds(i * piece, piece)
+        send(half_ref.at[here], half_hbm.at[here])
+    for copy in leaving:
+        copy.wait()
+
+
+def conv_kernel(signal_ref, gain_ref, table_ref, out_ref, mixer_spec, filter_spec, product):
     blocks, both, rows = signal_ref.shape
     share = both // 2
     table = table_ref[...]
-
-    def spectrum(signal):
-        flat = signal.reshape(blocks * share, rows)
-        value = jnp.dot(flat, table, preferred_element_type=jnp.float32)
-        return value.reshape(blocks, share, 2 * rows)
-
-    mixer_spec[...] = spectrum(signal_ref[:, :share, :])
-    filter_spec[...] = spectrum(signal_ref[:, share:, :])
-
     lane = lax.broadcasted_iota(jnp.int32, (8, 128), 1)
     sign = jnp.where(lane % 2 == 0, 1.0, -1.0).astype(jnp.float32)
-    lane_tiles = rows // 128
-
-    def tile(step, carry):
-        row = pl.multiple_of((step // lane_tiles) * 8, 8)
-        real = pl.multiple_of((step % lane_tiles) * 128, 128)
-        imag = pl.multiple_of(rows + (step % lane_tiles) * 128, 128)
-
-        def load(ref, block):
-            return (
-                ref[block, pl.ds(row, 8), pl.ds(real, 128)],
-                ref[block, pl.ds(row, 8), pl.ds(imag, 128)],
-            )
-
-        def window(block):
-            now_real, now_imag = load(mixer_spec, block)
-            if block > 0:
+    for part, spec in enumerate((mixer_spec, filter_spec)):
+        flat = signal_ref[:, part * share : (part + 1) * share, :].reshape(blocks * share, rows)
+        value = jnp.dot(flat, table, preferred_element_type=jnp.float32)
+        spec[...] = value.reshape(blocks, share, 2 * rows)
+
+    for column in range(0, rows, 128):
+        real, imag = slice(column, column + 128), slice(rows + column, rows + column + 128)
+        for row in range(0, share, 8):
+            here = slice(row, row + 8)
+
+            def load(ref, block):
+                return ref[block, here, real], ref[block, here, imag]
+
+            for block in reversed(range(1, blocks)):
+                now_real, now_imag = load(mixer_spec, block)
                 last_real, last_imag = load(mixer_spec, block - 1)
-                now_real, now_imag = now_real - sign * last_imag, now_imag + sign * last_real
-            return now_real, now_imag
-
-        for block in reversed(range(blocks)):
-            now_real, now_imag = window(block)
-            mixer_spec[block, pl.ds(row, 8), pl.ds(real, 128)] = now_real
-            mixer_spec[block, pl.ds(row, 8), pl.ds(imag, 128)] = now_imag
-
-        for first in range(0, blocks, GROUP):
-            sums = [[None] * 3 for _ in range(GROUP)]
-            held = {}
-            for lag in range(first + GROUP):
-                filter_real, filter_imag = load(filter_spec, lag)
-                filter_both = filter_real + filter_imag
+                mixer_spec[block, here, real] = now_real - sign * last_imag
+                mixer_spec[block, here, imag] = now_imag + sign * last_real
+
+            for first in range(0, blocks, GROUP):
+                sums = [[None] * 3 for _ in range(GROUP)]
+                held = {}
+                for lag in range(first + GROUP):
+                    filter_real, filter_imag = load(filter_spec, lag)
+                    filter_both = filter_real + filter_imag
+                    for i in range(GROUP):
+                        block = first + i - lag
+                        if block < 0:
+                            continue
+                        if block not in held:
+                            real_part, imag_part = load(mixer_spec, block)
+                            held[block] = (real_part, imag_part, real_part + imag_part)
+                        terms = (
+                            filter_real * held[block][0],
+                            filter_imag * held[block][1],
+                            filter_both * held[block][2],
+                        )
+                        for s in range(3):
+                            sums[i][s] = terms[s] if sums[i][s] is None else sums[i][s] + terms[s]
+                    held.pop(first + GROUP - 1 - lag, None)
                 for i in range(GROUP):
-                    block = first + i - lag
-                    if block < 0:
-                        continue
-                    if block not in held:
-                        real_part, imag_part = load(mixer_spec, block)
-                        held[block] = (real_part, imag_part, real_part + imag_part)
-                    terms = (
-                        filter_real * held[block][0],
-                        filter_imag * held[block][1],
-                        filter_both * held[block][2],
-                    )
-                    for s in range(3):
-                        sums[i][s] = terms[s] if sums[i][s] is None else sums[i][s] + terms[s]
-                held.pop(first + GROUP - 1 - lag, None)
-            for i in range(GROUP):
-                one, two, three = sums[i]
-                product[first + i, pl.ds(row, 8), pl.ds(real, 128)] = one - two
-                product[first + i, pl.ds(row, 8), pl.ds(imag, 128)] = three - one - two
-        return carry
-
-    lax.fori_loop(0, (share // 8) * lane_tiles, tile, 0)
+                    one, two, three = sums[i]
+                    product[first + i, here, real] = one - two
+                    product[first + i, here, imag] = three - one - two
+
     flat = product[...].astype(jnp.bfloat16).reshape(blocks * share, 2 * rows)
     conv = lax.dot_general(
         flat, table, (((1,), (1,)), ((), ())), preferred_element_type=jnp.float32
@@ -282,8 +277,15 @@
             pack_kernel,
             [((ctx_count, 2 * share, rows), half16), ((channels // 2, features), half16)],
             [HBM] * 4,
-            [VMEM] * 2,
-            [square, square, square, pltpu.SemaphoreType.DMA((4,))],
+            [HBM] * 2,
+            [
+                square,
+                square,
+                square,
+                pltpu.VMEM((channels // 2, features), half16),
+                pltpu.VMEM((ctx_count, 2 * share, rows), half16),
+                pltpu.SemaphoreType.DMA((5 + 2 * PIECES,)),
+            ],
             limit=60,
         )(key_branch, value_branch, filters, out_weight)
     with jax.named_scope("weights"):

time: 148 us -> 147 us (level)
  Pallas kernels: 19.7 us -> 17.9 us
  transfers between devices with their start and end apart: 28 -> 28, of which waited for: 10 -> 10; matrix products, arithmetic and copies ran while one was open for 0% -> 0% of each run, Pallas kernels for 8% -> 7%
where the time goes in v6:
time: 147 us; the launch traced here: 145 us
  starting transfers between devices  49.7 us (34%)
  waiting for transfers between devices  45.5 us (31%)
  blocking collectives  28.7 us (20%)
  Pallas kernels  17.9 us (12%)
  local copies, waits for them, and re-layouts  2.48 us (2%)
    all_to_all x1, blocking collectives, body(): lax.all_to_all(total, ('block', 'core'), split_axis=0, concat_axis=0, til...  28.7 us
    all_to_all x1, waiting for transfers between devices, body(): lax.all_to_all(outgoing, ('block', 'core'), split_axis=0, concat_axis=0,...  27.5 us
    ppermute x13, starting transfers between devices, along_y(): lax.ppermute(value, 'y', [(i, (i + steps) % count) for i in range(count)])  18.2 us
    ppermute x9, starting transfers between devices, swap(): return lambda value: lax.ppermute(value, axis, [(0, 1), (1, 0)])  12.8 us
    all_to_all x1, starting transfers between devices, body(): lax.all_to_all(outgoing, ('block', 'core'), split_axis=0, concat_axis=0,...  11.6 us
    ppermute x9, waiting for transfers between devices, swap(): return lambda value: lax.ppermute(value, axis, [(0, 1), (1, 0)])  8.61 us
    ppermute x5, starting transfers between devices, mirrored(): return lax.ppermute(value, ('core', 'y'), pairs)  6.99 us
    pallas_call x1, Pallas kernels, body(): whole(conv_kernel, [((ctx_count, share, rows), half16)], [VMEM] * 3, [VME...  5.71 us
  transfers between devices with their start and end apart: 28, of which 10 were waited for; matrix products, arithmetic and copies ran while one was open for 0% of the time, Pallas kernels for 7%

profile of v6, /device:TPU:2, one launch (start us, length us, event | category | flops | bytes accessed | tf_op | source)
XLA Modules:
  0.0 144.7 jit_solution(15074331837820597462)
XLA Ops:
  0.0 3.2 %pack.1 = (bf16[32,32,512]{2,1,0:T(8,128)(2,1)}, bf16[256,4096]{1,0:T(8,128)(2,1)}) custom-call(bf16[512,512]{1,0:T(8,128)(2,1)} %key_hbm.1, bf16[512,512]{1,0:T(8,128)(2,1)} %value_hbm.1, bf16[512,512]{1,0:T(8,128)(2,1)} %filter_hbm.1, bf16[512,4096]{1,0:T(8,128)(2,1)} %weight_ref.1), custom_call_target="tpu_custom_call" | custom-call | bytes 8388608 | tf_op jit(solution)/shard_map/pack/pallas_call | solution.py:276
  3.2 3.1 %collective-permute-start.1 = (bf16[256,4096]{1,0:T(8,128)(2,1)}, bf16[256,4096]{1,0:T(8,128)(2,1)S(1)}, u32[]{:S(2)}, u32[]{:S(2)}) collective-permute-start(bf16[256,4096]{1,0:T(8,128)(2,1)} %get-tuple-element.35), channel_id=1, source_target_pairs={{0,6},{2,0},{4,2},{6,4},{8,10},{10,12},{12,14},{14,8},{1,7},{3,1},... | collective-permute-start | bytes 6291464 | tf_op jit(solution)/shard_map/weights/ppermute | solution.py:233
  6.3 11.6 %all-to-all-start = ((bf16[32,32,512]{2,1,0:T(8,128)(2,1)}), bf16[32,32,512]{2,1,0:T(8,128)(2,1)S(1)}, u32[]{:S(2)}, u32[]{:S(2)}) async-start(bf16[32,32,512]{2,1,0:T(8,128)(2,1)} %get-tuple-element.34), calls=%async_computation | async-start | bytes 2097152 | tf_op jit(solution)/shard_map/all_to_all | solution.py:293
  18.1 27.5 %all-to-all-done.signal_ref = bf16[32,32,512]{2,1,0:T(8,128)(2,1)S(1)} async-done(((bf16[32,32,512]{2,1,0:T(8,128)(2,1)}), bf16[32,32,512]{2,1,0:T(8,128)(2,1)S(1)}, u32[]{:S(2)}, u32[]{:S(2)}) %all-to-all-start) | async-done | bytes 1048608 | tf_op jit(solution)/shard_map/all_to_all | solution.py:293
  45.6 1.2 copy-done.2
  46.8 5.7 %conv.1 = bf16[32,16,512]{2,1,0:T(8,128)(2,1)S(1)} custom-call(bf16[32,32,512]{2,1,0:T(8,128)(2,1)S(1)} %all-to-all-done.signal_ref, f32[16,1]{1,0:T(8,128)S(1)} %copy.9.gain_ref, bf16[512,1024]{1,0:T(8,128)(2,1)S(1)} %copy-done.2), custom_call_target="tpu_custom_call" | custom-call | bytes 8388608 | tf_op jit(solution)/shard_map/conv/pallas_call | solution.py:296
  52.6 1.0 collective-permute-start.4
  54.2 28.7 %all_to_all.10.total_ref = bf16[32,16,512]{2,1,0:T(8,128)(2,1)S(1)} all-to-all(bf16[32,16,512]{2,1,0:T(8,128)(2,1)S(1)} %conv.1), channel_id=1, replica_groups=mesh['block'=16,'core'=2,'y'=4,'z'=2] {'block','core'}, dimensions={0} | all-to-all | bytes 1048576 | tf_op jit(solution)/shard_map/all_to_all | solution.py:308
  83.0 1.3 collective-permute-start.8
  84.3 1.0 copy-done.3
  86.2 2.7 %collective-permute-start.6 = (bf16[128,512]{1,0:T(8,128)(2,1)S(1)}, bf16[128,512]{1,0:T(8,128)(2,1)S(1)}, u32[]{:S(2)}, u32[]{:S(2)}) collective-permute-start(bf16[128,512]{1,0:T(8,128)(2,1)S(1)} %get-tuple-element.42), channel_id=1, source_target_pairs={{0,6},{2,0},{4,2},{6,4},{8,10},{10,12},{12,14},{14,8},{1,7},{3,1},... | collective-permute-start | bytes 393224 | tf_op jit(solution)/shard_map/quarters/ppermute | solution.py:233
  90.5 5.2 %collective-permute-done.5.refs_0_ = bf16[128,512]{1,0:T(8,128)(2,1)S(1)} collective-permute-done((bf16[128,512]{1,0:T(8,128)(2,1)S(1)}, bf16[128,512]{1,0:T(8,128)(2,1)S(1)}, u32[]{:S(2)}, u32[]{:S(2)}) %collective-permute-start.5) | collective-permute-done | bytes 131104 | tf_op jit(solution)/shard_map/quarters/ppermute | solution.py:233
  95.8 2.6 %rest.3 = (bf16[64,2048]{1,0:T(8,128)(2,1)S(1)}, bf16[64,2048]{1,0:T(8,128)(2,1)S(1)}) custom-call(f32[128,4096]{1,0:T(8,128)S(1)} %own.1.partial_ref, bf16[128,512]{1,0:T(8,128)(2,1)S(1)} %collective-permute-done.5.refs_0_, bf16[128,512]{1,0:T(8,128)(2,1)S(1)} %collective-permute-done.6.refs_1_, bf16[128,512]{1,0:T(8,128)(2,1)S(1)} %collective-permute-done.7.refs_2_, ...), custom_call_target="tpu_custom_call" | custom-call | flops 536870912 | bytes 8388608 | tf_op jit(solution)/shard_map/rest/pallas_call | solution.py:326
  98.4 1.6 %collective-permute-start.13 = (bf16[64,2048]{1,0:T(8,128)(2,1)S(1)}, bf16[64,2048]{1,0:T(8,128)(2,1)S(1)}, u32[]{:S(2)}, u32[]{:S(2)}) collective-permute-start(bf16[64,2048]{1,0:T(8,128)(2,1)S(1)} %get-tuple-element.53), channel_id=1, source_target_pairs={{0,1},{1,0},{2,3},{3,2},{4,5},{5,4},{6,7},{7,6},{8,9},{9,8},{10,11... | collective-permute-start | bytes 786440 | tf_op jit(solution)/shard_map/gather/ppermute | solution.py:215
  100.0 2.6 %rest.2 = (bf16[64,2048]{1,0:T(8,128)(2,1)S(1)}, bf16[64,2048]{1,0:T(8,128)(2,1)S(1)}) custom-call(f32[128,4096]{1,0:T(8,128)S(1)} %own.1.partial_ref, bf16[128,512]{1,0:T(8,128)(2,1)S(1)} %collective-permute-done.5.refs_0_, bf16[128,512]{1,0:T(8,128)(2,1)S(1)} %collective-permute-done.6.refs_1_, bf16[128,512]{1,0:T(8,128)(2,1)S(1)} %collective-permute-done.7.refs_2_, ...), custom_call_target="tpu_custom_call" | custom-call | flops 536870912 | bytes 8388608 | tf_op jit(solution)/shard_map/rest/pallas_call | solution.py:326
  103.2 4.5 %collective-permute-done.13 = bf16[64,2048]{1,0:T(8,128)(2,1)S(1)} collective-permute-done((bf16[64,2048]{1,0:T(8,128)(2,1)S(1)}, bf16[64,2048]{1,0:T(8,128)(2,1)S(1)}, u32[]{:S(2)}, u32[]{:S(2)}) %collective-permute-start.13) | collective-permute-done | bytes 262176 | tf_op jit(solution)/shard_map/gather/ppermute | solution.py:215
  107.8 1.3 collective-permute-start.16
  109.9 1.5 %collective-permute-start.14 = (bf16[64,2048]{1,0:T(8,128)(2,1)S(1)}, bf16[64,2048]{1,0:T(8,128)(2,1)S(1)}, u32[]{:S(2)}, u32[]{:S(2)}) collective-permute-start(bf16[64,2048]{1,0:T(8,128)(2,1)S(1)} %add_convert_fusion.refs_4_), channel_id=1, source_target_pairs={{0,1},{1,0},{2,3},{3,2},{4,5},{5,4},{6,7},{7,6},{8,9},{9,8},{10,11... | collective-permute-start | bytes 786440 | tf_op jit(solution)/shard_map/gather/ppermute | solution.py:215
  111.4 1.9 %collective-permute-done.9 = bf16[64,2048]{1,0:T(8,128)(2,1)S(1)} collective-permute-done((bf16[64,2048]{1,0:T(8,128)(2,1)S(1)}, bf16[64,2048]{1,0:T(8,128)(2,1)S(1)}, u32[]{:S(2)}, u32[]{:S(2)}) %collective-permute-start.9) | collective-permute-done | bytes 262176 | tf_op jit(solution)/shard_map/gather/ppermute | solution.py:215
  113.4 1.4 collective-permute-start.12
  115.5 1.9 %collective-permute-start.10 = (bf16[64,2048]{1,0:T(8,128)(2,1)S(1)}, bf16[64,2048]{1,0:T(8,128)(2,1)S(1)}, u32[]{:S(2)}, u32[]{:S(2)}) collective-permute-start(bf16[64,2048]{1,0:T(8,128)(2,1)S(1)} %add_convert_fusion.1.refs_0_), channel_id=1, source_target_pairs={{0,1},{1,0},{2,3},{3,2},{4,5},{5,4},{6,7},{7,6},{8,9},{9,8},{10,11... | collective-permute-start | bytes 786440 | tf_op jit(solution)/shard_map/gather/ppermute | solution.py:215
  118.1 1.0 collective-permute-done.14.refs_5_
  119.1 3.2 %collective-permute-start.23 = (bf16[64,2048]{1,0:T(8,128)(2,1)S(1)}, bf16[64,2048]{1,0:T(8,128)(2,1)S(1)}, u32[]{:S(2)}, u32[]{:S(2)}) collective-permute-start(bf16[64,2048]{1,0:T(8,128)(2,1)S(1)} %collective-permute-done.16.refs_7_), channel_id=1, source_target_pairs={{0,6},{2,0},{4,2},{6,4},{1,7},{3,1},{5,3},{7,5},{8,14},{10,8},{12,... | collective-permute-start | bytes 786440 | tf_op jit(solution)/shard_map/gather/ppermute | solution.py:223
  122.3 2.2 %collective-permute-start.22 = (bf16[64,2048]{1,0:T(8,128)(2,1)S(1)}, bf16[64,2048]{1,0:T(8,128)(2,1)S(1)}, u32[]{:S(2)}, u32[]{:S(2)}) collective-permute-start(bf16[64,2048]{1,0:T(8,128)(2,1)S(1)} %collective-permute-done.16.refs_7_), channel_id=1, source_target_pairs={{0,1},{1,0},{2,3},{3,2},{4,5},{5,4},{6,7},{7,6},{8,9},{9,8},{10,11... | collective-permute-start | bytes 786440 | tf_op jit(solution)/shard_map/gather/ppermute | solution.py:215
  124.7 3.2 %collective-permute-start.18 = (bf16[64,2048]{1,0:T(8,128)(2,1)S(1)}, bf16[64,2048]{1,0:T(8,128)(2,1)S(1)}, u32[]{:S(2)}, u32[]{:S(2)}) collective-permute-start(bf16[64,2048]{1,0:T(8,128)(2,1)S(1)} %collective-permute-done.12.refs_3_), channel_id=1, source_target_pairs={{0,6},{2,0},{4,2},{6,4},{1,7},{3,1},{5,3},{7,5},{8,14},{10,8},{12,... | collective-permute-start | bytes 786440 | tf_op jit(solution)/shard_map/gather/ppermute | solution.py:223
  128.0 1.9 %collective-permute-done.24.refs_8_ = bf16[64,2048]{1,0:T(8,128)(2,1)S(1)} collective-permute-done((bf16[64,2048]{1,0:T(8,128)(2,1)S(1)}, bf16[64,2048]{1,0:T(8,128)(2,1)S(1)}, u32[]{:S(2)}, u32[]{:S(2)}) %collective-permute-start.24) | collective-permute-done | bytes 262176 | tf_op jit(solution)/shard_map/gather/ppermute | solution.py:223
  129.9 2.6 %collective-permute-start.17 = (bf16[64,2048]{1,0:T(8,128)(2,1)S(1)}, bf16[64,2048]{1,0:T(8,128)(2,1)S(1)}, u32[]{:S(2)}, u32[]{:S(2)}) collective-permute-start(bf16[64,2048]{1,0:T(8,128)(2,1)S(1)} %collective-permute-done.12.refs_3_), channel_id=1, source_target_pairs={{0,1},{1,0},{2,3},{3,2},{4,5},{5,4},{6,7},{7,6},{8,9},{9,8},{10,11... | collective-permute-start | bytes 786440 | tf_op jit(solution)/shard_map/gather/ppermute | solution.py:215
  132.6 3.2 %collective-permute-start.26 = (bf16[64,1024]{1,0:T(8,128)(2,1)S(1)}, bf16[64,1024]{1,0:T(8,128)(2,1)S(1)}, u32[]{:S(2)}, u32[]{:S(2)}) collective-permute-start(bf16[64,1024]{1,0:T(8,128)(2,1)S(1)} %slice.15), channel_id=1, source_target_pairs={{0,6},{2,0},{4,2},{6,4},{1,7},{3,1},{5,3},{7,5},{8,14},{10,8},{12,... | collective-permute-start | bytes 393224 | tf_op jit(solution)/shard_map/gather/ppermute | solution.py:223
  137.0 3.2 %collective-permute-start.21 = (bf16[64,1024]{1,0:T(8,128)(2,1)S(1)}, bf16[64,1024]{1,0:T(8,128)(2,1)S(1)}, u32[]{:S(2)}, u32[]{:S(2)}) collective-permute-start(bf16[64,1024]{1,0:T(8,128)(2,1)S(1)} %slice.13), channel_id=1, source_target_pairs={{0,6},{2,0},{4,2},{6,4},{1,7},{3,1},{5,3},{7,5},{8,14},{10,8},{12,... | collective-permute-start | bytes 393224 | tf_op jit(solution)/shard_map/gather/ppermute | solution.py:223
  140.2 1.4 gather.2.refs_0_
  141.6 1.5 %collective-permute-done.20.refs_4_ = bf16[64,1024]{1,0:T(8,128)(2,1)S(1)} collective-permute-done((bf16[64,1024]{1,0:T(8,128)(2,1)S(1)}, bf16[64,1024]{1,0:T(8,128)(2,1)S(1)}, u32[]{:S(2)}, u32[]{:S(2)}) %collective-permute-start.20) | collective-permute-done | bytes 131104 | tf_op jit(solution)/shard_map/gather/ppermute | solution.py:223
  143.2 1.4 gather.3
  (49 shorter events, 7.7 us)
Async XLA Ops:
  0.0 17.9 %copy-start = (f32[512]{0:T(512)S(1)}, f32[512]{0:T(512)}, u32[]{:S(2)}) copy-start(f32[512]{0:T(512)} %param.11) | copy-start | bytes 6148
  3.2 49.3 %collective-permute-start.1 = (bf16[256,4096]{1,0:T(8,128)(2,1)}, bf16[256,4096]{1,0:T(8,128)(2,1)S(1)}, u32[]{:S(2)}, u32[]{:S(2)}) collective-permute-start(bf16[256,4096]{1,0:T(8,128)(2,1)} %get-tuple-element.35), channel_id=1, source_target_pairs={{0,6},{2,0},{4,2},{6,4},{8,10},{10,12},{12,14},{14,8},{1,7},{3,1},... | collective-permute-start | bytes 6291464 | tf_op jit(solution)/shard_map/weights/ppermute | solution.py:233
  6.3 46.3 %collective-permute-start = (bf16[256,4096]{1,0:T(8,128)(2,1)}, bf16[256,4096]{1,0:T(8,128)(2,1)}, u32[]{:S(2)}, u32[]{:S(2)}) collective-permute-start(bf16[256,4096]{1,0:T(8,128)(2,1)} %get-tuple-element.35), channel_id=1, source_target_pairs={{0,2},{2,4},{4,6},{6,0},{8,14},{10,8},{12,10},{14,12},{1,3},{3,5},... | collective-permute-start | bytes 6291464 | tf_op jit(solution)/shard_map/weights/ppermute | solution.py:233
  6.3 39.3 %all-to-all-start = ((bf16[32,32,512]{2,1,0:T(8,128)(2,1)}), bf16[32,32,512]{2,1,0:T(8,128)(2,1)S(1)}, u32[]{:S(2)}, u32[]{:S(2)}) async-start(bf16[32,32,512]{2,1,0:T(8,128)(2,1)} %get-tuple-element.34), calls=%async_computation | async-start | bytes 2097152 | tf_op jit(solution)/shard_map/all_to_all | solution.py:293
  45.6 1.2 copy-start.2
  46.8 43.0 %copy-start.1 = (bf16[512,4096]{1,0:T(8,128)(2,1)S(1)}, bf16[512,4096]{1,0:T(8,128)(2,1)}, u32[]{:S(2)}) copy-start(bf16[512,4096]{1,0:T(8,128)(2,1)} %weight_ref.1) | copy-start | bytes 12582916
  52.6 30.4 %collective-permute-start.4 = (bf16[256,4096]{1,0:T(8,128)(2,1)S(1)}, bf16[256,4096]{1,0:T(8,128)(2,1)S(1)}, u32[]{:S(2)}, u32[]{:S(2)}) collective-permute-start(bf16[256,4096]{1,0:T(8,128)(2,1)S(1)} %collective-permute-done.1.refs_5_), channel_id=1, source_target_pairs={{0,8},{8,0},{1,9},{9,1},{2,10},{10,2},{3,11},{11,3},{4,12},{12,4},... | collective-permute-start | bytes 6291464 | tf_op jit(solution)/shard_map/weights/ppermute | solution.py:215
  53.6 29.4 %collective-permute-start.3 = (bf16[256,4096]{1,0:T(8,128)(2,1)}, bf16[256,4096]{1,0:T(8,128)(2,1)S(1)}, u32[]{:S(2)}, u32[]{:S(2)}) collective-permute-start(bf16[256,4096]{1,0:T(8,128)(2,1)} %collective-permute-done.refs_3_), channel_id=1, source_target_pairs={{0,8},{8,0},{1,9},{9,1},{2,10},{10,2},{3,11},{11,3},{4,12},{12,4},... | collective-permute-start | bytes 6291464 | tf_op jit(solution)/shard_map/weights/ppermute | solution.py:215
  53.7 29.3 %collective-permute-start.2 = (bf16[256,4096]{1,0:T(8,128)(2,1)}, bf16[256,4096]{1,0:T(8,128)(2,1)S(1)}, u32[]{:S(2)}, u32[]{:S(2)}) collective-permute-start(bf16[256,4096]{1,0:T(8,128)(2,1)} %collective-permute-done.refs_3_), channel_id=1, source_target_pairs={{0,2},{2,4},{4,6},{6,0},{8,14},{10,8},{12,10},{14,12},{1,3},{3,5},... | collective-permute-start | bytes 6291464 | tf_op jit(solution)/shard_map/weights/ppermute | solution.py:233
  83.0 12.8 %collective-permute-start.8 = (bf16[256,4096]{1,0:T(8,128)(2,1)S(1)}, bf16[256,4096]{1,0:T(8,128)(2,1)S(1)}, u32[]{:S(2)}, u32[]{:S(2)}) collective-permute-start(bf16[256,4096]{1,0:T(8,128)(2,1)S(1)} %collective-permute-done.2.refs_7_), channel_id=1, source_target_pairs={{0,8},{8,0},{1,9},{9,1},{2,10},{10,2},{3,11},{11,3},{4,12},{12,4},... | collective-permute-start | bytes 6291464 | tf_op jit(solution)/shard_map/weights/ppermute | solution.py:215
  84.3 1.0 copy-start.3
  85.6 10.2 %collective-permute-start.5 = (bf16[128,512]{1,0:T(8,128)(2,1)S(1)}, bf16[128,512]{1,0:T(8,128)(2,1)S(1)}, u32[]{:S(2)}, u32[]{:S(2)}) collective-permute-start(bf16[128,512]{1,0:T(8,128)(2,1)S(1)} %get-tuple-element.41), channel_id=1, source_target_pairs={{0,2},{2,4},{4,6},{6,0},{8,14},{10,8},{12,10},{14,12},{1,3},{3,5},... | collective-permute-start | bytes 393224 | tf_op jit(solution)/shard_map/quarters/ppermute | solution.py:233
  86.2 9.6 %collective-permute-start.6 = (bf16[128,512]{1,0:T(8,128)(2,1)S(1)}, bf16[128,512]{1,0:T(8,128)(2,1)S(1)}, u32[]{:S(2)}, u32[]{:S(2)}) collective-permute-start(bf16[128,512]{1,0:T(8,128)(2,1)S(1)} %get-tuple-element.42), channel_id=1, source_target_pairs={{0,6},{2,0},{4,2},{6,4},{8,10},{10,12},{12,14},{14,8},{1,7},{3,1},... | collective-permute-start | bytes 393224 | tf_op jit(solution)/shard_map/quarters/ppermute | solution.py:233
  88.9 6.9 %collective-permute-start.7 = (bf16[128,512]{1,0:T(8,128)(2,1)S(1)}, bf16[128,512]{1,0:T(8,128)(2,1)S(1)}, u32[]{:S(2)}, u32[]{:S(2)}) collective-permute-start(bf16[128,512]{1,0:T(8,128)(2,1)S(1)} %get-tuple-element.43), channel_id=1, source_target_pairs={{0,4},{2,6},{4,0},{6,2},{1,5},{3,7},{5,1},{7,3},{8,12},{10,14},{12... | collective-permute-start | bytes 393224 | tf_op jit(solution)/shard_map/quarters/ppermute | solution.py:223
  98.4 9.3 %collective-permute-start.13 = (bf16[64,2048]{1,0:T(8,128)(2,1)S(1)}, bf16[64,2048]{1,0:T(8,128)(2,1)S(1)}, u32[]{:S(2)}, u32[]{:S(2)}) collective-permute-start(bf16[64,2048]{1,0:T(8,128)(2,1)S(1)} %get-tuple-element.53), channel_id=1, source_target_pairs={{0,1},{1,0},{2,3},{3,2},{4,5},{5,4},{6,7},{7,6},{8,9},{9,8},{10,11... | collective-permute-start | bytes 786440 | tf_op jit(solution)/shard_map/gather/ppermute | solution.py:215
  102.6 10.7 %collective-permute-start.9 = (bf16[64,2048]{1,0:T(8,128)(2,1)S(1)}, bf16[64,2048]{1,0:T(8,128)(2,1)S(1)}, u32[]{:S(2)}, u32[]{:S(2)}) collective-permute-start(bf16[64,2048]{1,0:T(8,128)(2,1)S(1)} %get-tuple-element.48), channel_id=1, source_target_pairs={{0,1},{1,0},{2,3},{3,2},{4,5},{5,4},{6,7},{7,6},{8,9},{9,8},{10,11... | collective-permute-start | bytes 786440 | tf_op jit(solution)/shard_map/gather/ppermute | solution.py:215
  107.8 7.7 %collective-permute-start.16 = (bf16[64,2048]{1,0:T(8,128)(2,1)S(1)}, bf16[64,2048]{1,0:T(8,128)(2,1)S(1)}, u32[]{:S(2)}, u32[]{:S(2)}) collective-permute-start(bf16[64,2048]{1,0:T(8,128)(2,1)S(1)} %add_convert_fusion.refs_4_), channel_id=1, source_target_pairs={{0,6},{2,0},{4,2},{6,4},{1,7},{3,1},{5,3},{7,5},{8,14},{10,8},{12,... | collective-permute-start | bytes 786440 | tf_op jit(solution)/shard_map/gather/ppermute | solution.py:223
  109.1 9.0 %collective-permute-start.15 = (bf16[64,2048]{1,0:T(8,128)(2,1)S(1)}, bf16[64,2048]{1,0:T(8,128)(2,1)S(1)}, u32[]{:S(2)}, u32[]{:S(2)}) collective-permute-start(bf16[64,2048]{1,0:T(8,128)(2,1)S(1)} %add_convert_fusion.refs_4_), channel_id=1, source_target_pairs={{0,2},{2,4},{4,6},{6,0},{1,3},{3,5},{5,7},{7,1},{8,10},{10,12},{12... | collective-permute-start | bytes 786440 | tf_op jit(solution)/shard_map/gather/ppermute | solution.py:223
  109.9 9.2 %collective-permute-start.14 = (bf16[64,2048]{1,0:T(8,128)(2,1)S(1)}, bf16[64,2048]{1,0:T(8,128)(2,1)S(1)}, u32[]{:S(2)}, u32[]{:S(2)}) collective-permute-start(bf16[64,2048]{1,0:T(8,128)(2,1)S(1)} %add_convert_fusion.refs_4_), channel_id=1, source_target_pairs={{0,1},{1,0},{2,3},{3,2},{4,5},{5,4},{6,7},{7,6},{8,9},{9,8},{10,11... | collective-permute-start | bytes 786440 | tf_op jit(solution)/shard_map/gather/ppermute | solution.py:215
  113.4 9.0 %collective-permute-start.12 = (bf16[64,2048]{1,0:T(8,128)(2,1)S(1)}, bf16[64,2048]{1,0:T(8,128)(2,1)S(1)}, u32[]{:S(2)}, u32[]{:S(2)}) collective-permute-start(bf16[64,2048]{1,0:T(8,128)(2,1)S(1)} %add_convert_fusion.1.refs_0_), channel_id=1, source_target_pairs={{0,6},{2,0},{4,2},{6,4},{1,7},{3,1},{5,3},{7,5},{8,14},{10,8},{12,... | collective-permute-start | bytes 786440 | tf_op jit(solution)/shard_map/gather/ppermute | solution.py:223
  114.8 9.8 %collective-permute-start.11 = (bf16[64,2048]{1,0:T(8,128)(2,1)S(1)}, bf16[64,2048]{1,0:T(8,128)(2,1)S(1)}, u32[]{:S(2)}, u32[]{:S(2)}) collective-permute-start(bf16[64,2048]{1,0:T(8,128)(2,1)S(1)} %add_convert_fusion.1.refs_0_), channel_id=1, source_target_pairs={{0,2},{2,4},{4,6},{6,0},{1,3},{3,5},{5,7},{7,1},{8,10},{10,12},{12... | collective-permute-start | bytes 786440 | tf_op jit(solution)/shard_map/gather/ppermute | solution.py:223
  115.5 9.2 %collective-permute-start.10 = (bf16[64,2048]{1,0:T(8,128)(2,1)S(1)}, bf16[64,2048]{1,0:T(8,128)(2,1)S(1)}, u32[]{:S(2)}, u32[]{:S(2)}) collective-permute-start(bf16[64,2048]{1,0:T(8,128)(2,1)S(1)} %add_convert_fusion.1.refs_0_), channel_id=1, source_target_pairs={{0,1},{1,0},{2,3},{3,2},{4,5},{5,4},{6,7},{7,6},{8,9},{9,8},{10,11... | collective-permute-start | bytes 786440 | tf_op jit(solution)/shard_map/gather/ppermute | solution.py:215
  119.1 10.8 %collective-permute-start.24 = (bf16[64,2048]{1,0:T(8,128)(2,1)S(1)}, bf16[64,2048]{1,0:T(8,128)(2,1)S(1)}, u32[]{:S(2)}, u32[]{:S(2)}) collective-permute-start(bf16[64,2048]{1,0:T(8,128)(2,1)S(1)} %collective-permute-done.14.refs_5_), channel_id=1, source_target_pairs={{0,2},{2,4},{4,6},{6,0},{1,3},{3,5},{5,7},{7,1},{8,10},{10,12},{12... | collective-permute-start | bytes 786440 | tf_op jit(solution)/shard_map/gather/ppermute | solution.py:223
  119.1 13.4 %collective-permute-start.23 = (bf16[64,2048]{1,0:T(8,128)(2,1)S(1)}, bf16[64,2048]{1,0:T(8,128)(2,1)S(1)}, u32[]{:S(2)}, u32[]{:S(2)}) collective-permute-start(bf16[64,2048]{1,0:T(8,128)(2,1)S(1)} %collective-permute-done.16.refs_7_), channel_id=1, source_target_pairs={{0,6},{2,0},{4,2},{6,4},{1,7},{3,1},{5,3},{7,5},{8,14},{10,8},{12,... | collective-permute-start | bytes 786440 | tf_op jit(solution)/shard_map/gather/ppermute | solution.py:223
  122.3 10.2 %collective-permute-start.22 = (bf16[64,2048]{1,0:T(8,128)(2,1)S(1)}, bf16[64,2048]{1,0:T(8,128)(2,1)S(1)}, u32[]{:S(2)}, u32[]{:S(2)}) collective-permute-start(bf16[64,2048]{1,0:T(8,128)(2,1)S(1)} %collective-permute-done.16.refs_7_), channel_id=1, source_target_pairs={{0,1},{1,0},{2,3},{3,2},{4,5},{5,4},{6,7},{7,6},{8,9},{9,8},{10,11... | collective-permute-start | bytes 786440 | tf_op jit(solution)/shard_map/gather/ppermute | solution.py:215
  124.7 11.2 %collective-permute-start.19 = (bf16[64,2048]{1,0:T(8,128)(2,1)S(1)}, bf16[64,2048]{1,0:T(8,128)(2,1)S(1)}, u32[]{:S(2)}, u32[]{:S(2)}) collective-permute-start(bf16[64,2048]{1,0:T(8,128)(2,1)S(1)} %collective-permute-done.10.refs_1_), channel_id=1, source_target_pairs={{0,2},{2,4},{4,6},{6,0},{1,3},{3,5},{5,7},{7,1},{8,10},{10,12},{12... | collective-permute-start | bytes 786440 | tf_op jit(solution)/shard_map/gather/ppermute | solution.py:223
  124.7 11.2 %collective-permute-start.18 = (bf16[64,2048]{1,0:T(8,128)(2,1)S(1)}, bf16[64,2048]{1,0:T(8,128)(2,1)S(1)}, u32[]{:S(2)}, u32[]{:S(2)}) collective-permute-start(bf16[64,2048]{1,0:T(8,128)(2,1)S(1)} %collective-permute-done.12.refs_3_), channel_id=1, source_target_pairs={{0,6},{2,0},{4,2},{6,4},{1,7},{3,1},{5,3},{7,5},{8,14},{10,8},{12,... | collective-permute-start | bytes 786440 | tf_op jit(solution)/shard_map/gather/ppermute | solution.py:223
  129.9 7.0 %collective-permute-start.17 = (bf16[64,2048]{1,0:T(8,128)(2,1)S(1)}, bf16[64,2048]{1,0:T(8,128)(2,1)S(1)}, u32[]{:S(2)}, u32[]{:S(2)}) collective-permute-start(bf16[64,2048]{1,0:T(8,128)(2,1)S(1)} %collective-permute-done.12.refs_3_), channel_id=1, source_target_pairs={{0,1},{1,0},{2,3},{3,2},{4,5},{5,4},{6,7},{7,6},{8,9},{9,8},{10,11... | collective-permute-start | bytes 786440 | tf_op jit(solution)/shard_map/gather/ppermute | solution.py:215
  132.6 9.0 %collective-permute-start.25 = (bf16[64,1024]{1,0:T(8,128)(2,1)S(1)}, bf16[64,1024]{1,0:T(8,128)(2,1)S(1)}, u32[]{:S(2)}, u32[]{:S(2)}) collective-permute-start(bf16[64,1024]{1,0:T(8,128)(2,1)S(1)} %slice.14), channel_id=1, source_target_pairs={{0,2},{2,4},{4,6},{6,0},{1,3},{3,5},{5,7},{7,1},{8,10},{10,12},{12... | collective-permute-start | bytes 393224 | tf_op jit(solution)/shard_map/gather/ppermute | solution.py:223
  132.6 9.0 %collective-permute-start.26 = (bf16[64,1024]{1,0:T(8,128)(2,1)S(1)}, bf16[64,1024]{1,0:T(8,128)(2,1)S(1)}, u32[]{:S(2)}, u32[]{:S(2)}) collective-permute-start(bf16[64,1024]{1,0:T(8,128)(2,1)S(1)} %slice.15), channel_id=1, source_target_pairs={{0,6},{2,0},{4,2},{6,4},{1,7},{3,1},{5,3},{7,5},{8,14},{10,8},{12,... | collective-permute-start | bytes 393224 | tf_op jit(solution)/shard_map/gather/ppermute | solution.py:223
  136.9 6.3 %collective-permute-start.20 = (bf16[64,1024]{1,0:T(8,128)(2,1)S(1)}, bf16[64,1024]{1,0:T(8,128)(2,1)S(1)}, u32[]{:S(2)}, u32[]{:S(2)}) collective-permute-start(bf16[64,1024]{1,0:T(8,128)(2,1)S(1)} %slice.12), channel_id=1, source_target_pairs={{0,2},{2,4},{4,6},{6,0},{1,3},{3,5},{5,7},{7,1},{8,10},{10,12},{12... | collective-permute-start | bytes 393224 | tf_op jit(solution)/shard_map/gather/ppermute | solution.py:223
  137.0 6.2 %collective-permute-start.21 = (bf16[64,1024]{1,0:T(8,128)(2,1)S(1)}, bf16[64,1024]{1,0:T(8,128)(2,1)S(1)}, u32[]{:S(2)}, u32[]{:S(2)}) collective-permute-start(bf16[64,1024]{1,0:T(8,128)(2,1)S(1)} %slice.13), channel_id=1, source_target_pairs={{0,6},{2,0},{4,2},{6,4},{1,7},{3,1},{5,3},{7,5},{8,14},{10,8},{12,... | collective-permute-start | bytes 393224 | tf_op jit(solution)/shard_map/gather/ppermute | solution.py:223

commit v7 on v6

--- a/solution.py
+++ b/solution.py
@@ -302,13 +302,13 @@
             limit=24,
         )(arrived, gain, table)
     with jax.named_scope("weights"):
-        total, toward, back = lax.optimization_barrier((total, toward, back))
+        total, toward = lax.optimization_barrier((total, toward))
         far = mirrored(toward, 1)
-        swapped = [along_core(toward), along_core(back)]
+        swapped = [along_core(toward)]
     total = lax.all_to_all(total, ("block", "core"), split_axis=0, concat_axis=0, tiled=True)
     with jax.named_scope("weights"):
-        total, far, *swapped = lax.optimization_barrier((total, far, *swapped))
-        weights = (toward, swapped[1], back, swapped[0], far, along_core(far))
+        total, far, back, *swapped = lax.optimization_barrier((total, far, back, *swapped))
+        weights = (toward, along_core(back), back, swapped[0], far, along_core(far))
     with jax.named_scope("gate"):
         gated = whole(
             gate_kernel, [((quarter, channels), half16)] * 4, [VMEM] * 2, [VMEM] * 4, [square]

time: 147 us -> 145 us (0.986)
  blocking collectives: 28.7 us -> 0 us
  waiting for transfers between devices: 45.5 us -> 64.5 us
  local copies, waits for them, and re-layouts: 2.48 us -> 5.45 us
  Pallas kernels: 17.9 us -> 20.5 us
  starting transfers between devices: 49.7 us -> 51.5 us
    all_to_all x1 -> x0, blocking collectives: 28.7 us -> none  [body(): lax.all_to_all(total, ('block', 'core'), split_axis=0, concat_axis=0, til...]
    all_to_all x0 -> x1, waiting for transfers between devices: none -> 16.3 us  [body(): lax.all_to_all(total, ('block', 'core'), split_axis=0, concat_axis=0, til...]
    all_to_all x0 -> x1, starting transfers between devices: none -> 5.62 us  [body(): lax.all_to_all(total, ('block', 'core'), split_axis=0, concat_axis=0, til...]
    ppermute x9, starting transfers between devices: 12.8 us -> 8.88 us  [swap(): return lambda value: lax.ppermute(value, axis, [(0, 1), (1, 0)])]
    ppermute x13, waiting for transfers between devices: 4.17 us -> 7.77 us  [along_y(): lax.ppermute(value, 'y', [(i, (i + steps) % count) for i in range(count)])]
    unnamed x8 -> x10, local copies, waits for them, and re-layouts: 2.27 us -> 5.25 us
    pallas_call x2, Pallas kernels: 5.22 us -> 7.91 us  [body(): whole(functools.partial(rest_kernel, stream * width), [((quarter // 2, wi...]
  transfers between devices with their start and end apart: 28 -> 29, of which waited for: 10 -> 13; matrix products, arithmetic and copies ran while one was open for 0% -> 0% of each run, Pallas kernels for 7% -> 8%
where the time goes in v7:
time: 145 us; the launch traced here: 142 us
  waiting for transfers between devices  64.5 us (44%)
  starting transfers between devices  51.5 us (36%)
  Pallas kernels  20.5 us (14%)
  local copies, waits for them, and re-layouts  5.45 us (4%)
    all_to_all x1, waiting for transfers between devices, body(): lax.all_to_all(outgoing, ('block', 'core'), split_axis=0, concat_axis=0,...  26.4 us
    ppermute x13, starting transfers between devices, along_y(): lax.ppermute(value, 'y', [(i, (i + steps) % count) for i in range(count)])  17.7 us
    all_to_all x1, waiting for transfers between devices, body(): lax.all_to_all(total, ('block', 'core'), split_axis=0, concat_axis=0, til...  16.3 us
    all_to_all x1, starting transfers between devices, body(): lax.all_to_all(outgoing, ('block', 'core'), split_axis=0, concat_axis=0,...  12.2 us
    ppermute x9, starting transfers between devices, swap(): return lambda value: lax.ppermute(value, axis, [(0, 1), (1, 0)])  8.88 us
    pallas_call x2, Pallas kernels, body(): whole(functools.partial(rest_kernel, stream * width), [((quarter // 2, wi...  7.91 us
    ppermute x13, waiting for transfers between devices, along_y(): lax.ppermute(value, 'y', [(i, (i + steps) % count) for i in range(count)])  7.77 us
    ppermute x9, waiting for transfers between devices, swap(): return lambda value: lax.ppermute(value, axis, [(0, 1), (1, 0)])  7.44 us
  transfers between devices with their start and end apart: 29, of which 13 were waited for; matrix products, arithmetic and copies ran while one was open for 0% of the time, Pallas kernels for 8%

profile of v7, /device:TPU:2, one launch (start us, length us, event | category | flops | bytes accessed | tf_op | source)
XLA Modules:
  0.0 142.4 jit_solution(3053396034720101098)
XLA Ops:
  0.0 3.2 %pack.1 = (bf16[32,32,512]{2,1,0:T(8,128)(2,1)}, bf16[256,4096]{1,0:T(8,128)(2,1)}) custom-call(bf16[512,512]{1,0:T(8,128)(2,1)} %key_hbm.1, bf16[512,512]{1,0:T(8,128)(2,1)} %value_hbm.1, bf16[512,512]{1,0:T(8,128)(2,1)} %filter_hbm.1, bf16[512,4096]{1,0:T(8,128)(2,1)} %weight_ref.1), custom_call_target="tpu_custom_call" | custom-call | bytes 8388608 | tf_op jit(solution)/shard_map/pack/pallas_call | solution.py:276
  3.2 1.7 %collective-permute-start = (bf16[256,4096]{1,0:T(8,128)(2,1)}, bf16[256,4096]{1,0:T(8,128)(2,1)S(1)}, u32[]{:S(2)}, u32[]{:S(2)}) collective-permute-start(bf16[256,4096]{1,0:T(8,128)(2,1)} %get-tuple-element.34), channel_id=1, source_target_pairs={{0,2},{2,4},{4,6},{6,0},{8,14},{10,8},{12,10},{14,12},{1,3},{3,5},... | collective-permute-start | bytes 6291464 | tf_op jit(solution)/shard_map/weights/ppermute | solution.py:233
  4.9 12.2 %all-to-all-start = ((bf16[32,32,512]{2,1,0:T(8,128)(2,1)}), bf16[32,32,512]{2,1,0:T(8,128)(2,1)S(1)}, u32[]{:S(2)}, u32[]{:S(2)}) async-start(bf16[32,32,512]{2,1,0:T(8,128)(2,1)} %get-tuple-element.33), calls=%async_computation | async-start | bytes 2097152 | tf_op jit(solution)/shard_map/all_to_all | solution.py:293
  17.1 1.1 collective-permute-start.2
  18.4 26.4 %all-to-all-done.signal_ref = bf16[32,32,512]{2,1,0:T(8,128)(2,1)S(1)} async-done(((bf16[32,32,512]{2,1,0:T(8,128)(2,1)}), bf16[32,32,512]{2,1,0:T(8,128)(2,1)S(1)}, u32[]{:S(2)}, u32[]{:S(2)}) %all-to-all-start) | async-done | bytes 1048608 | tf_op jit(solution)/shard_map/all_to_all | solution.py:293
  44.8 1.2 copy-done.3
  46.0 5.7 %conv.1 = bf16[32,16,512]{2,1,0:T(8,128)(2,1)S(1)} custom-call(bf16[32,32,512]{2,1,0:T(8,128)(2,1)S(1)} %all-to-all-done.signal_ref, f32[16,1]{1,0:T(8,128)S(1)} %copy.9.gain_ref, bf16[512,1024]{1,0:T(8,128)(2,1)S(1)} %copy-done.3), custom_call_target="tpu_custom_call" | custom-call | bytes 8388608 | tf_op jit(solution)/shard_map/conv/pallas_call | solution.py:296
  54.4 5.6 %all-to-all-start.1 = ((bf16[32,16,512]{2,1,0:T(8,128)(2,1)}), bf16[32,16,512]{2,1,0:T(8,128)(2,1)S(1)}, u32[]{:S(2)}, u32[]{:S(2)}) async-start(bf16[32,16,512]{2,1,0:T(8,128)(2,1)} %copy-done.2), calls=%async_computation.1 | async-start | bytes 1048576 | tf_op jit(solution)/shard_map/all_to_all | solution.py:308
  60.0 16.3 %all-to-all-done.1.total_ref = bf16[32,16,512]{2,1,0:T(8,128)(2,1)S(1)} async-done(((bf16[32,16,512]{2,1,0:T(8,128)(2,1)}), bf16[32,16,512]{2,1,0:T(8,128)(2,1)S(1)}, u32[]{:S(2)}, u32[]{:S(2)}) %all-to-all-start.1) | async-done | bytes 524320 | tf_op jit(solution)/shard_map/all_to_all | solution.py:308
  76.3 4.4 %collective-permute-done.1.refs_7_ = bf16[256,4096]{1,0:T(8,128)(2,1)} collective-permute-done((bf16[256,4096]{1,0:T(8,128)(2,1)S(1)}, bf16[256,4096]{1,0:T(8,128)(2,1)}, u32[]{:S(2)}, u32[]{:S(2)}) %collective-permute-start.1) | collective-permute-done | bytes 2097184 | tf_op jit(solution)/shard_map/weights/ppermute | solution.py:233
  82.7 3.2 %collective-permute-start.5 = (bf16[128,512]{1,0:T(8,128)(2,1)S(1)}, bf16[128,512]{1,0:T(8,128)(2,1)S(1)}, u32[]{:S(2)}, u32[]{:S(2)}) collective-permute-start(bf16[128,512]{1,0:T(8,128)(2,1)S(1)} %get-tuple-element.40), channel_id=1, source_target_pairs={{0,6},{2,0},{4,2},{6,4},{8,10},{10,12},{12,14},{14,8},{1,7},{3,1},... | collective-permute-start | bytes 393224 | tf_op jit(solution)/shard_map/quarters/ppermute | solution.py:233
  85.9 2.2 %copy-done.1 = bf16[512,4096]{1,0:T(8,128)(2,1)S(1)} copy-done((bf16[512,4096]{1,0:T(8,128)(2,1)S(1)}, bf16[512,4096]{1,0:T(8,128)(2,1)}, u32[]{:S(2)}) %copy-start.1) | copy-done | bytes 4194328
  88.8 2.1 %collective-permute-done.4.refs_0_ = bf16[128,512]{1,0:T(8,128)(2,1)S(1)} collective-permute-done((bf16[128,512]{1,0:T(8,128)(2,1)S(1)}, bf16[128,512]{1,0:T(8,128)(2,1)S(1)}, u32[]{:S(2)}, u32[]{:S(2)}) %collective-permute-start.4) | collective-permute-done | bytes 131104 | tf_op jit(solution)/shard_map/quarters/ppermute | solution.py:233
  90.9 1.4 collective-permute-done.6.refs_2_
  92.4 4.0 %rest.3 = (bf16[64,2048]{1,0:T(8,128)(2,1)S(1)}, bf16[64,2048]{1,0:T(8,128)(2,1)S(1)}) custom-call(f32[128,4096]{1,0:T(8,128)S(1)} %own.1.partial_ref, bf16[128,512]{1,0:T(8,128)(2,1)S(1)} %collective-permute-done.4.refs_0_, bf16[128,512]{1,0:T(8,128)(2,1)S(1)} %collective-permute-done.5.refs_1_, bf16[128,512]{1,0:T(8,128)(2,1)S(1)} %collective-permute-done.6.refs_2_, ...), custom_call_target="tpu_custom_call" | custom-call | flops 536870912 | bytes 8388608 | tf_op jit(solution)/shard_map/rest/pallas_call | solution.py:326
  96.3 1.4 collective-permute-start.13
  97.7 4.0 %rest.2 = (bf16[64,2048]{1,0:T(8,128)(2,1)S(1)}, bf16[64,2048]{1,0:T(8,128)(2,1)S(1)}) custom-call(f32[128,4096]{1,0:T(8,128)S(1)} %own.1.partial_ref, bf16[128,512]{1,0:T(8,128)(2,1)S(1)} %collective-permute-done.4.refs_0_, bf16[128,512]{1,0:T(8,128)(2,1)S(1)} %collective-permute-done.5.refs_1_, bf16[128,512]{1,0:T(8,128)(2,1)S(1)} %collective-permute-done.6.refs_2_, ...), custom_call_target="tpu_custom_call" | custom-call | flops 536870912 | bytes 8388608 | tf_op jit(solution)/shard_map/rest/pallas_call | solution.py:326
  103.4 2.4 %collective-permute-start.16 = (bf16[64,2048]{1,0:T(8,128)(2,1)S(1)}, bf16[64,2048]{1,0:T(8,128)(2,1)S(1)}, u32[]{:S(2)}, u32[]{:S(2)}) collective-permute-start(bf16[64,2048]{1,0:T(8,128)(2,1)S(1)} %add_convert_fusion.refs_4_), channel_id=1, source_target_pairs={{0,6},{2,0},{4,2},{6,4},{1,7},{3,1},{5,3},{7,5},{8,14},{10,8},{12,... | collective-permute-start | bytes 786440 | tf_op jit(solution)/shard_map/gather/ppermute | solution.py:223
  105.8 1.9 %collective-permute-start.14 = (bf16[64,2048]{1,0:T(8,128)(2,1)S(1)}, bf16[64,2048]{1,0:T(8,128)(2,1)S(1)}, u32[]{:S(2)}, u32[]{:S(2)}) collective-permute-start(bf16[64,2048]{1,0:T(8,128)(2,1)S(1)} %add_convert_fusion.refs_4_), channel_id=1, source_target_pairs={{0,1},{1,0},{2,3},{3,2},{4,5},{5,4},{6,7},{7,6},{8,9},{9,8},{10,11... | collective-permute-start | bytes 786440 | tf_op jit(solution)/shard_map/gather/ppermute | solution.py:215
  107.7 3.4 %collective-permute-done.9 = bf16[64,2048]{1,0:T(8,128)(2,1)S(1)} collective-permute-done((bf16[64,2048]{1,0:T(8,128)(2,1)S(1)}, bf16[64,2048]{1,0:T(8,128)(2,1)S(1)}, u32[]{:S(2)}, u32[]{:S(2)}) %collective-permute-start.9) | collective-permute-done | bytes 262176 | tf_op jit(solution)/shard_map/gather/ppermute | solution.py:215
  111.1 2.2 %collective-permute-start.12 = (bf16[64,2048]{1,0:T(8,128)(2,1)S(1)}, bf16[64,2048]{1,0:T(8,128)(2,1)S(1)}, u32[]{:S(2)}, u32[]{:S(2)}) collective-permute-start(bf16[64,2048]{1,0:T(8,128)(2,1)S(1)} %add_convert_fusion.1.refs_0_), channel_id=1, source_target_pairs={{0,6},{2,0},{4,2},{6,4},{1,7},{3,1},{5,3},{7,5},{8,14},{10,8},{12,... | collective-permute-start | bytes 786440 | tf_op jit(solution)/shard_map/gather/ppermute | solution.py:223
  114.5 2.1 %collective-permute-done.14.refs_5_ = bf16[64,2048]{1,0:T(8,128)(2,1)S(1)} collective-permute-done((bf16[64,2048]{1,0:T(8,128)(2,1)S(1)}, bf16[64,2048]{1,0:T(8,128)(2,1)S(1)}, u32[]{:S(2)}, u32[]{:S(2)}) %collective-permute-start.14) | collective-permute-done | bytes 262176 | tf_op jit(solution)/shard_map/gather/ppermute | solution.py:215
  116.8 3.1 %collective-permute-start.23 = (bf16[64,2048]{1,0:T(8,128)(2,1)S(1)}, bf16[64,2048]{1,0:T(8,128)(2,1)S(1)}, u32[]{:S(2)}, u32[]{:S(2)}) collective-permute-start(bf16[64,2048]{1,0:T(8,128)(2,1)S(1)} %collective-permute-done.16.refs_7_), channel_id=1, source_target_pairs={{0,6},{2,0},{4,2},{6,4},{1,7},{3,1},{5,3},{7,5},{8,14},{10,8},{12,... | collective-permute-start | bytes 786440 | tf_op jit(solution)/shard_map/gather/ppermute | solution.py:223
  120.6 2.2 %collective-permute-done.11.refs_2_ = bf16[64,2048]{1,0:T(8,128)(2,1)S(1)} collective-permute-done((bf16[64,2048]{1,0:T(8,128)(2,1)S(1)}, bf16[64,2048]{1,0:T(8,128)(2,1)S(1)}, u32[]{:S(2)}, u32[]{:S(2)}) %collective-permute-start.11) | collective-permute-done | bytes 262176 | tf_op jit(solution)/shard_map/gather/ppermute | solution.py:223
  122.8 3.2 %collective-permute-start.18 = (bf16[64,2048]{1,0:T(8,128)(2,1)S(1)}, bf16[64,2048]{1,0:T(8,128)(2,1)S(1)}, u32[]{:S(2)}, u32[]{:S(2)}) collective-permute-start(bf16[64,2048]{1,0:T(8,128)(2,1)S(1)} %collective-permute-done.12.refs_3_), channel_id=1, source_target_pairs={{0,6},{2,0},{4,2},{6,4},{1,7},{3,1},{5,3},{7,5},{8,14},{10,8},{12,... | collective-permute-start | bytes 786440 | tf_op jit(solution)/shard_map/gather/ppermute | solution.py:223
  126.1 2.1 %collective-permute-done.24.refs_8_ = bf16[64,2048]{1,0:T(8,128)(2,1)S(1)} collective-permute-done((bf16[64,2048]{1,0:T(8,128)(2,1)S(1)}, bf16[64,2048]{1,0:T(8,128)(2,1)S(1)}, u32[]{:S(2)}, u32[]{:S(2)}) %collective-permute-start.24) | collective-permute-done | bytes 262176 | tf_op jit(solution)/shard_map/gather/ppermute | solution.py:223
  128.2 1.9 %collective-permute-start.17 = (bf16[64,2048]{1,0:T(8,128)(2,1)S(1)}, bf16[64,2048]{1,0:T(8,128)(2,1)S(1)}, u32[]{:S(2)}, u32[]{:S(2)}) collective-permute-start(bf16[64,2048]{1,0:T(8,128)(2,1)S(1)} %collective-permute-done.12.refs_3_), channel_id=1, source_target_pairs={{0,1},{1,0},{2,3},{3,2},{4,5},{5,4},{6,7},{7,6},{8,9},{9,8},{10,11... | collective-permute-start | bytes 786440 | tf_op jit(solution)/shard_map/gather/ppermute | solution.py:215
  130.3 3.2 %collective-permute-start.26 = (bf16[64,1024]{1,0:T(8,128)(2,1)S(1)}, bf16[64,1024]{1,0:T(8,128)(2,1)S(1)}, u32[]{:S(2)}, u32[]{:S(2)}) collective-permute-start(bf16[64,1024]{1,0:T(8,128)(2,1)S(1)} %slice.15), channel_id=1, source_target_pairs={{0,6},{2,0},{4,2},{6,4},{1,7},{3,1},{5,3},{7,5},{8,14},{10,8},{12,... | collective-permute-start | bytes 393224 | tf_op jit(solution)/shard_map/gather/ppermute | solution.py:223
  134.7 3.2 %collective-permute-start.21 = (bf16[64,1024]{1,0:T(8,128)(2,1)S(1)}, bf16[64,1024]{1,0:T(8,128)(2,1)S(1)}, u32[]{:S(2)}, u32[]{:S(2)}) collective-permute-start(bf16[64,1024]{1,0:T(8,128)(2,1)S(1)} %slice.13), channel_id=1, source_target_pairs={{0,6},{2,0},{4,2},{6,4},{1,7},{3,1},{5,3},{7,5},{8,14},{10,8},{12,... | collective-permute-start | bytes 393224 | tf_op jit(solution)/shard_map/gather/ppermute | solution.py:223
  137.9 1.4 gather.2.refs_0_
  139.3 1.5 %collective-permute-done.20.refs_4_ = bf16[64,1024]{1,0:T(8,128)(2,1)S(1)} collective-permute-done((bf16[64,1024]{1,0:T(8,128)(2,1)S(1)}, bf16[64,1024]{1,0:T(8,128)(2,1)S(1)}, u32[]{:S(2)}, u32[]{:S(2)}) %collective-permute-start.20) | collective-permute-done | bytes 131104 | tf_op jit(solution)/shard_map/gather/ppermute | solution.py:223
  140.9 1.4 gather.3
  (52 shorter events, 10.6 us)
Async XLA Ops:
  0.0 18.2 %copy-start = (f32[512]{0:T(512)S(1)}, f32[512]{0:T(512)}, u32[]{:S(2)}) copy-start(f32[512]{0:T(512)} %param.11) | copy-start | bytes 6148
  3.2 49.3 %collective-permute-start = (bf16[256,4096]{1,0:T(8,128)(2,1)}, bf16[256,4096]{1,0:T(8,128)(2,1)S(1)}, u32[]{:S(2)}, u32[]{:S(2)}) collective-permute-start(bf16[256,4096]{1,0:T(8,128)(2,1)} %get-tuple-element.34), channel_id=1, source_target_pairs={{0,2},{2,4},{4,6},{6,0},{8,14},{10,8},{12,10},{14,12},{1,3},{3,5},... | collective-permute-start | bytes 6291464 | tf_op jit(solution)/shard_map/weights/ppermute | solution.py:233
  4.9 39.9 %all-to-all-start = ((bf16[32,32,512]{2,1,0:T(8,128)(2,1)}), bf16[32,32,512]{2,1,0:T(8,128)(2,1)S(1)}, u32[]{:S(2)}, u32[]{:S(2)}) async-start(bf16[32,32,512]{2,1,0:T(8,128)(2,1)} %get-tuple-element.33), calls=%async_computation | async-start | bytes 2097152 | tf_op jit(solution)/shard_map/all_to_all | solution.py:293
  17.1 42.9 %collective-permute-start.2 = (bf16[256,4096]{1,0:T(8,128)(2,1)}, bf16[256,4096]{1,0:T(8,128)(2,1)}, u32[]{:S(2)}, u32[]{:S(2)}) collective-permute-start(bf16[256,4096]{1,0:T(8,128)(2,1)} %get-tuple-element.34), channel_id=1, source_target_pairs={{0,6},{2,0},{4,2},{6,4},{8,10},{10,12},{12,14},{14,8},{1,7},{3,1},... | collective-permute-start | bytes 6291464 | tf_op jit(solution)/shard_map/weights/ppermute | solution.py:233
  44.7 1.2 copy-start.3
  52.5 23.8 %collective-permute-start.3 = (bf16[256,4096]{1,0:T(8,128)(2,1)S(1)}, bf16[256,4096]{1,0:T(8,128)(2,1)}, u32[]{:S(2)}, u32[]{:S(2)}) collective-permute-start(bf16[256,4096]{1,0:T(8,128)(2,1)S(1)} %collective-permute-done.refs_3_), channel_id=1, source_target_pairs={{0,8},{8,0},{1,9},{9,1},{2,10},{10,2},{3,11},{11,3},{4,12},{12,4},... | collective-permute-start | bytes 6291464 | tf_op jit(solution)/shard_map/weights/ppermute | solution.py:215
  53.4 27.4 %collective-permute-start.1 = (bf16[256,4096]{1,0:T(8,128)(2,1)S(1)}, bf16[256,4096]{1,0:T(8,128)(2,1)}, u32[]{:S(2)}, u32[]{:S(2)}) collective-permute-start(bf16[256,4096]{1,0:T(8,128)(2,1)S(1)} %collective-permute-done.refs_3_), channel_id=1, source_target_pairs={{0,2},{2,4},{4,6},{6,0},{8,14},{10,8},{12,10},{14,12},{1,3},{3,5},... | collective-permute-start | bytes 6291464 | tf_op jit(solution)/shard_map/weights/ppermute | solution.py:233
  54.4 22.0 %all-to-all-start.1 = ((bf16[32,16,512]{2,1,0:T(8,128)(2,1)}), bf16[32,16,512]{2,1,0:T(8,128)(2,1)S(1)}, u32[]{:S(2)}, u32[]{:S(2)}) async-start(bf16[32,16,512]{2,1,0:T(8,128)(2,1)} %copy-done.2), calls=%async_computation.1 | async-start | bytes 1048576 | tf_op jit(solution)/shard_map/all_to_all | solution.py:308
  80.8 11.6 %collective-permute-start.7 = (bf16[256,4096]{1,0:T(8,128)(2,1)}, bf16[256,4096]{1,0:T(8,128)(2,1)S(1)}, u32[]{:S(2)}, u32[]{:S(2)}) collective-permute-start(bf16[256,4096]{1,0:T(8,128)(2,1)} %collective-permute-done.2.refs_5_), channel_id=1, source_target_pairs={{0,8},{8,0},{1,9},{9,1},{2,10},{10,2},{3,11},{11,3},{4,12},{12,4},... | collective-permute-start | bytes 6291464 | tf_op jit(solution)/shard_map/weights/ppermute | solution.py:215
  80.8 11.6 %collective-permute-start.8 = (bf16[256,4096]{1,0:T(8,128)(2,1)}, bf16[256,4096]{1,0:T(8,128)(2,1)S(1)}, u32[]{:S(2)}, u32[]{:S(2)}) collective-permute-start(bf16[256,4096]{1,0:T(8,128)(2,1)} %collective-permute-done.1.refs_7_), channel_id=1, source_target_pairs={{0,8},{8,0},{1,9},{9,1},{2,10},{10,2},{3,11},{11,3},{4,12},{12,4},... | collective-permute-start | bytes 6291464 | tf_op jit(solution)/shard_map/weights/ppermute | solution.py:215
  82.6 8.4 %collective-permute-start.4 = (bf16[128,512]{1,0:T(8,128)(2,1)S(1)}, bf16[128,512]{1,0:T(8,128)(2,1)S(1)}, u32[]{:S(2)}, u32[]{:S(2)}) collective-permute-start(bf16[128,512]{1,0:T(8,128)(2,1)S(1)} %get-tuple-element.39), channel_id=1, source_target_pairs={{0,2},{2,4},{4,6},{6,0},{8,14},{10,8},{12,10},{14,12},{1,3},{3,5},... | collective-permute-start | bytes 393224 | tf_op jit(solution)/shard_map/quarters/ppermute | solution.py:233
  82.7 8.3 %collective-permute-start.5 = (bf16[128,512]{1,0:T(8,128)(2,1)S(1)}, bf16[128,512]{1,0:T(8,128)(2,1)S(1)}, u32[]{:S(2)}, u32[]{:S(2)}) collective-permute-start(bf16[128,512]{1,0:T(8,128)(2,1)S(1)} %get-tuple-element.40), channel_id=1, source_target_pairs={{0,6},{2,0},{4,2},{6,4},{8,10},{10,12},{12,14},{14,8},{1,7},{3,1},... | collective-permute-start | bytes 393224 | tf_op jit(solution)/shard_map/quarters/ppermute | solution.py:233
  85.9 6.5 %collective-permute-start.6 = (bf16[128,512]{1,0:T(8,128)(2,1)S(1)}, bf16[128,512]{1,0:T(8,128)(2,1)S(1)}, u32[]{:S(2)}, u32[]{:S(2)}) collective-permute-start(bf16[128,512]{1,0:T(8,128)(2,1)S(1)} %get-tuple-element.41), channel_id=1, source_target_pairs={{0,4},{2,6},{4,0},{6,2},{1,5},{3,7},{5,1},{7,3},{8,12},{10,14},{12... | collective-permute-start | bytes 393224 | tf_op jit(solution)/shard_map/quarters/ppermute | solution.py:223
  85.9 2.2 %copy-start.1 = (bf16[512,4096]{1,0:T(8,128)(2,1)S(1)}, bf16[512,4096]{1,0:T(8,128)(2,1)}, u32[]{:S(2)}) copy-start(bf16[512,4096]{1,0:T(8,128)(2,1)} %weight_ref.1) | copy-start | bytes 12582916
  96.3 7.0 %collective-permute-start.13 = (bf16[64,2048]{1,0:T(8,128)(2,1)S(1)}, bf16[64,2048]{1,0:T(8,128)(2,1)S(1)}, u32[]{:S(2)}, u32[]{:S(2)}) collective-permute-start(bf16[64,2048]{1,0:T(8,128)(2,1)S(1)} %get-tuple-element.51), channel_id=1, source_target_pairs={{0,1},{1,0},{2,3},{3,2},{4,5},{5,4},{6,7},{7,6},{8,9},{9,8},{10,11... | collective-permute-start | bytes 786440 | tf_op jit(solution)/shard_map/gather/ppermute | solution.py:215
  101.7 9.3 %collective-permute-start.9 = (bf16[64,2048]{1,0:T(8,128)(2,1)S(1)}, bf16[64,2048]{1,0:T(8,128)(2,1)S(1)}, u32[]{:S(2)}, u32[]{:S(2)}) collective-permute-start(bf16[64,2048]{1,0:T(8,128)(2,1)S(1)} %get-tuple-element.46), channel_id=1, source_target_pairs={{0,1},{1,0},{2,3},{3,2},{4,5},{5,4},{6,7},{7,6},{8,9},{9,8},{10,11... | collective-permute-start | bytes 786440 | tf_op jit(solution)/shard_map/gather/ppermute | solution.py:215
  103.4 9.9 %collective-permute-start.16 = (bf16[64,2048]{1,0:T(8,128)(2,1)S(1)}, bf16[64,2048]{1,0:T(8,128)(2,1)S(1)}, u32[]{:S(2)}, u32[]{:S(2)}) collective-permute-start(bf16[64,2048]{1,0:T(8,128)(2,1)S(1)} %add_convert_fusion.refs_4_), channel_id=1, source_target_pairs={{0,6},{2,0},{4,2},{6,4},{1,7},{3,1},{5,3},{7,5},{8,14},{10,8},{12,... | collective-permute-start | bytes 786440 | tf_op jit(solution)/shard_map/gather/ppermute | solution.py:223
  105.8 8.7 %collective-permute-start.15 = (bf16[64,2048]{1,0:T(8,128)(2,1)S(1)}, bf16[64,2048]{1,0:T(8,128)(2,1)S(1)}, u32[]{:S(2)}, u32[]{:S(2)}) collective-permute-start(bf16[64,2048]{1,0:T(8,128)(2,1)S(1)} %add_convert_fusion.refs_4_), channel_id=1, source_target_pairs={{0,2},{2,4},{4,6},{6,0},{1,3},{3,5},{5,7},{7,1},{8,10},{10,12},{12... | collective-permute-start | bytes 786440 | tf_op jit(solution)/shard_map/gather/ppermute | solution.py:223
  105.8 10.8 %collective-permute-start.14 = (bf16[64,2048]{1,0:T(8,128)(2,1)S(1)}, bf16[64,2048]{1,0:T(8,128)(2,1)S(1)}, u32[]{:S(2)}, u32[]{:S(2)}) collective-permute-start(bf16[64,2048]{1,0:T(8,128)(2,1)S(1)} %add_convert_fusion.refs_4_), channel_id=1, source_target_pairs={{0,1},{1,0},{2,3},{3,2},{4,5},{5,4},{6,7},{7,6},{8,9},{9,8},{10,11... | collective-permute-start | bytes 786440 | tf_op jit(solution)/shard_map/gather/ppermute | solution.py:215
  111.1 8.8 %collective-permute-start.12 = (bf16[64,2048]{1,0:T(8,128)(2,1)S(1)}, bf16[64,2048]{1,0:T(8,128)(2,1)S(1)}, u32[]{:S(2)}, u32[]{:S(2)}) collective-permute-start(bf16[64,2048]{1,0:T(8,128)(2,1)S(1)} %add_convert_fusion.1.refs_0_), channel_id=1, source_target_pairs={{0,6},{2,0},{4,2},{6,4},{1,7},{3,1},{5,3},{7,5},{8,14},{10,8},{12,... | collective-permute-start | bytes 786440 | tf_op jit(solution)/shard_map/gather/ppermute | solution.py:223
  113.3 9.5 %collective-permute-start.11 = (bf16[64,2048]{1,0:T(8,128)(2,1)S(1)}, bf16[64,2048]{1,0:T(8,128)(2,1)S(1)}, u32[]{:S(2)}, u32[]{:S(2)}) collective-permute-start(bf16[64,2048]{1,0:T(8,128)(2,1)S(1)} %add_convert_fusion.1.refs_0_), channel_id=1, source_target_pairs={{0,2},{2,4},{4,6},{6,0},{1,3},{3,5},{5,7},{7,1},{8,10},{10,12},{12... | collective-permute-start | bytes 786440 | tf_op jit(solution)/shard_map/gather/ppermute | solution.py:223
  113.3 9.5 %collective-permute-start.10 = (bf16[64,2048]{1,0:T(8,128)(2,1)S(1)}, bf16[64,2048]{1,0:T(8,128)(2,1)S(1)}, u32[]{:S(2)}, u32[]{:S(2)}) collective-permute-start(bf16[64,2048]{1,0:T(8,128)(2,1)S(1)} %add_convert_fusion.1.refs_0_), channel_id=1, source_target_pairs={{0,1},{1,0},{2,3},{3,2},{4,5},{5,4},{6,7},{7,6},{8,9},{9,8},{10,11... | collective-permute-start | bytes 786440 | tf_op jit(solution)/shard_map/gather/ppermute | solution.py:215
  116.6 11.6 %collective-permute-start.24 = (bf16[64,2048]{1,0:T(8,128)(2,1)S(1)}, bf16[64,2048]{1,0:T(8,128)(2,1)S(1)}, u32[]{:S(2)}, u32[]{:S(2)}) collective-permute-start(bf16[64,2048]{1,0:T(8,128)(2,1)S(1)} %collective-permute-done.14.refs_5_), channel_id=1, source_target_pairs={{0,2},{2,4},{4,6},{6,0},{1,3},{3,5},{5,7},{7,1},{8,10},{10,12},{12... | collective-permute-start | bytes 786440 | tf_op jit(solution)/shard_map/gather/ppermute | solution.py:223
  116.8 13.4 %collective-permute-start.23 = (bf16[64,2048]{1,0:T(8,128)(2,1)S(1)}, bf16[64,2048]{1,0:T(8,128)(2,1)S(1)}, u32[]{:S(2)}, u32[]{:S(2)}) collective-permute-start(bf16[64,2048]{1,0:T(8,128)(2,1)S(1)} %collective-permute-done.16.refs_7_), channel_id=1, source_target_pairs={{0,6},{2,0},{4,2},{6,4},{1,7},{3,1},{5,3},{7,5},{8,14},{10,8},{12,... | collective-permute-start | bytes 786440 | tf_op jit(solution)/shard_map/gather/ppermute | solution.py:223
  119.9 10.3 %collective-permute-start.22 = (bf16[64,2048]{1,0:T(8,128)(2,1)S(1)}, bf16[64,2048]{1,0:T(8,128)(2,1)S(1)}, u32[]{:S(2)}, u32[]{:S(2)}) collective-permute-start(bf16[64,2048]{1,0:T(8,128)(2,1)S(1)} %collective-permute-done.16.refs_7_), channel_id=1, source_target_pairs={{0,1},{1,0},{2,3},{3,2},{4,5},{5,4},{6,7},{7,6},{8,9},{9,8},{10,11... | collective-permute-start | bytes 786440 | tf_op jit(solution)/shard_map/gather/ppermute | solution.py:215
  122.8 10.7 %collective-permute-start.19 = (bf16[64,2048]{1,0:T(8,128)(2,1)S(1)}, bf16[64,2048]{1,0:T(8,128)(2,1)S(1)}, u32[]{:S(2)}, u32[]{:S(2)}) collective-permute-start(bf16[64,2048]{1,0:T(8,128)(2,1)S(1)} %collective-permute-done.10.refs_1_), channel_id=1, source_target_pairs={{0,2},{2,4},{4,6},{6,0},{1,3},{3,5},{5,7},{7,1},{8,10},{10,12},{12... | collective-permute-start | bytes 786440 | tf_op jit(solution)/shard_map/gather/ppermute | solution.py:223
  122.8 10.7 %collective-permute-start.18 = (bf16[64,2048]{1,0:T(8,128)(2,1)S(1)}, bf16[64,2048]{1,0:T(8,128)(2,1)S(1)}, u32[]{:S(2)}, u32[]{:S(2)}) collective-permute-start(bf16[64,2048]{1,0:T(8,128)(2,1)S(1)} %collective-permute-done.12.refs_3_), channel_id=1, source_target_pairs={{0,6},{2,0},{4,2},{6,4},{1,7},{3,1},{5,3},{7,5},{8,14},{10,8},{12,... | collective-permute-start | bytes 786440 | tf_op jit(solution)/shard_map/gather/ppermute | solution.py:223
  128.2 6.4 %collective-permute-start.17 = (bf16[64,2048]{1,0:T(8,128)(2,1)S(1)}, bf16[64,2048]{1,0:T(8,128)(2,1)S(1)}, u32[]{:S(2)}, u32[]{:S(2)}) collective-permute-start(bf16[64,2048]{1,0:T(8,128)(2,1)S(1)} %collective-permute-done.12.refs_3_), channel_id=1, source_target_pairs={{0,1},{1,0},{2,3},{3,2},{4,5},{5,4},{6,7},{7,6},{8,9},{9,8},{10,11... | collective-permute-start | bytes 786440 | tf_op jit(solution)/shard_map/gather/ppermute | solution.py:215
  130.2 9.1 %collective-permute-start.25 = (bf16[64,1024]{1,0:T(8,128)(2,1)S(1)}, bf16[64,1024]{1,0:T(8,128)(2,1)S(1)}, u32[]{:S(2)}, u32[]{:S(2)}) collective-permute-start(bf16[64,1024]{1,0:T(8,128)(2,1)S(1)} %slice.14), channel_id=1, source_target_pairs={{0,2},{2,4},{4,6},{6,0},{1,3},{3,5},{5,7},{7,1},{8,10},{10,12},{12... | collective-permute-start | bytes 393224 | tf_op jit(solution)/shard_map/gather/ppermute | solution.py:223
  130.3 9.1 %collective-permute-start.26 = (bf16[64,1024]{1,0:T(8,128)(2,1)S(1)}, bf16[64,1024]{1,0:T(8,128)(2,1)S(1)}, u32[]{:S(2)}, u32[]{:S(2)}) collective-permute-start(bf16[64,1024]{1,0:T(8,128)(2,1)S(1)} %slice.15), channel_id=1, source_target_pairs={{0,6},{2,0},{4,2},{6,4},{1,7},{3,1},{5,3},{7,5},{8,14},{10,8},{12,... | collective-permute-start | bytes 393224 | tf_op jit(solution)/shard_map/gather/ppermute | solution.py:223
  134.6 6.3 %collective-permute-start.20 = (bf16[64,1024]{1,0:T(8,128)(2,1)S(1)}, bf16[64,1024]{1,0:T(8,128)(2,1)S(1)}, u32[]{:S(2)}, u32[]{:S(2)}) collective-permute-start(bf16[64,1024]{1,0:T(8,128)(2,1)S(1)} %slice.12), channel_id=1, source_target_pairs={{0,2},{2,4},{4,6},{6,0},{1,3},{3,5},{5,7},{7,1},{8,10},{10,12},{12... | collective-permute-start | bytes 393224 | tf_op jit(solution)/shard_map/gather/ppermute | solution.py:223
  134.7 6.2 %collective-permute-start.21 = (bf16[64,1024]{1,0:T(8,128)(2,1)S(1)}, bf16[64,1024]{1,0:T(8,128)(2,1)S(1)}, u32[]{:S(2)}, u32[]{:S(2)}) collective-permute-start(bf16[64,1024]{1,0:T(8,128)(2,1)S(1)} %slice.13), channel_id=1, source_target_pairs={{0,6},{2,0},{4,2},{6,4},{1,7},{3,1},{5,3},{7,5},{8,14},{10,8},{12,... | collective-permute-start | bytes 393224 | tf_op jit(solution)/shard_map/gather/ppermute | solution.py:223
  (2 other events, 1.8 us)

commit v8 on v7

--- a/solution.py
+++ b/solution.py
@@ -307,14 +307,17 @@
         swapped = [along_core(toward)]
     total = lax.all_to_all(total, ("block", "core"), split_axis=0, concat_axis=0, tiled=True)
     with jax.named_scope("weights"):
-        total, far, back, *swapped = lax.optimization_barrier((total, far, back, *swapped))
-        weights = (toward, along_core(back), back, swapped[0], far, along_core(far))
+        total, *swapped = lax.optimization_barrier((total, *swapped))
     with jax.named_scope("gate"):
-        gated = whole(
+        gated = list(whole(
             gate_kernel, [((quarter, channels), half16)] * 4, [VMEM] * 2, [VMEM] * 4, [square]
-        )(total, query_branch)
+        )(total, query_branch))
     with jax.named_scope("quarters"):
         others = mirrored(gated[1], 1), mirrored(gated[2], -1), along_y(gated[3], 2)
+    with jax.named_scope("weights"):
+        swapped_back = along_core(back)
+        gated[0], far = lax.optimization_barrier((gated[0], far))
+        weights = (toward, swapped_back, back, swapped[0], far, along_core(far))
     cost = quarter * channels * features
     with jax.named_scope("own"):
         (partial_value,) = whole(

time: 145 us -> 144 us (level)
  waiting for transfers between devices: 64.5 us -> 62.5 us
  transfers between devices with their start and end apart: 29 -> 29, of which waited for: 13 -> 12; matrix products, arithmetic and copies ran while one was open for 0% -> 0% of each run, Pallas kernels for 8% -> 9%
where the time goes in v8:
time: 144 us; the launch traced here: 142 us
  waiting for transfers between devices  62.5 us (43%)
  starting transfers between devices  51.5 us (36%)
  Pallas kernels  21.8 us (15%)
  local copies, waits for them, and re-layouts  5.48 us (4%)
    all_to_all x1, waiting for transfers between devices, body(): lax.all_to_all(outgoing, ('block', 'core'), split_axis=0, concat_axis=0,...  26.4 us
    ppermute x13, starting transfers between devices, along_y(): lax.ppermute(value, 'y', [(i, (i + steps) % count) for i in range(count)])  18.6 us
    all_to_all x1, waiting for transfers between devices, body(): lax.all_to_all(total, ('block', 'core'), split_axis=0, concat_axis=0, til...  16.1 us
    all_to_all x1, starting transfers between devices, body(): lax.all_to_all(outgoing, ('block', 'core'), split_axis=0, concat_axis=0,...  12.2 us
    pallas_call x2, Pallas kernels, body(): whole(functools.partial(rest_kernel, stream * width), [((quarter // 2, wi...  9.16 us
    ppermute x9, starting transfers between devices, swap(): return lambda value: lax.ppermute(value, axis, [(0, 1), (1, 0)])  8.16 us
    ppermute x5, starting transfers between devices, mirrored(): return lax.ppermute(value, ('core', 'y'), pairs)  7.01 us
    ppermute x5, waiting for transfers between devices, mirrored(): return lax.ppermute(value, ('core', 'y'), pairs)  6.88 us
  transfers between devices with their start and end apart: 29, of which 12 were waited for; matrix products, arithmetic and copies ran while one was open for 0% of the time, Pallas kernels for 9%

profile of v8, /device:TPU:2, one launch (start us, length us, event | category | flops | bytes accessed | tf_op | source)
XLA Modules:
  0.0 141.8 jit_solution(9653277540805535532)
XLA Ops:
  0.0 3.2 %pack.1 = (bf16[32,32,512]{2,1,0:T(8,128)(2,1)}, bf16[256,4096]{1,0:T(8,128)(2,1)}) custom-call(bf16[512,512]{1,0:T(8,128)(2,1)} %key_hbm.1, bf16[512,512]{1,0:T(8,128)(2,1)} %value_hbm.1, bf16[512,512]{1,0:T(8,128)(2,1)} %filter_hbm.1, bf16[512,4096]{1,0:T(8,128)(2,1)} %weight_ref.1), custom_call_target="tpu_custom_call" | custom-call | bytes 8388608 | tf_op jit(solution)/shard_map/pack/pallas_call | solution.py:276
  3.2 1.7 %collective-permute-start = (bf16[256,4096]{1,0:T(8,128)(2,1)}, bf16[256,4096]{1,0:T(8,128)(2,1)S(1)}, u32[]{:S(2)}, u32[]{:S(2)}) collective-permute-start(bf16[256,4096]{1,0:T(8,128)(2,1)} %get-tuple-element.34), channel_id=1, source_target_pairs={{0,2},{2,4},{4,6},{6,0},{8,14},{10,8},{12,10},{14,12},{1,3},{3,5},... | collective-permute-start | bytes 6291464 | tf_op jit(solution)/shard_map/weights/ppermute | solution.py:233
  4.9 12.2 %all-to-all-start = ((bf16[32,32,512]{2,1,0:T(8,128)(2,1)}), bf16[32,32,512]{2,1,0:T(8,128)(2,1)S(1)}, u32[]{:S(2)}, u32[]{:S(2)}) async-start(bf16[32,32,512]{2,1,0:T(8,128)(2,1)} %get-tuple-element.33), calls=%async_computation | async-start | bytes 2097152 | tf_op jit(solution)/shard_map/all_to_all | solution.py:293
  17.1 1.1 collective-permute-start.6
  18.4 26.4 %all-to-all-done.signal_ref = bf16[32,32,512]{2,1,0:T(8,128)(2,1)S(1)} async-done(((bf16[32,32,512]{2,1,0:T(8,128)(2,1)}), bf16[32,32,512]{2,1,0:T(8,128)(2,1)S(1)}, u32[]{:S(2)}, u32[]{:S(2)}) %all-to-all-start) | async-done | bytes 1048608 | tf_op jit(solution)/shard_map/all_to_all | solution.py:293
  44.8 1.2 copy-done.3
  46.0 5.7 %conv.1 = bf16[32,16,512]{2,1,0:T(8,128)(2,1)S(1)} custom-call(bf16[32,32,512]{2,1,0:T(8,128)(2,1)S(1)} %all-to-all-done.signal_ref, f32[16,1]{1,0:T(8,128)S(1)} %copy.9.gain_ref, bf16[512,1024]{1,0:T(8,128)(2,1)S(1)} %copy-done.3), custom_call_target="tpu_custom_call" | custom-call | bytes 8388608 | tf_op jit(solution)/shard_map/conv/pallas_call | solution.py:296
  54.4 5.6 %all-to-all-start.1 = ((bf16[32,16,512]{2,1,0:T(8,128)(2,1)}), bf16[32,16,512]{2,1,0:T(8,128)(2,1)S(1)}, u32[]{:S(2)}, u32[]{:S(2)}) async-start(bf16[32,16,512]{2,1,0:T(8,128)(2,1)} %copy-done.2), calls=%async_computation.1 | async-start | bytes 1048576 | tf_op jit(solution)/shard_map/all_to_all | solution.py:308
  60.3 16.1 %all-to-all-done.1.total_ref = bf16[32,16,512]{2,1,0:T(8,128)(2,1)S(1)} async-done(((bf16[32,16,512]{2,1,0:T(8,128)(2,1)}), bf16[32,16,512]{2,1,0:T(8,128)(2,1)S(1)}, u32[]{:S(2)}, u32[]{:S(2)}) %all-to-all-start.1) | async-done | bytes 524320 | tf_op jit(solution)/shard_map/all_to_all | solution.py:308
  76.4 1.0 copy-done.4
  77.7 3.1 %collective-permute-done.2.refs_7_ = bf16[256,4096]{1,0:T(8,128)(2,1)} collective-permute-done((bf16[256,4096]{1,0:T(8,128)(2,1)S(1)}, bf16[256,4096]{1,0:T(8,128)(2,1)}, u32[]{:S(2)}, u32[]{:S(2)}) %collective-permute-start.2) | collective-permute-done | bytes 2097184 | tf_op jit(solution)/shard_map/weights/ppermute | solution.py:233
  80.8 3.2 %collective-permute-start.4 = (bf16[128,512]{1,0:T(8,128)(2,1)S(1)}, bf16[128,512]{1,0:T(8,128)(2,1)S(1)}, u32[]{:S(2)}, u32[]{:S(2)}) collective-permute-start(bf16[128,512]{1,0:T(8,128)(2,1)S(1)} %get-tuple-element.41), channel_id=1, source_target_pairs={{0,6},{2,0},{4,2},{6,4},{8,10},{10,12},{12,14},{14,8},{1,7},{3,1},... | collective-permute-start | bytes 393224 | tf_op jit(solution)/shard_map/quarters/ppermute | solution.py:233
  84.0 2.2 %copy-done.1 = bf16[512,4096]{1,0:T(8,128)(2,1)S(1)} copy-done((bf16[512,4096]{1,0:T(8,128)(2,1)S(1)}, bf16[512,4096]{1,0:T(8,128)(2,1)}, u32[]{:S(2)}) %copy-start.1) | copy-done | bytes 4194328
  87.0 3.8 %collective-permute-done.3.refs_0_ = bf16[128,512]{1,0:T(8,128)(2,1)S(1)} collective-permute-done((bf16[128,512]{1,0:T(8,128)(2,1)S(1)}, bf16[128,512]{1,0:T(8,128)(2,1)S(1)}, u32[]{:S(2)}, u32[]{:S(2)}) %collective-permute-start.3) | collective-permute-done | bytes 131104 | tf_op jit(solution)/shard_map/quarters/ppermute | solution.py:233
  90.7 4.6 %rest.3 = (bf16[64,2048]{1,0:T(8,128)(2,1)S(1)}, bf16[64,2048]{1,0:T(8,128)(2,1)S(1)}) custom-call(f32[128,4096]{1,0:T(8,128)S(1)} %own.1.partial_ref, bf16[128,512]{1,0:T(8,128)(2,1)S(1)} %collective-permute-done.3.refs_0_, bf16[128,512]{1,0:T(8,128)(2,1)S(1)} %collective-permute-done.4.refs_1_, bf16[128,512]{1,0:T(8,128)(2,1)S(1)} %collective-permute-done.5.refs_2_, ...), custom_call_target="tpu_custom_call" | custom-call | flops 536870912 | bytes 8388608 | tf_op jit(solution)/shard_map/rest/pallas_call | solution.py:329
  95.3 1.4 %collective-permute-start.13 = (bf16[64,2048]{1,0:T(8,128)(2,1)S(1)}, bf16[64,2048]{1,0:T(8,128)(2,1)S(1)}, u32[]{:S(2)}, u32[]{:S(2)}) collective-permute-start(bf16[64,2048]{1,0:T(8,128)(2,1)S(1)} %get-tuple-element.51), channel_id=1, source_target_pairs={{0,1},{1,0},{2,3},{3,2},{4,5},{5,4},{6,7},{7,6},{8,9},{9,8},{10,11... | collective-permute-start | bytes 786440 | tf_op jit(solution)/shard_map/gather/ppermute | solution.py:215
  96.7 4.6 %rest.2 = (bf16[64,2048]{1,0:T(8,128)(2,1)S(1)}, bf16[64,2048]{1,0:T(8,128)(2,1)S(1)}) custom-call(f32[128,4096]{1,0:T(8,128)S(1)} %own.1.partial_ref, bf16[128,512]{1,0:T(8,128)(2,1)S(1)} %collective-permute-done.3.refs_0_, bf16[128,512]{1,0:T(8,128)(2,1)S(1)} %collective-permute-done.4.refs_1_, bf16[128,512]{1,0:T(8,128)(2,1)S(1)} %collective-permute-done.5.refs_2_, ...), custom_call_target="tpu_custom_call" | custom-call | flops 536870912 | bytes 8388608 | tf_op jit(solution)/shard_map/rest/pallas_call | solution.py:329
  102.2 2.8 %collective-permute-start.16 = (bf16[64,2048]{1,0:T(8,128)(2,1)S(1)}, bf16[64,2048]{1,0:T(8,128)(2,1)S(1)}, u32[]{:S(2)}, u32[]{:S(2)}) collective-permute-start(bf16[64,2048]{1,0:T(8,128)(2,1)S(1)} %add_convert_fusion.refs_4_), channel_id=1, source_target_pairs={{0,6},{2,0},{4,2},{6,4},{1,7},{3,1},{5,3},{7,5},{8,14},{10,8},{12,... | collective-permute-start | bytes 786440 | tf_op jit(solution)/shard_map/gather/ppermute | solution.py:223
  105.0 1.7 %collective-permute-start.14 = (bf16[64,2048]{1,0:T(8,128)(2,1)S(1)}, bf16[64,2048]{1,0:T(8,128)(2,1)S(1)}, u32[]{:S(2)}, u32[]{:S(2)}) collective-permute-start(bf16[64,2048]{1,0:T(8,128)(2,1)S(1)} %add_convert_fusion.refs_4_), channel_id=1, source_target_pairs={{0,1},{1,0},{2,3},{3,2},{4,5},{5,4},{6,7},{7,6},{8,9},{9,8},{10,11... | collective-permute-start | bytes 786440 | tf_op jit(solution)/shard_map/gather/ppermute | solution.py:215
  106.7 3.5 %collective-permute-done.9 = bf16[64,2048]{1,0:T(8,128)(2,1)S(1)} collective-permute-done((bf16[64,2048]{1,0:T(8,128)(2,1)S(1)}, bf16[64,2048]{1,0:T(8,128)(2,1)S(1)}, u32[]{:S(2)}, u32[]{:S(2)}) %collective-permute-start.9) | collective-permute-done | bytes 262176 | tf_op jit(solution)/shard_map/gather/ppermute | solution.py:215
  110.3 2.6 %collective-permute-start.12 = (bf16[64,2048]{1,0:T(8,128)(2,1)S(1)}, bf16[64,2048]{1,0:T(8,128)(2,1)S(1)}, u32[]{:S(2)}, u32[]{:S(2)}) collective-permute-start(bf16[64,2048]{1,0:T(8,128)(2,1)S(1)} %add_convert_fusion.1.refs_0_), channel_id=1, source_target_pairs={{0,6},{2,0},{4,2},{6,4},{1,7},{3,1},{5,3},{7,5},{8,14},{10,8},{12,... | collective-permute-start | bytes 786440 | tf_op jit(solution)/shard_map/gather/ppermute | solution.py:223
  113.8 2.1 %collective-permute-done.14.refs_5_ = bf16[64,2048]{1,0:T(8,128)(2,1)S(1)} collective-permute-done((bf16[64,2048]{1,0:T(8,128)(2,1)S(1)}, bf16[64,2048]{1,0:T(8,128)(2,1)S(1)}, u32[]{:S(2)}, u32[]{:S(2)}) %collective-permute-start.14) | collective-permute-done | bytes 262176 | tf_op jit(solution)/shard_map/gather/ppermute | solution.py:215
  116.2 2.9 %collective-permute-start.23 = (bf16[64,2048]{1,0:T(8,128)(2,1)S(1)}, bf16[64,2048]{1,0:T(8,128)(2,1)S(1)}, u32[]{:S(2)}, u32[]{:S(2)}) collective-permute-start(bf16[64,2048]{1,0:T(8,128)(2,1)S(1)} %collective-permute-done.16.refs_7_), channel_id=1, source_target_pairs={{0,6},{2,0},{4,2},{6,4},{1,7},{3,1},{5,3},{7,5},{8,14},{10,8},{12,... | collective-permute-start | bytes 786440 | tf_op jit(solution)/shard_map/gather/ppermute | solution.py:223
  119.7 2.1 %collective-permute-done.11.refs_2_ = bf16[64,2048]{1,0:T(8,128)(2,1)S(1)} collective-permute-done((bf16[64,2048]{1,0:T(8,128)(2,1)S(1)}, bf16[64,2048]{1,0:T(8,128)(2,1)S(1)}, u32[]{:S(2)}, u32[]{:S(2)}) %collective-permute-start.11) | collective-permute-done | bytes 262176 | tf_op jit(solution)/shard_map/gather/ppermute | solution.py:223
  122.0 3.2 %collective-permute-start.18 = (bf16[64,2048]{1,0:T(8,128)(2,1)S(1)}, bf16[64,2048]{1,0:T(8,128)(2,1)S(1)}, u32[]{:S(2)}, u32[]{:S(2)}) collective-permute-start(bf16[64,2048]{1,0:T(8,128)(2,1)S(1)} %collective-permute-done.12.refs_3_), channel_id=1, source_target_pairs={{0,6},{2,0},{4,2},{6,4},{1,7},{3,1},{5,3},{7,5},{8,14},{10,8},{12,... | collective-permute-start | bytes 786440 | tf_op jit(solution)/shard_map/gather/ppermute | solution.py:223
  125.2 2.2 %collective-permute-done.24.refs_8_ = bf16[64,2048]{1,0:T(8,128)(2,1)S(1)} collective-permute-done((bf16[64,2048]{1,0:T(8,128)(2,1)S(1)}, bf16[64,2048]{1,0:T(8,128)(2,1)S(1)}, u32[]{:S(2)}, u32[]{:S(2)}) %collective-permute-start.24) | collective-permute-done | bytes 262176 | tf_op jit(solution)/shard_map/gather/ppermute | solution.py:223
  127.4 2.2 %collective-permute-start.17 = (bf16[64,2048]{1,0:T(8,128)(2,1)S(1)}, bf16[64,2048]{1,0:T(8,128)(2,1)S(1)}, u32[]{:S(2)}, u32[]{:S(2)}) collective-permute-start(bf16[64,2048]{1,0:T(8,128)(2,1)S(1)} %collective-permute-done.12.refs_3_), channel_id=1, source_target_pairs={{0,1},{1,0},{2,3},{3,2},{4,5},{5,4},{6,7},{7,6},{8,9},{9,8},{10,11... | collective-permute-start | bytes 786440 | tf_op jit(solution)/shard_map/gather/ppermute | solution.py:215
  129.7 3.2 %collective-permute-start.26 = (bf16[64,1024]{1,0:T(8,128)(2,1)S(1)}, bf16[64,1024]{1,0:T(8,128)(2,1)S(1)}, u32[]{:S(2)}, u32[]{:S(2)}) collective-permute-start(bf16[64,1024]{1,0:T(8,128)(2,1)S(1)} %slice.15), channel_id=1, source_target_pairs={{0,6},{2,0},{4,2},{6,4},{1,7},{3,1},{5,3},{7,5},{8,14},{10,8},{12,... | collective-permute-start | bytes 393224 | tf_op jit(solution)/shard_map/gather/ppermute | solution.py:223
  134.1 3.2 %collective-permute-start.21 = (bf16[64,1024]{1,0:T(8,128)(2,1)S(1)}, bf16[64,1024]{1,0:T(8,128)(2,1)S(1)}, u32[]{:S(2)}, u32[]{:S(2)}) collective-permute-start(bf16[64,1024]{1,0:T(8,128)(2,1)S(1)} %slice.13), channel_id=1, source_target_pairs={{0,6},{2,0},{4,2},{6,4},{1,7},{3,1},{5,3},{7,5},{8,14},{10,8},{12,... | collective-permute-start | bytes 393224 | tf_op jit(solution)/shard_map/gather/ppermute | solution.py:223
  137.3 1.4 gather.2.refs_0_
  138.7 1.5 %collective-permute-done.20.refs_4_ = bf16[64,1024]{1,0:T(8,128)(2,1)S(1)} collective-permute-done((bf16[64,1024]{1,0:T(8,128)(2,1)S(1)}, bf16[64,1024]{1,0:T(8,128)(2,1)S(1)}, u32[]{:S(2)}, u32[]{:S(2)}) %collective-permute-start.20) | collective-permute-done | bytes 131104 | tf_op jit(solution)/shard_map/gather/ppermute | solution.py:223
  140.2 1.4 gather.3
  (52 shorter events, 8.1 us)
Async XLA Ops:
  0.0 18.2 %copy-start = (f32[512]{0:T(512)S(1)}, f32[512]{0:T(512)}, u32[]{:S(2)}) copy-start(f32[512]{0:T(512)} %param.11) | copy-start | bytes 6148
  3.2 49.3 %collective-permute-start = (bf16[256,4096]{1,0:T(8,128)(2,1)}, bf16[256,4096]{1,0:T(8,128)(2,1)S(1)}, u32[]{:S(2)}, u32[]{:S(2)}) collective-permute-start(bf16[256,4096]{1,0:T(8,128)(2,1)} %get-tuple-element.34), channel_id=1, source_target_pairs={{0,2},{2,4},{4,6},{6,0},{8,14},{10,8},{12,10},{14,12},{1,3},{3,5},... | collective-permute-start | bytes 6291464 | tf_op jit(solution)/shard_map/weights/ppermute | solution.py:233
  4.9 39.9 %all-to-all-start = ((bf16[32,32,512]{2,1,0:T(8,128)(2,1)}), bf16[32,32,512]{2,1,0:T(8,128)(2,1)S(1)}, u32[]{:S(2)}, u32[]{:S(2)}) async-start(bf16[32,32,512]{2,1,0:T(8,128)(2,1)} %get-tuple-element.33), calls=%async_computation | async-start | bytes 2097152 | tf_op jit(solution)/shard_map/all_to_all | solution.py:293
  17.1 43.0 %collective-permute-start.6 = (bf16[256,4096]{1,0:T(8,128)(2,1)}, bf16[256,4096]{1,0:T(8,128)(2,1)}, u32[]{:S(2)}, u32[]{:S(2)}) collective-permute-start(bf16[256,4096]{1,0:T(8,128)(2,1)} %get-tuple-element.34), channel_id=1, source_target_pairs={{0,6},{2,0},{4,2},{6,4},{8,10},{10,12},{12,14},{14,8},{1,7},{3,1},... | collective-permute-start | bytes 6291464 | tf_op jit(solution)/shard_map/weights/ppermute | solution.py:233
  44.7 1.2 copy-start.3
  52.5 23.8 %collective-permute-start.1 = (bf16[256,4096]{1,0:T(8,128)(2,1)S(1)}, bf16[256,4096]{1,0:T(8,128)(2,1)}, u32[]{:S(2)}, u32[]{:S(2)}) collective-permute-start(bf16[256,4096]{1,0:T(8,128)(2,1)S(1)} %collective-permute-done.refs_3_), channel_id=1, source_target_pairs={{0,8},{8,0},{1,9},{9,1},{2,10},{10,2},{3,11},{11,3},{4,12},{12,4},... | collective-permute-start | bytes 6291464 | tf_op jit(solution)/shard_map/weights/ppermute | solution.py:215
  53.4 27.4 %collective-permute-start.2 = (bf16[256,4096]{1,0:T(8,128)(2,1)S(1)}, bf16[256,4096]{1,0:T(8,128)(2,1)}, u32[]{:S(2)}, u32[]{:S(2)}) collective-permute-start(bf16[256,4096]{1,0:T(8,128)(2,1)S(1)} %collective-permute-done.refs_3_), channel_id=1, source_target_pairs={{0,2},{2,4},{4,6},{6,0},{8,14},{10,8},{12,10},{14,12},{1,3},{3,5},... | collective-permute-start | bytes 6291464 | tf_op jit(solution)/shard_map/weights/ppermute | solution.py:233
  54.4 22.0 %all-to-all-start.1 = ((bf16[32,16,512]{2,1,0:T(8,128)(2,1)}), bf16[32,16,512]{2,1,0:T(8,128)(2,1)S(1)}, u32[]{:S(2)}, u32[]{:S(2)}) async-start(bf16[32,16,512]{2,1,0:T(8,128)(2,1)} %copy-done.2), calls=%async_computation.1 | async-start | bytes 1048576 | tf_op jit(solution)/shard_map/all_to_all | solution.py:308
  60.1 26.9 %collective-permute-start.7 = (bf16[256,4096]{1,0:T(8,128)(2,1)}, bf16[256,4096]{1,0:T(8,128)(2,1)}, u32[]{:S(2)}, u32[]{:S(2)}) collective-permute-start(bf16[256,4096]{1,0:T(8,128)(2,1)} %collective-permute-done.6.refs_5_), channel_id=1, source_target_pairs={{0,8},{8,0},{1,9},{9,1},{2,10},{10,2},{3,11},{11,3},{4,12},{12,4},... | collective-permute-start | bytes 6291464 | tf_op jit(solution)/shard_map/weights/ppermute | solution.py:215
  80.8 9.9 %collective-permute-start.8 = (bf16[256,4096]{1,0:T(8,128)(2,1)}, bf16[256,4096]{1,0:T(8,128)(2,1)S(1)}, u32[]{:S(2)}, u32[]{:S(2)}) collective-permute-start(bf16[256,4096]{1,0:T(8,128)(2,1)} %collective-permute-done.2.refs_7_), channel_id=1, source_target_pairs={{0,8},{8,0},{1,9},{9,1},{2,10},{10,2},{3,11},{11,3},{4,12},{12,4},... | collective-permute-start | bytes 6291464 | tf_op jit(solution)/shard_map/weights/ppermute | solution.py:215
  80.8 9.9 %collective-permute-start.3 = (bf16[128,512]{1,0:T(8,128)(2,1)S(1)}, bf16[128,512]{1,0:T(8,128)(2,1)S(1)}, u32[]{:S(2)}, u32[]{:S(2)}) collective-permute-start(bf16[128,512]{1,0:T(8,128)(2,1)S(1)} %get-tuple-element.40), channel_id=1, source_target_pairs={{0,2},{2,4},{4,6},{6,0},{8,14},{10,8},{12,10},{14,12},{1,3},{3,5},... | collective-permute-start | bytes 393224 | tf_op jit(solution)/shard_map/quarters/ppermute | solution.py:233
  80.8 9.9 %collective-permute-start.4 = (bf16[128,512]{1,0:T(8,128)(2,1)S(1)}, bf16[128,512]{1,0:T(8,128)(2,1)S(1)}, u32[]{:S(2)}, u32[]{:S(2)}) collective-permute-start(bf16[128,512]{1,0:T(8,128)(2,1)S(1)} %get-tuple-element.41), channel_id=1, source_target_pairs={{0,6},{2,0},{4,2},{6,4},{8,10},{10,12},{12,14},{14,8},{1,7},{3,1},... | collective-permute-start | bytes 393224 | tf_op jit(solution)/shard_map/quarters/ppermute | solution.py:233
  84.0 6.7 %collective-permute-start.5 = (bf16[128,512]{1,0:T(8,128)(2,1)S(1)}, bf16[128,512]{1,0:T(8,128)(2,1)S(1)}, u32[]{:S(2)}, u32[]{:S(2)}) collective-permute-start(bf16[128,512]{1,0:T(8,128)(2,1)S(1)} %get-tuple-element.42), channel_id=1, source_target_pairs={{0,4},{2,6},{4,0},{6,2},{1,5},{3,7},{5,1},{7,3},{8,12},{10,14},{12... | collective-permute-start | bytes 393224 | tf_op jit(solution)/shard_map/quarters/ppermute | solution.py:223
  84.0 2.2 %copy-start.1 = (bf16[512,4096]{1,0:T(8,128)(2,1)S(1)}, bf16[512,4096]{1,0:T(8,128)(2,1)}, u32[]{:S(2)}) copy-start(bf16[512,4096]{1,0:T(8,128)(2,1)} %weight_ref.1) | copy-start | bytes 12582916
  95.3 6.8 %collective-permute-start.13 = (bf16[64,2048]{1,0:T(8,128)(2,1)S(1)}, bf16[64,2048]{1,0:T(8,128)(2,1)S(1)}, u32[]{:S(2)}, u32[]{:S(2)}) collective-permute-start(bf16[64,2048]{1,0:T(8,128)(2,1)S(1)} %get-tuple-element.51), channel_id=1, source_target_pairs={{0,1},{1,0},{2,3},{3,2},{4,5},{5,4},{6,7},{7,6},{8,9},{9,8},{10,11... | collective-permute-start | bytes 786440 | tf_op jit(solution)/shard_map/gather/ppermute | solution.py:215
  101.3 8.9 %collective-permute-start.9 = (bf16[64,2048]{1,0:T(8,128)(2,1)S(1)}, bf16[64,2048]{1,0:T(8,128)(2,1)S(1)}, u32[]{:S(2)}, u32[]{:S(2)}) collective-permute-start(bf16[64,2048]{1,0:T(8,128)(2,1)S(1)} %get-tuple-element.46), channel_id=1, source_target_pairs={{0,1},{1,0},{2,3},{3,2},{4,5},{5,4},{6,7},{7,6},{8,9},{9,8},{10,11... | collective-permute-start | bytes 786440 | tf_op jit(solution)/shard_map/gather/ppermute | solution.py:215
  102.2 10.8 %collective-permute-start.16 = (bf16[64,2048]{1,0:T(8,128)(2,1)S(1)}, bf16[64,2048]{1,0:T(8,128)(2,1)S(1)}, u32[]{:S(2)}, u32[]{:S(2)}) collective-permute-start(bf16[64,2048]{1,0:T(8,128)(2,1)S(1)} %add_convert_fusion.refs_4_), channel_id=1, source_target_pairs={{0,6},{2,0},{4,2},{6,4},{1,7},{3,1},{5,3},{7,5},{8,14},{10,8},{12,... | collective-permute-start | bytes 786440 | tf_op jit(solution)/shard_map/gather/ppermute | solution.py:223
  105.0 8.8 %collective-permute-start.15 = (bf16[64,2048]{1,0:T(8,128)(2,1)S(1)}, bf16[64,2048]{1,0:T(8,128)(2,1)S(1)}, u32[]{:S(2)}, u32[]{:S(2)}) collective-permute-start(bf16[64,2048]{1,0:T(8,128)(2,1)S(1)} %add_convert_fusion.refs_4_), channel_id=1, source_target_pairs={{0,2},{2,4},{4,6},{6,0},{1,3},{3,5},{5,7},{7,1},{8,10},{10,12},{12... | collective-permute-start | bytes 786440 | tf_op jit(solution)/shard_map/gather/ppermute | solution.py:223
  105.0 10.9 %collective-permute-start.14 = (bf16[64,2048]{1,0:T(8,128)(2,1)S(1)}, bf16[64,2048]{1,0:T(8,128)(2,1)S(1)}, u32[]{:S(2)}, u32[]{:S(2)}) collective-permute-start(bf16[64,2048]{1,0:T(8,128)(2,1)S(1)} %add_convert_fusion.refs_4_), channel_id=1, source_target_pairs={{0,1},{1,0},{2,3},{3,2},{4,5},{5,4},{6,7},{7,6},{8,9},{9,8},{10,11... | collective-permute-start | bytes 786440 | tf_op jit(solution)/shard_map/gather/ppermute | solution.py:215
  110.3 9.3 %collective-permute-start.12 = (bf16[64,2048]{1,0:T(8,128)(2,1)S(1)}, bf16[64,2048]{1,0:T(8,128)(2,1)S(1)}, u32[]{:S(2)}, u32[]{:S(2)}) collective-permute-start(bf16[64,2048]{1,0:T(8,128)(2,1)S(1)} %add_convert_fusion.1.refs_0_), channel_id=1, source_target_pairs={{0,6},{2,0},{4,2},{6,4},{1,7},{3,1},{5,3},{7,5},{8,14},{10,8},{12,... | collective-permute-start | bytes 786440 | tf_op jit(solution)/shard_map/gather/ppermute | solution.py:223
  113.0 8.8 %collective-permute-start.11 = (bf16[64,2048]{1,0:T(8,128)(2,1)S(1)}, bf16[64,2048]{1,0:T(8,128)(2,1)S(1)}, u32[]{:S(2)}, u32[]{:S(2)}) collective-permute-start(bf16[64,2048]{1,0:T(8,128)(2,1)S(1)} %add_convert_fusion.1.refs_0_), channel_id=1, source_target_pairs={{0,2},{2,4},{4,6},{6,0},{1,3},{3,5},{5,7},{7,1},{8,10},{10,12},{12... | collective-permute-start | bytes 786440 | tf_op jit(solution)/shard_map/gather/ppermute | solution.py:223
  113.0 9.0 %collective-permute-start.10 = (bf16[64,2048]{1,0:T(8,128)(2,1)S(1)}, bf16[64,2048]{1,0:T(8,128)(2,1)S(1)}, u32[]{:S(2)}, u32[]{:S(2)}) collective-permute-start(bf16[64,2048]{1,0:T(8,128)(2,1)S(1)} %add_convert_fusion.1.refs_0_), channel_id=1, source_target_pairs={{0,1},{1,0},{2,3},{3,2},{4,5},{5,4},{6,7},{7,6},{8,9},{9,8},{10,11... | collective-permute-start | bytes 786440 | tf_op jit(solution)/shard_map/gather/ppermute | solution.py:215
  115.9 11.5 %collective-permute-start.24 = (bf16[64,2048]{1,0:T(8,128)(2,1)S(1)}, bf16[64,2048]{1,0:T(8,128)(2,1)S(1)}, u32[]{:S(2)}, u32[]{:S(2)}) collective-permute-start(bf16[64,2048]{1,0:T(8,128)(2,1)S(1)} %collective-permute-done.14.refs_5_), channel_id=1, source_target_pairs={{0,2},{2,4},{4,6},{6,0},{1,3},{3,5},{5,7},{7,1},{8,10},{10,12},{12... | collective-permute-start | bytes 786440 | tf_op jit(solution)/shard_map/gather/ppermute | solution.py:223
  116.2 13.4 %collective-permute-start.23 = (bf16[64,2048]{1,0:T(8,128)(2,1)S(1)}, bf16[64,2048]{1,0:T(8,128)(2,1)S(1)}, u32[]{:S(2)}, u32[]{:S(2)}) collective-permute-start(bf16[64,2048]{1,0:T(8,128)(2,1)S(1)} %collective-permute-done.16.refs_7_), channel_id=1, source_target_pairs={{0,6},{2,0},{4,2},{6,4},{1,7},{3,1},{5,3},{7,5},{8,14},{10,8},{12,... | collective-permute-start | bytes 786440 | tf_op jit(solution)/shard_map/gather/ppermute | solution.py:223
  119.6 10.0 %collective-permute-start.22 = (bf16[64,2048]{1,0:T(8,128)(2,1)S(1)}, bf16[64,2048]{1,0:T(8,128)(2,1)S(1)}, u32[]{:S(2)}, u32[]{:S(2)}) collective-permute-start(bf16[64,2048]{1,0:T(8,128)(2,1)S(1)} %collective-permute-done.16.refs_7_), channel_id=1, source_target_pairs={{0,1},{1,0},{2,3},{3,2},{4,5},{5,4},{6,7},{7,6},{8,9},{9,8},{10,11... | collective-permute-start | bytes 786440 | tf_op jit(solution)/shard_map/gather/ppermute | solution.py:215
  121.9 11.0 %collective-permute-start.19 = (bf16[64,2048]{1,0:T(8,128)(2,1)S(1)}, bf16[64,2048]{1,0:T(8,128)(2,1)S(1)}, u32[]{:S(2)}, u32[]{:S(2)}) collective-permute-start(bf16[64,2048]{1,0:T(8,128)(2,1)S(1)} %collective-permute-done.10.refs_1_), channel_id=1, source_target_pairs={{0,2},{2,4},{4,6},{6,0},{1,3},{3,5},{5,7},{7,1},{8,10},{10,12},{12... | collective-permute-start | bytes 786440 | tf_op jit(solution)/shard_map/gather/ppermute | solution.py:223
  122.0 11.0 %collective-permute-start.18 = (bf16[64,2048]{1,0:T(8,128)(2,1)S(1)}, bf16[64,2048]{1,0:T(8,128)(2,1)S(1)}, u32[]{:S(2)}, u32[]{:S(2)}) collective-permute-start(bf16[64,2048]{1,0:T(8,128)(2,1)S(1)} %collective-permute-done.12.refs_3_), channel_id=1, source_target_pairs={{0,6},{2,0},{4,2},{6,4},{1,7},{3,1},{5,3},{7,5},{8,14},{10,8},{12,... | collective-permute-start | bytes 786440 | tf_op jit(solution)/shard_map/gather/ppermute | solution.py:223
  127.4 6.5 %collective-permute-start.17 = (bf16[64,2048]{1,0:T(8,128)(2,1)S(1)}, bf16[64,2048]{1,0:T(8,128)(2,1)S(1)}, u32[]{:S(2)}, u32[]{:S(2)}) collective-permute-start(bf16[64,2048]{1,0:T(8,128)(2,1)S(1)} %collective-permute-done.12.refs_3_), channel_id=1, source_target_pairs={{0,1},{1,0},{2,3},{3,2},{4,5},{5,4},{6,7},{7,6},{8,9},{9,8},{10,11... | collective-permute-start | bytes 786440 | tf_op jit(solution)/shard_map/gather/ppermute | solution.py:215
  129.6 9.0 %collective-permute-start.25 = (bf16[64,1024]{1,0:T(8,128)(2,1)S(1)}, bf16[64,1024]{1,0:T(8,128)(2,1)S(1)}, u32[]{:S(2)}, u32[]{:S(2)}) collective-permute-start(bf16[64,1024]{1,0:T(8,128)(2,1)S(1)} %slice.14), channel_id=1, source_target_pairs={{0,2},{2,4},{4,6},{6,0},{1,3},{3,5},{5,7},{7,1},{8,10},{10,12},{12... | collective-permute-start | bytes 393224 | tf_op jit(solution)/shard_map/gather/ppermute | solution.py:223
  129.7 9.0 %collective-permute-start.26 = (bf16[64,1024]{1,0:T(8,128)(2,1)S(1)}, bf16[64,1024]{1,0:T(8,128)(2,1)S(1)}, u32[]{:S(2)}, u32[]{:S(2)}) collective-permute-start(bf16[64,1024]{1,0:T(8,128)(2,1)S(1)} %slice.15), channel_id=1, source_target_pairs={{0,6},{2,0},{4,2},{6,4},{1,7},{3,1},{5,3},{7,5},{8,14},{10,8},{12,... | collective-permute-start | bytes 393224 | tf_op jit(solution)/shard_map/gather/ppermute | solution.py:223
  134.0 6.3 %collective-permute-start.20 = (bf16[64,1024]{1,0:T(8,128)(2,1)S(1)}, bf16[64,1024]{1,0:T(8,128)(2,1)S(1)}, u32[]{:S(2)}, u32[]{:S(2)}) collective-permute-start(bf16[64,1024]{1,0:T(8,128)(2,1)S(1)} %slice.12), channel_id=1, source_target_pairs={{0,2},{2,4},{4,6},{6,0},{1,3},{3,5},{5,7},{7,1},{8,10},{10,12},{12... | collective-permute-start | bytes 393224 | tf_op jit(solution)/shard_map/gather/ppermute | solution.py:223
  134.1 6.2 %collective-permute-start.21 = (bf16[64,1024]{1,0:T(8,128)(2,1)S(1)}, bf16[64,1024]{1,0:T(8,128)(2,1)S(1)}, u32[]{:S(2)}, u32[]{:S(2)}) collective-permute-start(bf16[64,1024]{1,0:T(8,128)(2,1)S(1)} %slice.13), channel_id=1, source_target_pairs={{0,6},{2,0},{4,2},{6,4},{1,7},{3,1},{5,3},{7,5},{8,14},{10,8},{12,... | collective-permute-start | bytes 393224 | tf_op jit(solution)/shard_map/gather/ppermute | solution.py:223
  (2 other events, 1.9 us)
